TPU v7x, 32 devices: a whole 2x2x4 slice. The times are simulated.
32 devices in a mesh: stream: 4 (over z), span: 2 (over x), wall: 4 (over y, core).
Axes of the slice: x: 2, y: 2, z: 4, core: 2. Of those that a mesh axis runs over, the one named last changes fastest.
Arguments:
- adj_init: float32 [17, 48, 32, 256], P(None, 'stream', 'wall', 'span'), may hold values from -1.2 to 1.2
- adj_source: float32 [17, 48, 32, 256], P(None, 'stream', 'wall', 'span'), may hold values from -12 to 12
- velocity: float32 [3, 48, 32, 256], P(None, 'stream', 'wall', 'span'), may hold values from -4 to 4
- sound: float32 [48, 32, 256], P('stream', 'wall', 'span'), may hold values from 0.5 to 2
- face_couple: float32 [3, 2, 17, 17], replicated, may hold values from -0.36 to 0.36
- precond_inv: float32 [17, 17], replicated, may hold values from -0.3 to 1.3
- wall_code: int32 [48, 256], replicated, may hold values from 0 to 3
- spall_mask: int32 [48, 256], replicated, may hold values 0 or 1
- wall_table: float32 [4, 17], replicated, may hold values from 0.5 to 2
- spall_gain: float32 [17], replicated, may hold values from 0.5 to 3
Outputs:
- adjoint_out: float32 [17, 48, 32, 256], P(None, 'stream', 'wall', 'span')
- residual_out: float32 [17, 48, 32, 256], P(None, 'stream', 'wall', 'span')
All inputs are finite; a program needn't handle non-finite values.
Results may differ from a plain program's by a relative error of at most 0.00015.
Values sent between devices are 32-bit elements; how exact they have to be, the bound alone decides.
No kernel may reach another device: no remote copies, remote signals or barrier semaphores. Data moves between devices by JAX's collectives and lax.ppermute only.
A program may use at most 128 MiB of HBM per device.

v0:
```python
import functools

import jax
import jax.numpy as jnp
import numpy as np
from jax import lax
from jax.experimental import pallas as pl
from jax.experimental.pallas import tpu as pltpu
from jax.sharding import PartitionSpec as P

AXES = ("stream", "span", "wall")
F32 = jnp.float32
BF16 = jnp.bfloat16
HIGHEST = lax.Precision.HIGHEST


class Dims:
    def __init__(self, shape):
        self.V, self.X, self.W, self.Z = shape
        self.G = self.V + 1
        while self.G * self.W % 16:
            self.G += 1
        self.B = self.G * self.W
        self.rows = self.V * self.X * self.W
        self.wall_rows = self.X * self.G + 8
        self.wall_k = -(-self.G // 8) * 8
        self.per = self.Z // (2 * self.X)
        self.span_groups = -(-(self.V + 1) // self.per)

    def block(self, group, x):
        return pl.ds((group * self.X + x) * self.W, self.W)

    def plane(self, ref, x):
        return jnp.concatenate([ref[self.block(v, x), :] for v in range(self.V)], axis=0)

    def store_plane(self, ref, x, value):
        for v in range(self.V):
            ref[self.block(v, x), :] = value[v * self.W : (v + 1) * self.W]

    def each(self, factor):
        return jnp.concatenate([factor] * self.V, axis=0)


def lanes(d, rows):
    return lax.broadcasted_iota(jnp.int32, (rows, d.Z), 1)


def row_ids(d):
    return lax.broadcasted_iota(jnp.int32, (d.W, d.Z), 0)


def radius_at(d, vel, snd, direction, x):
    return jnp.abs(vel[d.block(direction, x), :]) + snd[d.block(0, x), :]


def split3(value):
    high = value.astype(BF16)
    low = (value - high.astype(F32)).astype(BF16)
    return jnp.concatenate([high, low, high], axis=0)


def padded_plane(d, value):
    extra = d.B - value.shape[0]
    if not extra:
        return value
    return jnp.concatenate([value, jnp.zeros((extra, value.shape[1]), F32)], axis=0)


def dot(a, b):
    return jnp.dot(a, b, preferred_element_type=F32)


def pack_faces(d, block_of, radius_of, rows_of, even_s, even_w, s_a, s_b, w_a, w_b, z_out):
    V, X, W, Z, G = d.V, d.X, d.W, d.Z, d.G
    zero = jnp.zeros((W, Z), F32)
    for g in range(G):
        if g < V:
            first, last = block_of(g, 0), block_of(g, X - 1)
        elif g == V and radius_of is not None:
            first, last = radius_of(0, 0), radius_of(0, X - 1)
        else:
            first = last = zero
        s_a[g * W : (g + 1) * W, :] = jnp.where(even_s, last, first)
        s_b[g * W : (g + 1) * W, :] = jnp.where(even_s, first, last)
    tail = jnp.zeros((G - V, Z), F32)
    for x in range(X):
        first, last = rows_of(x, 0), rows_of(x, W - 1)
        w_a[x * G : x * G + V, :] = jnp.where(even_w, last, first)
        w_b[x * G : x * G + V, :] = jnp.where(even_w, first, last)
        w_a[x * G + V : (x + 1) * G, :] = tail
        w_b[x * G + V : (x + 1) * G, :] = tail
        if radius_of is not None:
            radius = radius_of(1, x)
            first, last = radius[:1], radius[W - 1 :]
            w_a[x * G + V : x * G + V + 1, :] = jnp.where(even_w, last, first)
            w_b[x * G + V : x * G + V + 1, :] = jnp.where(even_w, first, last)
    w_a[X * G :, :] = jnp.zeros((8, Z), F32)
    w_b[X * G :, :] = jnp.zeros((8, Z), F32)
    pair = lanes(d, W) // 2
    groups = [zero] * d.span_groups
    for x in range(X):
        for v in range(V + 1):
            if v < V:
                value = block_of(v, x)
            elif radius_of is not None:
                value = radius_of(2, x)
            else:
                continue
            spot = X * (v % d.per) + x
            moved = pltpu.roll(value, (2 * spot + 1) % Z, 1)
            groups[v // d.per] = jnp.where(pair == spot, moved, groups[v // d.per])
    for q in range(d.span_groups):
        z_out[q * W : (q + 1) * W, :] = groups[q]


def parity(axis):
    return lax.rem(lax.axis_index(axis), 2) == 0


def pack_kernel(d, adj, vel, snd, s_a, s_b, w_a, w_b, z_out):
    pack_faces(
        d,
        lambda v, x: adj[d.block(v, x), :],
        functools.partial(radius_at, d, vel, snd),
        lambda x, w: adj[pl.ds(x * d.W + w, d.V, stride=d.X * d.W), :],
        parity("stream"),
        parity("wall"),
        s_a,
        s_b,
        w_a,
        w_b,
        z_out,
    )


def make_matrices(d, couple, precond, mk, mw, pk):
    V, W, B = d.V, d.W, d.B
    K = d.wall_k
    row = lax.broadcasted_iota(jnp.int32, (B, 3 * B), 0)
    col = lax.broadcasted_iota(jnp.int32, (B, 3 * B), 1)
    shift = lax.rem(col, W) - lax.rem(row, W)
    same, lower, upper = shift == 0, shift == -1, shift == 1
    spread = lax.broadcasted_iota(jnp.int32, (B, V), 0) // W
    spread = (spread == lax.broadcasted_iota(jnp.int32, (B, V), 1)).astype(BF16)
    down = lax.broadcasted_iota(jnp.int32, (2 * V, 3 * B), 0)
    across = lax.broadcasted_iota(jnp.int32, (2 * V, 3 * B), 1)
    wide_high = (lax.rem(across, B) // W == down) & (across < 2 * B) & (down < V)
    wide_low = (lax.rem(across, B) // W == down - V) & (across >= 2 * B)
    wide = (wide_high | wide_low).astype(BF16)

    def halves(m, contract):
        high = m.astype(BF16)
        low = (m - high.astype(F32)).astype(BF16)
        dims = (((1,), (contract,)), ((), ()))
        parts = [lax.dot_general(spread, p, dims, preferred_element_type=F32) for p in (high, low)]
        return jnp.concatenate(parts, axis=1).astype(BF16)

    def spread_out(parts, mask):
        return jnp.where(mask, dot(parts, wide), 0.0).astype(BF16)

    couples = [halves(couple[n], 1) for n in range(6)]
    for n in range(6):
        mk[n * B : (n + 1) * B, :] = spread_out(couples[n], {2: lower, 3: upper}.get(n, same))
    pk[...] = spread_out(halves(precond[...], 0), same)
    down = lax.broadcasted_iota(jnp.int32, (2 * V, 6 * K), 0)
    across = lax.broadcasted_iota(jnp.int32, (2 * V, 6 * K), 1)
    wide_high = (lax.rem(across, K) == down) & (across < 4 * K) & (down < V)
    wide_low = (lax.rem(across, K) == down - V) & (across >= 4 * K)
    wide = (wide_high | wide_low).astype(BF16)
    row = lax.rem(lax.broadcasted_iota(jnp.int32, (B, 6 * K), 0), W)
    side = lax.rem(lax.broadcasted_iota(jnp.int32, (B, 6 * K), 1) // K, 2)
    low_side = jnp.where((row == 0) & (side == 0), dot(couples[2], wide), 0.0)
    high_side = jnp.where((row == W - 1) & (side == 1), dot(couples[3], wide), 0.0)
    mw[...] = (low_side + high_side).astype(BF16)


def make_wall(d, codes, mask, table, gain, wall_out):
    X, Z = d.X, d.Z
    place = lax.axis_index("stream")
    lane0 = pl.multiple_of(lax.axis_index("span") * Z, Z)
    kinds = table.shape[0]

    def window(ref):
        value = ref[:X, pl.ds(lane0, Z)]
        for s in range(1, lax.axis_size("stream")):
            value = jnp.where(place == s, ref[s * X : (s + 1) * X, pl.ds(lane0, Z)], value)
        return value

    code, spall = window(codes), window(mask).astype(F32)
    pieces = []
    for x in range(X):
        here = code[x : x + 1]
        pieces.append(
            jnp.concatenate(
                [(here == k).astype(F32) for k in range(kinds)] + [spall[x : x + 1]], axis=0
            )
        )
    hot = jnp.concatenate(pieces, axis=1)
    full = jnp.concatenate([table[...], gain[...]], axis=0)
    wall_out[...] = lax.dot_general(
        full, hot, (((0,), (0,)), ((), ())), precision=HIGHEST, preferred_element_type=F32
    )


def sweep_local(d, adj, src, vel, snd, mk, wall_coef, rates_of, out, rs_out):
    V, X, W, Z, B = d.V, d.X, d.W, d.Z, d.B
    n = V * W
    lane, row = lanes(d, W), row_ids(d)
    wall_flag = (lax.axis_index("wall") == 0).astype(F32)
    radius = [[radius_at(d, vel, snd, k, x) for x in range(X)] for k in range(3)]
    step = 2
    products = {}

    def product(x, k):
        chunk, offset = products[x]
        return chunk[k * B : k * B + n, offset * Z : (offset + 1) * Z]

    def finish(x):
        a = d.plane(adj, x)
        total = 1.0
        terms = []
        half = [0.5 * radius[k][x] for k in range(3)]
        for k, neighbour in ((0, x - 1), (1, x + 1)):
            rate = half[0]
            if 0 <= neighbour < X:
                rate = rate + 0.5 * radius[0][neighbour]
                terms.append((rate, product(neighbour, k)))
            total = total + rate
        for k, edge, turn in ((2, 0, 1), (3, W - 1, W - 1)):
            near = jnp.where(row == edge, 0.0, pltpu.roll(half[1], turn, 0))
            rate = half[1] + near
            terms.append((rate, product(x, k)))
            total = total + rate
        for k, edge, turn in ((4, 0, 1), (5, Z - 1, Z - 1)):
            near = jnp.where(lane == edge, 0.0, pltpu.roll(half[2], turn, 1))
            total = total + half[2] + near
            rate = jnp.where(lane == edge, 0.0, half[2] + near)
            terms.append((rate, pltpu.roll(product(x, k), turn, 1)))
        if rates_of is None:
            rs_out[d.block(0, x), :] = total
        else:
            total = rates_of[d.block(0, x), :]
        result = d.plane(src, x) - d.each(total) * a
        for rate, value in terms:
            result = result - d.each(rate) * value
        d.store_plane(out, x, result)
        spot = pl.ds(x * W, V, stride=X * W)
        factor = wall_flag * radius[1][x][:1]
        coef = wall_coef[:, x * Z : (x + 1) * Z]
        out[spot, :] = out[spot, :] - factor * coef * adj[spot, :]

    done = 0
    for start in range(0, X, step):
        here = list(range(start, min(X, start + step)))
        right = jnp.concatenate([padded_plane(d, d.plane(adj, x)) for x in here], axis=1)
        chunk = dot(mk[...], split3(right))
        for offset, x in enumerate(here):
            products[x] = (chunk, offset)
        while done < X and (done + 1 in products or (done + 1 == X and done in products)):
            finish(done)
            done += 1


def first_local_kernel(
    d, adj, src, vel, snd, couple, precond, codes, mask, table, gain, out, rs, mk, mw, pk, wall_coef
):
    make_matrices(d, couple, precond, mk, mw, pk)
    make_wall(d, codes, mask, table, gain, wall_coef)
    sweep_local(d, adj, src, vel, snd, mk, wall_coef, None, out, rs)


def later_local_kernel(d, adj, src, vel, snd, rs, mk, wall_coef, out):
    sweep_local(d, adj, src, vel, snd, mk, wall_coef, rs, out, None)


def halo_terms(d, s0, s1, w0, w1, zl, zr, mk, mw):
    V, X, W, Z, G, B = d.V, d.X, d.W, d.Z, d.G, d.B
    n = V * W
    even_s, even_w = parity("stream"), parity("wall")
    si, wi = lax.axis_index("stream"), lax.axis_index("wall")
    has = lambda flag: flag.astype(F32)
    s_low, s_high = has(si > 0), has(si < lax.axis_size("stream") - 1)
    w_low, w_high = has(wi > 0), has(wi < lax.axis_size("wall") - 1)
    low = jnp.where(even_s, s1[...], s0[...]) * s_low
    high = jnp.where(even_s, s0[...], s1[...]) * s_high
    stream = (dot(mk[:B], split3(low))[:n], dot(mk[B : 2 * B], split3(high))[:n])
    stream_radius = (low[n : n + W], high[n : n + W])

    def wall_rows(x):
        rows = pl.ds(x * G, d.wall_k)
        a, b = w0[rows, :], w1[rows, :]
        return jnp.where(even_w, b, a) * w_low, jnp.where(even_w, a, b) * w_high

    def wall(x):
        return jnp.concatenate(wall_rows(x), axis=0)

    row = row_ids(d)

    def wall_radius(x):
        rows = pl.ds(x * G + V, 1)
        a, b = w0[rows, :], w1[rows, :]
        first = jnp.where(even_w, b, a) * w_low
        last = jnp.where(even_w, a, b) * w_high
        return jnp.where(row == 0, first, jnp.where(row == W - 1, last, 0.0))

    even = lax.rem(lanes(d, W), 2) == 0
    pieces = []
    for v in range(V + 1):
        q = pl.ds((v // d.per) * W, W)
        value = jnp.where(even, zl[q, :], zr[q, :])
        turn = (Z - 2 * X * (v % d.per)) % Z
        pieces.append(pltpu.roll(value, turn, 1) if turn else value)
    span_radius = jnp.where(even, pieces[V], pltpu.roll(pieces[V], Z - 2, 1))
    pieces += [jnp.zeros((W, Z), F32)] * (G - V - 1)
    both = dot(mk[4 * B : 6 * B], split3(jnp.concatenate(pieces, axis=0)))
    even = lax.rem(lanes(d, n), 2) == 0
    span = jnp.where(even, both[:n], pltpu.roll(both[B : B + n], Z - 2, 1))
    at = lambda value, x: pltpu.roll(value, (Z - 2 * x) % Z, 1) if x else value
    return (
        stream,
        stream_radius,
        wall,
        wall_radius,
        lambda x: at(span, x),
        lambda x: at(span_radius, x),
    )


def finish_sweep(d, partial, adj, rs_of, halo_rates, corrections, halo, mw, pk, put):
    V, X, W, Z = d.V, d.X, d.W, d.Z
    n = V * W
    stream, _, wall, _, span, _ = halo
    for start in range(0, X, 2):
        here = list(range(start, min(X, start + 2)))
        from_wall = dot(mw[...], split3(jnp.concatenate([wall(x) for x in here], axis=1)))
        residuals = []
        for k, x in enumerate(here):
            low, high, rate_wall, rate_span = halo_rates(x)
            res = d.plane(partial, x)
            if corrections is not None:
                res = res - d.each(corrections(x)) * d.plane(adj, x)
            res = res - d.each(rate_wall) * from_wall[:n, k * Z : (k + 1) * Z]
            res = res - d.each(rate_span) * span(x)
            if low is not None:
                res = res - d.each(low) * stream[0]
            if high is not None:
                res = res - d.each(high) * stream[1]
            residuals.append(res)
        right = jnp.concatenate([padded_plane(d, r) for r in residuals], axis=1)
        update = dot(pk[...], split3(right))
        for k, x in enumerate(here):
            inverse = 1.0 / rs_of(x)
            new = d.plane(adj, x) + update[:n, k * Z : (k + 1) * Z] * d.each(inverse)
            put(x, new, residuals[k])


def first_halo_kernel(
    d, partial, adj, rs, vel, snd, s0, s1, w0, w1, zl, zr, mk, mw, pk,
    new_adj, rs_full, rates, s_a, s_b, w_a, w_b, z_out,
):
    X, W, Z = d.X, d.W, d.Z
    halo = halo_terms(d, s0, s1, w0, w1, zl, zr, mk, mw)
    _, stream_radius, _, wall_radius, _, span_radius = halo
    lane, row = lanes(d, W), row_ids(d)
    edge_lane = (lane == 0) | (lane == Z - 1)
    edge_row = (row == 0) | (row == W - 1)
    kept = {}
    for x in range(X):
        from_wall = 0.5 * wall_radius(x)
        from_span = jnp.where(edge_lane, 0.5 * span_radius(x), 0.0)
        rate_wall = jnp.where(edge_row, 0.5 * radius_at(d, vel, snd, 1, x) + from_wall, 0.0)
        rate_span = jnp.where(edge_lane, 0.5 * radius_at(d, vel, snd, 2, x) + from_span, 0.0)
        correction = from_wall + from_span
        low = high = None
        if x == 0:
            correction = correction + 0.5 * stream_radius[0]
            low = 0.5 * (radius_at(d, vel, snd, 0, x) + stream_radius[0])
            rates[d.block(2, 0), :] = low
        if x == X - 1:
            correction = correction + 0.5 * stream_radius[1]
            high = 0.5 * (radius_at(d, vel, snd, 0, x) + stream_radius[1])
            rates[d.block(2, 1 % X) if X > 1 else pl.ds((2 * X + 1) * W, W), :] = high
        rates[d.block(0, x), :] = rate_wall
        rates[d.block(1, x), :] = rate_span
        total = rs[d.block(0, x), :] + correction
        rs_full[d.block(0, x), :] = total
        kept[x] = (correction, total, (low, high, rate_wall, rate_span))

    def put(x, new, _):
        d.store_plane(new_adj, x, new)

    finish_sweep(
        d, partial, adj, lambda x: kept[x][1], lambda x: kept[x][2], lambda x: kept[x][0],
        halo, mw, pk, put,
    )
    pack_faces(
        d,
        lambda v, x: new_adj[d.block(v, x), :],
        None,
        lambda x, w: new_adj[pl.ds(x * W + w, d.V, stride=X * W), :],
        parity("stream"),
        parity("wall"),
        s_a, s_b, w_a, w_b, z_out,
    )


def last_halo_kernel(
    d, partial, adj, rs_full, rates, s0, s1, w0, w1, zl, zr, mk, mw, pk, new_adj, residual
):
    X, W = d.X, d.W
    halo = halo_terms(d, s0, s1, w0, w1, zl, zr, mk, mw)

    def halo_rates(x):
        low = rates[pl.ds(2 * X * W, W), :] if x == 0 else None
        high = rates[pl.ds((2 * X + 1) * W, W), :] if x == X - 1 else None
        return low, high, rates[d.block(0, x), :], rates[d.block(1, x), :]

    def put(x, new, res):
        d.store_plane(new_adj, x, new)
        d.store_plane(residual, x, res)

    finish_sweep(
        d, partial, adj, lambda x: rs_full[d.block(0, x), :], halo_rates, None, halo, mw, pk, put
    )


def exchange_pairs(sizes, axis, odd, spare):
    ids = np.arange(int(np.prod(sizes))).reshape(sizes)
    pairs = []
    for at in np.ndindex(*sizes):
        to = list(at)
        step = 1 if (at[axis] - odd) % 2 == 0 else -1
        if at[axis] >= odd and 0 <= at[axis] + step < sizes[axis]:
            to[axis] += step
        elif (at[spare] ^ 1) < sizes[spare]:
            to[spare] ^= 1
        else:
            continue
        pairs.append((int(ids[at]), int(ids[tuple(to)])))
    return pairs


def swap_lines(sizes, s_a, s_b, w_a, w_b, z):
    move = lambda value, pairs: lax.ppermute(value, AXES, pairs)
    s0 = move(s_a, exchange_pairs(sizes, 0, 0, 2))
    s1 = move(s_b, exchange_pairs(sizes, 0, 1, 2))
    w1 = move(w_b, exchange_pairs(sizes, 2, 1, 1))
    w0 = move(w_a, exchange_pairs(sizes, 2, 0, 1))
    peers = sizes[1]
    if peers == 1:
        zl = zr = z
    elif peers == 2:
        zl = zr = lax.ppermute(z, "span", [(0, 1), (1, 0)])
    else:
        up = [(i, (i + 1) % peers) for i in range(peers)]
        zl = lax.ppermute(z, "span", up)
        zr = lax.ppermute(z, "span", [(j, i) for i, j in up])
    return s0, s1, w0, w1, zl, zr


def call(kernel, d, outs, flops, args, in_vmem=True, out_vmem=True):
    name = kernel.__name__
    if out_vmem:
        shapes = tuple(pltpu.VMEM(s, t) for s, t in outs)
    else:
        shapes = tuple(jax.ShapeDtypeStruct(s, t) for s, t in outs)
    if in_vmem:
        args = [pltpu.with_memory_space_constraint(a, pltpu.VMEM) for a in args]
    moved = sum(int(np.prod(a.shape)) * a.dtype.itemsize for a in args)
    return pl.pallas_call(
        functools.partial(kernel, d),
        out_shape=shapes,
        in_specs=[pl.BlockSpec(memory_space=pltpu.VMEM)] * len(args),
        out_specs=tuple(pl.BlockSpec(memory_space=pltpu.VMEM) for _ in outs),
        compiler_params=pltpu.CompilerParams(vmem_limit_bytes=24 * 2**20),
        cost_estimate=pl.CostEstimate(flops=flops, bytes_accessed=moved, transcendentals=0),
        name=name,
    )(*args)


def on_device(sizes, adj, source, velocity, sound, couple, precond, codes, mask, table, gain):
    shape = adj.shape
    d = Dims(shape)
    X, W, Z, B = d.X, d.W, d.Z, d.B
    adj = adj.reshape(d.rows, Z)
    source = source.reshape(d.rows, Z)
    velocity = velocity.reshape(3 * X * W, Z)
    sound = sound.reshape(X * W, Z)
    couple = couple.reshape((6,) + couple.shape[2:])
    gain = gain.reshape(1, -1)
    vmem = lambda a: pltpu.with_memory_space_constraint(a, pltpu.VMEM)

    faces = [((B, Z), F32)] * 2 + [((d.wall_rows, Z), F32)] * 2 + [((d.span_groups * W, Z), F32)]
    field, scalar = ((d.rows, Z), F32), ((X * W, Z), F32)
    packets = call(pack_kernel, d, faces, 0, [adj, velocity, sound])
    got = swap_lines(sizes, *packets)
    partial, rs, mk, mw, pk, wall_coef = call(
        first_local_kernel,
        d,
        [
            field,
            scalar,
            ((6 * B, 3 * B), BF16),
            ((B, 6 * d.wall_k), BF16),
            ((B, 3 * B), BF16),
            ((d.V, X * Z), F32),
        ],
        10**9,
        [adj, source, velocity, sound, couple, precond, codes, mask, table, gain],
    )
    adj1, rs_full, rates, *packets = call(
        first_halo_kernel,
        d,
        [field, scalar, ((2 * (X + 1) * W, Z), F32)] + faces,
        10**8,
        [partial, adj, rs, velocity, sound, *got, mk, mw, pk],
    )
    got = swap_lines(sizes, *packets)
    (partial,) = call(
        later_local_kernel, d, [field], 10**9, [adj1, source, velocity, sound, rs_full, mk, wall_coef]
    )
    adj2, residual = call(
        last_halo_kernel,
        d,
        [field, field],
        10**8,
        [partial, adj1, rs_full, rates, *got, mk, mw, pk],
        out_vmem=False,
    )
    return adj2.reshape(shape), residual.reshape(shape)


def solution(mesh):
    sizes = tuple(mesh.shape[a] for a in AXES)
    field = P(None, "stream", "wall", "span")
    return jax.shard_map(
        functools.partial(on_device, sizes),
        mesh=mesh,
        in_specs=(field, field, field, P("stream", "wall", "span")) + (P(),) * 6,
        out_specs=(field, field),
        check_vma=False,
    )
```

profile of v0, /device:TPU:0, one launch (start us, length us, event | category | flops | bytes accessed | tf_op | source)
XLA Modules:
  0.0 24.7 jit_solution(4920739493168874140)
XLA Ops:
  0.6 1.1 %copy-done = f32[17,12,8,128]{3,2,1,0:T(8,128)S(1)} copy-done((f32[17,12,8,128]{3,2,1,0:T(8,128)S(1)}, f32[17,12,8,128]{3,2,1,0:T(8,128)}, u32[]{:S(2)}) %copy-start) | copy-done | bytes 835608
  1.8 0.9 %copy-done.1 = f32[3,12,8,128]{3,2,1,0:T(8,128)S(1)} copy-done((f32[3,12,8,128]{3,2,1,0:T(8,128)S(1)}, f32[3,12,8,128]{3,2,1,0:T(8,128)}, u32[]{:S(2)}) %copy-start.1) | copy-done | bytes 147480
  2.7 0.8 %copy-done.4 = f32[12,8,128]{2,1,0:T(8,128)S(1)} copy-done((f32[12,8,128]{2,1,0:T(8,128)S(1)}, f32[12,8,128]{2,1,0:T(8,128)}, u32[]{:S(2)}) %copy-start.4) | copy-done | bytes 49176
  3.5 0.4 %pack_kernel.1 = (f32[144,128]{1,0:T(8,128)S(1)}, f32[144,128]{1,0:T(8,128)S(1)}, f32[224,128]{1,0:T(8,128)S(1)}, f32[224,128]{1,0:T(8,128)S(1)}, f32[32,128]{1,0:T(8,128)S(1)}) custom-call(f32[1632,128]{1,0:T(8,128)S(1)} %bitcast.8, f32[288,128]{1,0:T(8,128)S(1)} %bitcast.11, f32[96,128]{1,0:T(8,128)S(1)} %bitcast.17), custom_call_target="tpu_custom_call" | custom-call | bytes 1032192 | tf_op jit(solution)/shard_map/pack_kernel/pallas_call | solution.py:470
  3.9 0.5 %collective-permute-start.2 = (f32[224,128]{1,0:T(8,128)S(1)}, f32[224,128]{1,0:T(8,128)S(1)}, u32[]{:S(2)}, u32[]{:S(2)}) collective-permute-start(f32[224,128]{1,0:T(8,128)S(1)} %get-tuple-element.27), channel_id=1, source_target_pairs={{0,1},{1,0},{2,3},{3,2},{4,5},{5,4},{6,7},{7,6},{8,9},{9,8},{10,11... | collective-permute-start | bytes 344072 | tf_op jit(solution)/shard_map/ppermute | solution.py:444
  4.4 2.6 %collective-permute-start.3 = (f32[224,128]{1,0:T(8,128)S(1)}, f32[224,128]{1,0:T(8,128)S(1)}, u32[]{:S(2)}, u32[]{:S(2)}) collective-permute-start(f32[224,128]{1,0:T(8,128)S(1)} %get-tuple-element.28), channel_id=1, source_target_pairs={{0,4},{1,2},{2,1},{3,7},{4,0},{5,6},{6,5},{7,3},{8,12},{9,10},{10,... | collective-permute-start | bytes 344072 | tf_op jit(solution)/shard_map/ppermute | solution.py:444
  7.0 0.1 collective-permute-start.4
  7.1 2.0 %collective-permute-start = (f32[144,128]{1,0:T(8,128)S(1)}, f32[144,128]{1,0:T(8,128)S(1)}, u32[]{:S(2)}, u32[]{:S(2)}) collective-permute-start(f32[144,128]{1,0:T(8,128)S(1)} %get-tuple-element.25), channel_id=1, source_target_pairs={{0,8},{1,9},{2,10},{3,11},{4,12},{5,13},{6,14},{7,15},{8,0},{9,1},... | collective-permute-start | bytes 221192 | tf_op jit(solution)/shard_map/ppermute | solution.py:444
  9.1 0.5 %collective-permute-start.1 = (f32[144,128]{1,0:T(8,128)S(1)}, f32[144,128]{1,0:T(8,128)S(1)}, u32[]{:S(2)}, u32[]{:S(2)}) collective-permute-start(f32[144,128]{1,0:T(8,128)S(1)} %get-tuple-element.26), channel_id=1, source_target_pairs={{0,1},{1,0},{2,3},{3,2},{4,5},{5,4},{6,7},{7,6},{8,16},{9,17},{10,... | collective-permute-start | bytes 221192 | tf_op jit(solution)/shard_map/ppermute | solution.py:444
  9.7 0.0 copy-start.8
  9.7 0.0 copy-start.9
  9.7 0.2 copy-done.5
  9.9 0.0 copy-done.6
  9.9 0.4 %copy-done.8 = f32[4,17]{1,0:T(4,128)S(1)} copy-done((f32[4,17]{1,0:T(4,128)S(1)}, f32[4,17]{1,0:T(4,128)}, u32[]{:S(2)}) %copy-start.8) | copy-done | bytes 296
  10.4 2.8 %first_local_kernel.1 = (f32[1632,128]{1,0:T(8,128)S(1)}, f32[96,128]{1,0:T(8,128)S(1)}, bf16[864,432]{1,0:T(8,128)(2,1)S(1)}, bf16[144,144]{1,0:T(8,128)(2,1)S(...) custom-call(f32[1632,128]{1,0:T(8,128)S(1)} %bitcast.9, f32[1632,128]{1,0:T(8,128)S(1)} %bitcast.15, ...), custom_call_target="tpu_custom_call" | custom-call | flops 1000000000 | bytes 1974512 | tf_op jit(solution)/shard_map/first_local_kernel/pallas_call | solution.py:470
  13.2 0.0 collective-permute-done.1.s1
  13.2 1.7 %first_halo_kernel.1 = (f32[1632,128]{1,0:T(8,128)S(1)}, f32[96,128]{1,0:T(8,128)S(1)}, f32[208,128]{1,0:T(8,128)S(1)}, f32[144,128]{1,0:T(8,128)S(1)}, f32[144,...) custom-call(f32[1632,128]{1,0:T(8,128)S(1)} %get-tuple-element.23.partial, ...), custom_call_target="tpu_custom_call" | custom-call | flops 100000000 | bytes 3238912 | tf_op jit(solution)/shard_map/first_halo_kernel/pallas_call | solution.py:470
  14.9 0.2 collective-permute-start.7
  15.1 1.3 %collective-permute-start.8 = (f32[224,128]{1,0:T(8,128)S(1)}, f32[224,128]{1,0:T(8,128)S(1)}, u32[]{:S(2)}, u32[]{:S(2)}) collective-permute-start(f32[224,128]{1,0:T(8,128)S(1)} %get-tuple-element.40), channel_id=1, source_target_pairs={{0,4},{1,2},{2,1},{3,7},{4,0},{5,6},{6,5},{7,3},{8,12},{9,10},{10,... | collective-permute-start | bytes 344072 | tf_op jit(solution)/shard_map/ppermute | solution.py:444
  16.5 0.7 %collective-permute-start.9 = (f32[32,128]{1,0:T(8,128)S(1)}, f32[32,128]{1,0:T(8,128)S(1)}, u32[]{:S(2)}, u32[]{:S(2)}) collective-permute-start(f32[32,128]{1,0:T(8,128)S(1)} %get-tuple-element.41), channel_id=1, source_target_pairs={{0,4},{4,0},{1,5},{5,1},{2,6},{6,2},{3,7},{7,3},{8,12},{12,8},{9,1... | collective-permute-start | bytes 49160 | tf_op jit(solution)/shard_map/ppermute | solution.py:453
  17.1 2.8 %collective-permute-start.5 = (f32[144,128]{1,0:T(8,128)S(1)}, f32[144,128]{1,0:T(8,128)S(1)}, u32[]{:S(2)}, u32[]{:S(2)}) collective-permute-start(f32[144,128]{1,0:T(8,128)S(1)} %get-tuple-element.37), channel_id=1, source_target_pairs={{0,8},{1,9},{2,10},{3,11},{4,12},{5,13},{6,14},{7,15},{8,0},{9,1},... | collective-permute-start | bytes 221192 | tf_op jit(solution)/shard_map/ppermute | solution.py:444
  19.9 1.8 %later_local_kernel.1.partial = f32[1632,128]{1,0:T(8,128)S(1)} custom-call(f32[1632,128]{1,0:T(8,128)S(1)} %get-tuple-element.33.adj, f32[1632,128]{1,0:T(8,128)S(1)} %bitcast.16, f32[288,128]{1,0:T(8,128)S(1)} %bitcast.14, f32[96,128]{1,0:T(8,128)S(1)} %bitcast.20, f32[96,128]{1,0:T(8,128)S(1)} %get-tuple-element.34.rs.rs_full, ...), custom_call_target="tpu_custom_call" | custom-call | flops 1000000000 | bytes 2767872 | tf_op jit(solution)/shard_map/later_local_kernel/pallas_call | solution.py:470
  21.7 0.5 %collective-permute-done.5.s0 = f32[144,128]{1,0:T(8,128)S(1)} collective-permute-done((f32[144,128]{1,0:T(8,128)S(1)}, f32[144,128]{1,0:T(8,128)S(1)}, u32[]{:S(2)}, u32[]{:S(2)}) %collective-permute-start.5) | collective-permute-done | bytes 73760 | tf_op jit(solution)/shard_map/ppermute | solution.py:444
  22.2 2.5 %last_halo_kernel.1 = (f32[1632,128]{1,0:T(8,128)}, f32[1632,128]{1,0:T(8,128)}) custom-call(f32[1632,128]{1,0:T(8,128)S(1)} %later_local_kernel.1.partial, f32[1632,128]{1,0:T(8,128)S(1)} %get-tuple-element.33.adj, f32[96,128]{1,0:T(8,128)S(1)} %get-tuple-element.34.rs.rs_full, f32[208,128]{1,0:T(8,128)S(1)} %get-tuple-element.36.rates, ...), custom_call_target="tpu_custom_call" | custom-call | flops 100000000 | bytes 3148800 | tf_op jit(solution)/shard_map/last_halo_kernel/pallas_call | solution.py:470
  (24 shorter events, 0.1 us)
Async XLA Ops:
  0.6 1.2 %copy-start = (f32[17,12,8,128]{3,2,1,0:T(8,128)S(1)}, f32[17,12,8,128]{3,2,1,0:T(8,128)}, u32[]{:S(2)}) copy-start(f32[17,12,8,128]{3,2,1,0:T(8,128)} %param.10) | copy-start | bytes 2506756
  1.8 0.9 %copy-start.1 = (f32[3,12,8,128]{3,2,1,0:T(8,128)S(1)}, f32[3,12,8,128]{3,2,1,0:T(8,128)}, u32[]{:S(2)}) copy-start(f32[3,12,8,128]{3,2,1,0:T(8,128)} %param.12) | copy-start | bytes 442372
  2.7 0.8 %copy-start.4 = (f32[12,8,128]{2,1,0:T(8,128)S(1)}, f32[12,8,128]{2,1,0:T(8,128)}, u32[]{:S(2)}) copy-start(f32[12,8,128]{2,1,0:T(8,128)} %param.13) | copy-start | bytes 147460
  3.5 6.2 %copy-start.10 = (f32[3,2,17,17]{3,1,2,0:T(2,128)S(1)}, f32[3,2,17,17]{3,1,2,0:T(2,128)}, u32[]{:S(2)}) copy-start(f32[3,2,17,17]{3,1,2,0:T(2,128)} %param.14) | copy-start | bytes 20812
  3.5 6.2 %copy-start.2 = (f32[3,12,8,128]{3,2,1,0:T(8,128)S(1)}, f32[3,12,8,128]{3,2,1,0:T(8,128)}, u32[]{:S(2)}) copy-start(f32[3,12,8,128]{3,2,1,0:T(8,128)} %param.12) | copy-start | bytes 442372
  3.5 6.2 %copy-start.3 = (f32[17,12,8,128]{3,2,1,0:T(8,128)S(1)}, f32[17,12,8,128]{3,2,1,0:T(8,128)}, u32[]{:S(2)}) copy-start(f32[17,12,8,128]{3,2,1,0:T(8,128)} %param.11) | copy-start | bytes 2506756
  3.9 9.3 %collective-permute-start.2 = (f32[224,128]{1,0:T(8,128)S(1)}, f32[224,128]{1,0:T(8,128)S(1)}, u32[]{:S(2)}, u32[]{:S(2)}) collective-permute-start(f32[224,128]{1,0:T(8,128)S(1)} %get-tuple-element.27), channel_id=1, source_target_pairs={{0,1},{1,0},{2,3},{3,2},{4,5},{5,4},{6,7},{7,6},{8,9},{9,8},{10,11... | collective-permute-start | bytes 344072 | tf_op jit(solution)/shard_map/ppermute | solution.py:444
  4.4 8.8 %collective-permute-start.3 = (f32[224,128]{1,0:T(8,128)S(1)}, f32[224,128]{1,0:T(8,128)S(1)}, u32[]{:S(2)}, u32[]{:S(2)}) collective-permute-start(f32[224,128]{1,0:T(8,128)S(1)} %get-tuple-element.28), channel_id=1, source_target_pairs={{0,4},{1,2},{2,1},{3,7},{4,0},{5,6},{6,5},{7,3},{8,12},{9,10},{10,... | collective-permute-start | bytes 344072 | tf_op jit(solution)/shard_map/ppermute | solution.py:444
  7.0 6.2 %collective-permute-start.4 = (f32[32,128]{1,0:T(8,128)S(1)}, f32[32,128]{1,0:T(8,128)S(1)}, u32[]{:S(2)}, u32[]{:S(2)}) collective-permute-start(f32[32,128]{1,0:T(8,128)S(1)} %get-tuple-element.29), channel_id=1, source_target_pairs={{0,4},{4,0},{1,5},{5,1},{2,6},{6,2},{3,7},{7,3},{8,12},{12,8},{9,1... | collective-permute-start | bytes 49160 | tf_op jit(solution)/shard_map/ppermute | solution.py:453
  7.1 6.1 %collective-permute-start = (f32[144,128]{1,0:T(8,128)S(1)}, f32[144,128]{1,0:T(8,128)S(1)}, u32[]{:S(2)}, u32[]{:S(2)}) collective-permute-start(f32[144,128]{1,0:T(8,128)S(1)} %get-tuple-element.25), channel_id=1, source_target_pairs={{0,8},{1,9},{2,10},{3,11},{4,12},{5,13},{6,14},{7,15},{8,0},{9,1},... | collective-permute-start | bytes 221192 | tf_op jit(solution)/shard_map/ppermute | solution.py:444
  9.1 0.8 %copy-start.5 = (s32[48,256]{1,0:T(8,128)S(1)}, s32[48,256]{1,0:T(8,128)}, u32[]{:S(2)}) copy-start(s32[48,256]{1,0:T(8,128)} %codes.1) | copy-start | bytes 147460
  9.1 0.8 %copy-start.6 = (s32[48,256]{1,0:T(8,128)S(1)}, s32[48,256]{1,0:T(8,128)}, u32[]{:S(2)}) copy-start(s32[48,256]{1,0:T(8,128)} %mask.1) | copy-start | bytes 147460
  9.1 0.8 %copy-start.7 = (f32[17,17]{1,0:T(8,128)S(1)}, f32[17,17]{1,0:T(8,128)}, u32[]{:S(2)}) copy-start(f32[17,17]{1,0:T(8,128)} %precond.1) | copy-start | bytes 3472
  9.1 4.1 %collective-permute-start.1 = (f32[144,128]{1,0:T(8,128)S(1)}, f32[144,128]{1,0:T(8,128)S(1)}, u32[]{:S(2)}, u32[]{:S(2)}) collective-permute-start(f32[144,128]{1,0:T(8,128)S(1)} %get-tuple-element.26), channel_id=1, source_target_pairs={{0,1},{1,0},{2,3},{3,2},{4,5},{5,4},{6,7},{7,6},{8,16},{9,17},{10,... | collective-permute-start | bytes 221192 | tf_op jit(solution)/shard_map/ppermute | solution.py:444
  9.7 0.7 %copy-start.8 = (f32[4,17]{1,0:T(4,128)S(1)}, f32[4,17]{1,0:T(4,128)}, u32[]{:S(2)}) copy-start(f32[4,17]{1,0:T(4,128)} %table.1) | copy-start | bytes 820
  9.7 0.7 %copy-start.9 = (f32[17]{0:T(128)S(1)}, f32[17]{0:T(128)}, u32[]{:S(2)}) copy-start(f32[17]{0:T(128)} %param.19) | copy-start | bytes 208
  14.9 7.3 %collective-permute-start.7 = (f32[224,128]{1,0:T(8,128)S(1)}, f32[224,128]{1,0:T(8,128)S(1)}, u32[]{:S(2)}, u32[]{:S(2)}) collective-permute-start(f32[224,128]{1,0:T(8,128)S(1)} %get-tuple-element.39), channel_id=1, source_target_pairs={{0,1},{1,0},{2,3},{3,2},{4,5},{5,4},{6,7},{7,6},{8,9},{9,8},{10,11... | collective-permute-start | bytes 344072 | tf_op jit(solution)/shard_map/ppermute | solution.py:444
  15.1 7.1 %collective-permute-start.8 = (f32[224,128]{1,0:T(8,128)S(1)}, f32[224,128]{1,0:T(8,128)S(1)}, u32[]{:S(2)}, u32[]{:S(2)}) collective-permute-start(f32[224,128]{1,0:T(8,128)S(1)} %get-tuple-element.40), channel_id=1, source_target_pairs={{0,4},{1,2},{2,1},{3,7},{4,0},{5,6},{6,5},{7,3},{8,12},{9,10},{10,... | collective-permute-start | bytes 344072 | tf_op jit(solution)/shard_map/ppermute | solution.py:444
  16.5 5.3 %collective-permute-start.9 = (f32[32,128]{1,0:T(8,128)S(1)}, f32[32,128]{1,0:T(8,128)S(1)}, u32[]{:S(2)}, u32[]{:S(2)}) collective-permute-start(f32[32,128]{1,0:T(8,128)S(1)} %get-tuple-element.41), channel_id=1, source_target_pairs={{0,4},{4,0},{1,5},{5,1},{2,6},{6,2},{3,7},{7,3},{8,12},{12,8},{9,1... | collective-permute-start | bytes 49160 | tf_op jit(solution)/shard_map/ppermute | solution.py:453
  17.1 5.1 %collective-permute-start.5 = (f32[144,128]{1,0:T(8,128)S(1)}, f32[144,128]{1,0:T(8,128)S(1)}, u32[]{:S(2)}, u32[]{:S(2)}) collective-permute-start(f32[144,128]{1,0:T(8,128)S(1)} %get-tuple-element.37), channel_id=1, source_target_pairs={{0,8},{1,9},{2,10},{3,11},{4,12},{5,13},{6,14},{7,15},{8,0},{9,1},... | collective-permute-start | bytes 221192 | tf_op jit(solution)/shard_map/ppermute | solution.py:444
  19.9 2.3 %collective-permute-start.6 = (f32[144,128]{1,0:T(8,128)S(1)}, f32[144,128]{1,0:T(8,128)S(1)}, u32[]{:S(2)}, u32[]{:S(2)}) collective-permute-start(f32[144,128]{1,0:T(8,128)S(1)} %get-tuple-element.38), channel_id=1, source_target_pairs={{0,1},{1,0},{2,3},{3,2},{4,5},{5,4},{6,7},{7,6},{8,16},{9,17},{10,... | collective-permute-start | bytes 221192 | tf_op jit(solution)/shard_map/ppermute | solution.py:444
where the time goes:
time: 25 us; the launch traced here: 24.7 us
  starting transfers between devices  10.7 us (43%)
  Pallas kernels  9.2 us (37%)
  local copies, waits for them, and re-layouts  3.54 us (14%)
  between operations  0.76 us (3%)
  waiting for transfers between devices  0.52 us (2%)
    ppermute x8, starting transfers between devices, swap_lines(): move = lambda value, pairs: lax.ppermute(value, AXES, pairs)  9.94 us
    pallas_call x5, Pallas kernels, call(): pl.pallas_call(functools.partial(kernel, d), out_shape=shapes, in_specs=[...  9.2 us
    unnamed x23, local copies, waits for them, and re-layouts  3.54 us
    ppermute x2, starting transfers between devices, swap_lines(): zl = zr = lax.ppermute(z, 'span', [(0, 1), (1, 0)])  0.77 us
    ppermute x8, waiting for transfers between devices, swap_lines(): move = lambda value, pairs: lax.ppermute(value, AXES, pairs)  0.51 us
  transfers between devices with their start and end apart: 10, of which 1 were waited for; matrix products, arithmetic and copies ran while one was open for 0% of the time, Pallas kernels for 19%

commit v1 on v0

--- a/solution.py
+++ b/solution.py
@@ -12,6 +12,7 @@
 F32 = jnp.float32
 BF16 = jnp.bfloat16
 HIGHEST = lax.Precision.HIGHEST
+STORE = 6
 
 
 class Dims:
@@ -21,7 +22,8 @@
         while self.G * self.W % 16:
             self.G += 1
         self.B = self.G * self.W
-        self.rows = self.V * self.X * self.W
+        self.n = self.V * self.W
+        self.rows = self.n * self.X
         self.wall_rows = self.X * self.G + 8
         self.wall_k = -(-self.G // 8) * 8
         self.per = self.Z // (2 * self.X)
@@ -36,6 +38,12 @@
     def store_plane(self, ref, x, value):
         for v in range(self.V):
             ref[self.block(v, x), :] = value[v * self.W : (v + 1) * self.W]
+
+    def plane3(self, ref, x):
+        return ref[:, x * self.W : (x + 1) * self.W, :].reshape(self.n, self.Z)
+
+    def planes_at(self, start, count):
+        return (slice(None), pl.ds(start * self.W, count * self.W), slice(None))
 
     def each(self, factor):
         return jnp.concatenate([factor] * self.V, axis=0)
@@ -70,25 +78,42 @@
     return jnp.dot(a, b, preferred_element_type=F32)
 
 
-def pack_faces(d, block_of, radius_of, rows_of, even_s, even_w, s_a, s_b, w_a, w_b, z_out):
+def pack_faces(
+    d, block_of, radius_of, rows_of, even_s, even_w, s_a, s_b, w_a, w_b, z_out
+):
     V, X, W, Z, G = d.V, d.X, d.W, d.Z, d.G
     zero = jnp.zeros((W, Z), F32)
+    pair = lanes(d, W) // 2
+    groups = [zero] * d.span_groups
+
+    def span_columns(v, x, value):
+        spot = X * (v % d.per) + x
+        moved = pltpu.roll(value, (2 * spot + 1) % Z, 1)
+        groups[v // d.per] = jnp.where(pair == spot, moved, groups[v // d.per])
+
     for g in range(G):
         if g < V:
             first, last = block_of(g, 0), block_of(g, X - 1)
+            for x in range(X):
+                span_columns(g, x, block_of(g, x))
         elif g == V and radius_of is not None:
             first, last = radius_of(0, 0), radius_of(0, X - 1)
+            for x in range(X):
+                span_columns(V, x, radius_of(2, x))
         else:
             first = last = zero
         s_a[g * W : (g + 1) * W, :] = jnp.where(even_s, last, first)
         s_b[g * W : (g + 1) * W, :] = jnp.where(even_s, first, last)
+    for q in range(d.span_groups):
+        z_out[q * W : (q + 1) * W, :] = groups[q]
     tail = jnp.zeros((G - V, Z), F32)
     for x in range(X):
         first, last = rows_of(x, 0), rows_of(x, W - 1)
         w_a[x * G : x * G + V, :] = jnp.where(even_w, last, first)
         w_b[x * G : x * G + V, :] = jnp.where(even_w, first, last)
-        w_a[x * G + V : (x + 1) * G, :] = tail
-        w_b[x * G + V : (x + 1) * G, :] = tail
+        if radius_of is None or G - V > 1:
+            w_a[x * G + V : (x + 1) * G, :] = tail
+            w_b[x * G + V : (x + 1) * G, :] = tail
         if radius_of is not None:
             radius = radius_of(1, x)
             first, last = radius[:1], radius[W - 1 :]
@@ -96,28 +121,22 @@
             w_b[x * G + V : x * G + V + 1, :] = jnp.where(even_w, first, last)
     w_a[X * G :, :] = jnp.zeros((8, Z), F32)
     w_b[X * G :, :] = jnp.zeros((8, Z), F32)
-    pair = lanes(d, W) // 2
-    groups = [zero] * d.span_groups
-    for x in range(X):
-        for v in range(V + 1):
-            if v < V:
-                value = block_of(v, x)
-            elif radius_of is not None:
-                value = radius_of(2, x)
-            else:
-                continue
-            spot = X * (v % d.per) + x
-            moved = pltpu.roll(value, (2 * spot + 1) % Z, 1)
-            groups[v // d.per] = jnp.where(pair == spot, moved, groups[v // d.per])
-    for q in range(d.span_groups):
-        z_out[q * W : (q + 1) * W, :] = groups[q]
 
 
 def parity(axis):
     return lax.rem(lax.axis_index(axis), 2) == 0
 
 
-def pack_kernel(d, adj, vel, snd, s_a, s_b, w_a, w_b, z_out):
+def pack_kernel(d, *refs):
+    count = (len(refs) - 6) // 2
+    held, kept = refs[:count], refs[count : 2 * count]
+    s_a, s_b, w_a, w_b, z_out, sems = refs[2 * count :]
+    adj, vel, snd = kept[:3]
+    copies = [pltpu.make_async_copy(held[k], kept[k], sems.at[k]) for k in range(count)]
+    for copy in copies:
+        copy.start()
+    for copy in copies:
+        copy.wait()
     pack_faces(
         d,
         lambda v, x: adj[d.block(v, x), :],
@@ -134,44 +153,61 @@
 
 
 def make_matrices(d, couple, precond, mk, mw, pk):
-    V, W, B = d.V, d.W, d.B
-    K = d.wall_k
-    row = lax.broadcasted_iota(jnp.int32, (B, 3 * B), 0)
-    col = lax.broadcasted_iota(jnp.int32, (B, 3 * B), 1)
-    shift = lax.rem(col, W) - lax.rem(row, W)
-    same, lower, upper = shift == 0, shift == -1, shift == 1
-    spread = lax.broadcasted_iota(jnp.int32, (B, V), 0) // W
-    spread = (spread == lax.broadcasted_iota(jnp.int32, (B, V), 1)).astype(BF16)
-    down = lax.broadcasted_iota(jnp.int32, (2 * V, 3 * B), 0)
-    across = lax.broadcasted_iota(jnp.int32, (2 * V, 3 * B), 1)
-    wide_high = (lax.rem(across, B) // W == down) & (across < 2 * B) & (down < V)
-    wide_low = (lax.rem(across, B) // W == down - V) & (across >= 2 * B)
-    wide = (wide_high | wide_low).astype(BF16)
-
-    def halves(m, contract):
+    V, W, B, n, K = d.V, d.W, d.B, d.n, d.wall_k
+    stack = -(-V // 8) * 8
+
+    def expand(m, contract, high_mask, low_mask):
         high = m.astype(BF16)
         low = (m - high.astype(F32)).astype(BF16)
-        dims = (((1,), (contract,)), ((), ()))
-        parts = [lax.dot_general(spread, p, dims, preferred_element_type=F32) for p in (high, low)]
-        return jnp.concatenate(parts, axis=1).astype(BF16)
-
-    def spread_out(parts, mask):
-        return jnp.where(mask, dot(parts, wide), 0.0).astype(BF16)
-
-    couples = [halves(couple[n], 1) for n in range(6)]
-    for n in range(6):
-        mk[n * B : (n + 1) * B, :] = spread_out(couples[n], {2: lower, 3: upper}.get(n, same))
-    pk[...] = spread_out(halves(precond[...], 0), same)
-    down = lax.broadcasted_iota(jnp.int32, (2 * V, 6 * K), 0)
-    across = lax.broadcasted_iota(jnp.int32, (2 * V, 6 * K), 1)
-    wide_high = (lax.rem(across, K) == down) & (across < 4 * K) & (down < V)
-    wide_low = (lax.rem(across, K) == down - V) & (across >= 4 * K)
-    wide = (wide_high | wide_low).astype(BF16)
-    row = lax.rem(lax.broadcasted_iota(jnp.int32, (B, 6 * K), 0), W)
-    side = lax.rem(lax.broadcasted_iota(jnp.int32, (B, 6 * K), 1) // K, 2)
-    low_side = jnp.where((row == 0) & (side == 0), dot(couples[2], wide), 0.0)
-    high_side = jnp.where((row == W - 1) & (side == 1), dot(couples[3], wide), 0.0)
-    mw[...] = (low_side + high_side).astype(BF16)
+        dims = (((contract,), (0,)), ((), ()))
+        wide = lax.dot_general(high, high_mask, dims, preferred_element_type=F32)
+        wide = wide + lax.dot_general(low, low_mask, dims, preferred_element_type=F32)
+        extra = jnp.zeros((stack - V, wide.shape[1]), F32)
+        return jnp.concatenate([wide, extra], axis=0) if stack > V else wide
+
+    down = lax.broadcasted_iota(jnp.int32, (V, 3 * B), 0)
+    across = lax.broadcasted_iota(jnp.int32, (V, 3 * B), 1)
+    match = lax.rem(across, B) // W == down
+    high_mask, low_mask = (match & (across < 2 * B)), (match & (across >= 2 * B))
+    high_mask, low_mask = high_mask.astype(BF16), low_mask.astype(BF16)
+    blocks = [(couple[k // 2, k % 2], 0) for k in range(6)] + [(precond[...], 1)]
+    wide = [expand(m, contract, high_mask, low_mask) for m, contract in blocks]
+    wide = jnp.concatenate(wide, axis=0).astype(BF16)
+    lane = lax.broadcasted_iota(jnp.int32, (W, 7 * stack), 1)
+    spread = [(lane == k * stack + v).astype(F32) for k in range(7) for v in range(V)]
+    full = dot(jnp.concatenate(spread, axis=0).astype(BF16), wide)
+    row = lax.broadcasted_iota(jnp.int32, (W, 3 * B), 0)
+    col = lax.rem(lax.broadcasted_iota(jnp.int32, (W, 3 * B), 1), W)
+    same, lower, upper = [(col - row == k).astype(F32) for k in (0, -1, 1)]
+    for k in range(7):
+        mask = {2: lower, 3: upper}.get(k, same)
+        block = full[k * n : (k + 1) * n].reshape(V, W, 3 * B) * mask[None]
+        block = block.reshape(n, 3 * B).astype(BF16)
+        if k < 6:
+            mk[k * n : (k + 1) * n, :] = block
+        else:
+            pk[...] = block
+    down = lax.broadcasted_iota(jnp.int32, (V, 6 * K), 0)
+    across = lax.broadcasted_iota(jnp.int32, (V, 6 * K), 1)
+    match = lax.rem(across, K) == down
+    side = lax.rem(across // K, 2)
+    wide = [
+        expand(
+            couple[1, k],
+            0,
+            (match & (side == k) & (across < 4 * K)).astype(BF16),
+            (match & (side == k) & (across >= 4 * K)).astype(BF16),
+        )
+        for k in range(2)
+    ]
+    wide = jnp.concatenate(wide, axis=0).astype(BF16)
+    lane = lax.broadcasted_iota(jnp.int32, (W, 2 * stack), 1)
+    row = lax.broadcasted_iota(jnp.int32, (W, 2 * stack), 0)
+    spread = [
+        (((lane == v) & (row == 0)) | ((lane == stack + v) & (row == W - 1))).astype(F32)
+        for v in range(V)
+    ]
+    mw[...] = dot(jnp.concatenate(spread, axis=0).astype(BF16), wide).astype(BF16)
 
 
 def make_wall(d, codes, mask, table, gain, wall_out):
@@ -203,8 +239,7 @@
 
 
 def sweep_local(d, adj, src, vel, snd, mk, wall_coef, rates_of, out, rs_out):
-    V, X, W, Z, B = d.V, d.X, d.W, d.Z, d.B
-    n = V * W
+    V, X, W, Z, n = d.V, d.X, d.W, d.Z, d.n
     lane, row = lanes(d, W), row_ids(d)
     wall_flag = (lax.axis_index("wall") == 0).astype(F32)
     radius = [[radius_at(d, vel, snd, k, x) for x in range(X)] for k in range(3)]
@@ -213,7 +248,7 @@
 
     def product(x, k):
         chunk, offset = products[x]
-        return chunk[k * B : k * B + n, offset * Z : (offset + 1) * Z]
+        return chunk[k * n : (k + 1) * n, offset * Z : (offset + 1) * Z]
 
     def finish(x):
         a = d.plane(adj, x)
@@ -240,7 +275,7 @@
             rs_out[d.block(0, x), :] = total
         else:
             total = rates_of[d.block(0, x), :]
-        result = d.plane(src, x) - d.each(total) * a
+        result = d.plane3(src, x) - d.each(total) * a
         for rate, value in terms:
             result = result - d.each(rate) * value
         d.store_plane(out, x, result)
@@ -262,7 +297,8 @@
 
 
 def first_local_kernel(
-    d, adj, src, vel, snd, couple, precond, codes, mask, table, gain, out, rs, mk, mw, pk, wall_coef
+    d, adj, src, vel, snd, couple, precond, codes, mask, table, gain,
+    out, rs, mk, mw, pk, wall_coef,
 ):
     make_matrices(d, couple, precond, mk, mw, pk)
     make_wall(d, codes, mask, table, gain, wall_coef)
@@ -274,8 +310,7 @@
 
 
 def halo_terms(d, s0, s1, w0, w1, zl, zr, mk, mw):
-    V, X, W, Z, G, B = d.V, d.X, d.W, d.Z, d.G, d.B
-    n = V * W
+    V, X, W, Z, G, n = d.V, d.X, d.W, d.Z, d.G, d.n
     even_s, even_w = parity("stream"), parity("wall")
     si, wi = lax.axis_index("stream"), lax.axis_index("wall")
     has = lambda flag: flag.astype(F32)
@@ -283,7 +318,8 @@
     w_low, w_high = has(wi > 0), has(wi < lax.axis_size("wall") - 1)
     low = jnp.where(even_s, s1[...], s0[...]) * s_low
     high = jnp.where(even_s, s0[...], s1[...]) * s_high
-    stream = (dot(mk[:B], split3(low))[:n], dot(mk[B : 2 * B], split3(high))[:n])
+    both = dot(mk[: 2 * n], split3(jnp.concatenate([low, high], axis=1)))
+    stream = both[:n, :Z], both[n:, Z:]
     stream_radius = (low[n : n + W], high[n : n + W])
 
     def wall_rows(x):
@@ -312,9 +348,9 @@
         pieces.append(pltpu.roll(value, turn, 1) if turn else value)
     span_radius = jnp.where(even, pieces[V], pltpu.roll(pieces[V], Z - 2, 1))
     pieces += [jnp.zeros((W, Z), F32)] * (G - V - 1)
-    both = dot(mk[4 * B : 6 * B], split3(jnp.concatenate(pieces, axis=0)))
+    both = dot(mk[4 * n :], split3(jnp.concatenate(pieces, axis=0)))
     even = lax.rem(lanes(d, n), 2) == 0
-    span = jnp.where(even, both[:n], pltpu.roll(both[B : B + n], Z - 2, 1))
+    span = jnp.where(even, both[:n], pltpu.roll(both[n:], Z - 2, 1))
     at = lambda value, x: pltpu.roll(value, (Z - 2 * x) % Z, 1) if x else value
     return (
         stream,
@@ -405,9 +441,10 @@
 
 
 def last_halo_kernel(
-    d, partial, adj, rs_full, rates, s0, s1, w0, w1, zl, zr, mk, mw, pk, new_adj, residual
+    d, partial, adj, rs_full, rates, s0, s1, w0, w1, zl, zr, mk, mw, pk,
+    new_adj, residual, new_adj_here, residual_here, sems,
 ):
-    X, W = d.X, d.W
+    X, W, Z = d.X, d.W, d.Z
     halo = halo_terms(d, s0, s1, w0, w1, zl, zr, mk, mw)
 
     def halo_rates(x):
@@ -415,13 +452,25 @@
         high = rates[pl.ds((2 * X + 1) * W, W), :] if x == X - 1 else None
         return low, high, rates[d.block(0, x), :], rates[d.block(1, x), :]
 
+    copies = []
+
     def put(x, new, res):
-        d.store_plane(new_adj, x, new)
-        d.store_plane(residual, x, res)
+        here = d.planes_at(x, 1)
+        new_adj_here[here] = new.reshape(d.V, W, Z)
+        residual_here[here] = res.reshape(d.V, W, Z)
+        if (x + 1) % STORE == 0 or x == X - 1:
+            start = x - x % STORE
+            part = d.planes_at(start, x + 1 - start)
+            for k, (a, b) in enumerate(((new_adj_here, new_adj), (residual_here, residual))):
+                copy = pltpu.make_async_copy(a.at[part], b.at[part], sems.at[k, start // STORE])
+                copy.start()
+                copies.append(copy)
 
     finish_sweep(
         d, partial, adj, lambda x: rs_full[d.block(0, x), :], halo_rates, None, halo, mw, pk, put
     )
+    for copy in copies:
+        copy.wait()
 
 
 def exchange_pairs(sizes, axis, odd, spare):
@@ -458,55 +507,67 @@
     return s0, s1, w0, w1, zl, zr
 
 
-def call(kernel, d, outs, flops, args, in_vmem=True, out_vmem=True):
-    name = kernel.__name__
-    if out_vmem:
-        shapes = tuple(pltpu.VMEM(s, t) for s, t in outs)
-    else:
-        shapes = tuple(jax.ShapeDtypeStruct(s, t) for s, t in outs)
-    if in_vmem:
-        args = [pltpu.with_memory_space_constraint(a, pltpu.VMEM) for a in args]
+def call(kernel, d, outs, flops, args, held=(), scratch=(), out_held=False):
+    space = lambda k: pltpu.HBM if k in held else pltpu.VMEM
+    out_space = pltpu.HBM if out_held else pltpu.VMEM
+    args = [pltpu.with_memory_space_constraint(a, space(k)) for k, a in enumerate(args)]
     moved = sum(int(np.prod(a.shape)) * a.dtype.itemsize for a in args)
     return pl.pallas_call(
         functools.partial(kernel, d),
-        out_shape=shapes,
-        in_specs=[pl.BlockSpec(memory_space=pltpu.VMEM)] * len(args),
-        out_specs=tuple(pl.BlockSpec(memory_space=pltpu.VMEM) for _ in outs),
+        out_shape=tuple(out_space(s, t) for s, t in outs),
+        in_specs=[pl.BlockSpec(memory_space=space(k)) for k in range(len(args))],
+        out_specs=tuple(pl.BlockSpec(memory_space=out_space) for _ in outs),
+        scratch_shapes=scratch,
         compiler_params=pltpu.CompilerParams(vmem_limit_bytes=24 * 2**20),
         cost_estimate=pl.CostEstimate(flops=flops, bytes_accessed=moved, transcendentals=0),
-        name=name,
+        name=kernel.__name__,
     )(*args)
 
 
 def on_device(sizes, adj, source, velocity, sound, couple, precond, codes, mask, table, gain):
     shape = adj.shape
     d = Dims(shape)
-    X, W, Z, B = d.X, d.W, d.Z, d.B
-    adj = adj.reshape(d.rows, Z)
-    source = source.reshape(d.rows, Z)
-    velocity = velocity.reshape(3 * X * W, Z)
-    sound = sound.reshape(X * W, Z)
-    couple = couple.reshape((6,) + couple.shape[2:])
-    gain = gain.reshape(1, -1)
-    vmem = lambda a: pltpu.with_memory_space_constraint(a, pltpu.VMEM)
-
+    V, X, W, Z, B, n = d.V, d.X, d.W, d.Z, d.B, d.n
+    inputs = [
+        adj.reshape(d.rows, Z),
+        velocity.reshape(3 * X * W, Z),
+        sound.reshape(X * W, Z),
+        precond,
+        codes,
+        mask,
+        table,
+        gain.reshape(1, -1),
+    ]
+    source = source.reshape(V, X * W, Z)
     faces = [((B, Z), F32)] * 2 + [((d.wall_rows, Z), F32)] * 2 + [((d.span_groups * W, Z), F32)]
     field, scalar = ((d.rows, Z), F32), ((X * W, Z), F32)
-    packets = call(pack_kernel, d, faces, 0, [adj, velocity, sound])
-    got = swap_lines(sizes, *packets)
+    planes = ((V, X * W, Z), F32)
+    stores = -(-X // STORE)
+    sems = lambda *counts: pltpu.SemaphoreType.DMA(counts)
+    *kept, s_a, s_b, w_a, w_b, z = call(
+        pack_kernel,
+        d,
+        [(a.shape, a.dtype) for a in inputs] + faces,
+        0,
+        inputs,
+        held=range(len(inputs)),
+        scratch=[sems(len(inputs))],
+    )
+    adj, velocity, sound = kept[:3]
+    got = swap_lines(sizes, s_a, s_b, w_a, w_b, z)
     partial, rs, mk, mw, pk, wall_coef = call(
         first_local_kernel,
         d,
         [
             field,
             scalar,
-            ((6 * B, 3 * B), BF16),
-            ((B, 6 * d.wall_k), BF16),
-            ((B, 3 * B), BF16),
-            ((d.V, X * Z), F32),
+            ((6 * n, 3 * B), BF16),
+            ((n, 6 * d.wall_k), BF16),
+            ((n, 3 * B), BF16),
+            ((V, X * Z), F32),
         ],
         10**9,
-        [adj, source, velocity, sound, couple, precond, codes, mask, table, gain],
+        [adj, source, velocity, sound, couple] + kept[3:],
     )
     adj1, rs_full, rates, *packets = call(
         first_halo_kernel,
@@ -517,15 +578,20 @@
     )
     got = swap_lines(sizes, *packets)
     (partial,) = call(
-        later_local_kernel, d, [field], 10**9, [adj1, source, velocity, sound, rs_full, mk, wall_coef]
+        later_local_kernel,
+        d,
+        [field],
+        10**9,
+        [adj1, source, velocity, sound, rs_full, mk, wall_coef],
     )
     adj2, residual = call(
         last_halo_kernel,
         d,
-        [field, field],
+        [planes, planes],
         10**8,
         [partial, adj1, rs_full, rates, *got, mk, mw, pk],
-        out_vmem=False,
+        scratch=[pltpu.VMEM(*planes), pltpu.VMEM(*planes), sems(2, stores)],
+        out_held=True,
     )
     return adj2.reshape(shape), residual.reshape(shape)
 

time: 25 us -> 22.3 us (0.89)
  local copies, waits for them, and re-layouts: 3.54 us -> 0.02 us
  Pallas kernels: 9.2 us -> 10.2 us
    unnamed x23 -> x5, local copies, waits for them, and re-layouts: 3.54 us -> 0.02 us
    pallas_call x5, Pallas kernels: 9.2 us -> 10.2 us  [call(): pl.pallas_call(functools.partial(kernel, d), out_shape=tuple((out_space(s...]
  transfers between devices with their start and end apart: 10 -> 10, of which waited for: 1 -> 1; matrix products, arithmetic and copies ran while one was open for 0% -> 0% of each run, Pallas kernels for 19% -> 21%
where the time goes in v1:
time: 22.3 us; the launch traced here: 22.2 us
  starting transfers between devices  10.7 us (48%)
  Pallas kernels  10.2 us (46%)
  between operations  0.76 us (3%)
  waiting for transfers between devices  0.49 us (2%)
    pallas_call x5, Pallas kernels, call(): pl.pallas_call(functools.partial(kernel, d), out_shape=tuple((out_space(s...  10.2 us
    ppermute x8, starting transfers between devices, swap_lines(): move = lambda value, pairs: lax.ppermute(value, AXES, pairs)  9.97 us
    ppermute x2, starting transfers between devices, swap_lines(): zl = zr = lax.ppermute(z, 'span', [(0, 1), (1, 0)])  0.73 us
    ppermute x8, waiting for transfers between devices, swap_lines(): move = lambda value, pairs: lax.ppermute(value, AXES, pairs)  0.49 us
  transfers between devices with their start and end apart: 10, of which 1 were waited for; matrix products, arithmetic and copies ran while one was open for 0% of the time, Pallas kernels for 21%

profile of v1, /device:TPU:0, one launch (start us, length us, event | category | flops | bytes accessed | tf_op | source)
XLA Modules:
  0.0 22.2 jit_solution(1319881644352172026)
XLA Ops:
  0.7 1.7 %pack_kernel.1 = (f32[1632,128]{1,0:T(8,128)S(1)}, f32[288,128]{1,0:T(8,128)S(1)}, f32[96,128]{1,0:T(8,128)S(1)}, f32[17,17]{1,0:T(8,128)S(1)}, s32[48,256]{1,0:...) custom-call(f32[1632,128]{1,0:T(8,128)} %bitcast.9, ...), custom_call_target="tpu_custom_call" | custom-call | bytes 1131992 | tf_op jit(solution)/shard_map/pack_kernel/pallas_call | solution.py:515
  2.4 0.5 %collective-permute-start.2 = (f32[224,128]{1,0:T(8,128)S(1)}, f32[224,128]{1,0:T(8,128)S(1)}, u32[]{:S(2)}, u32[]{:S(2)}) collective-permute-start(f32[224,128]{1,0:T(8,128)S(1)} %get-tuple-element.43), channel_id=1, source_target_pairs={{0,1},{1,0},{2,3},{3,2},{4,5},{5,4},{6,7},{7,6},{8,9},{9,8},{10,11... | collective-permute-start | bytes 344072 | tf_op jit(solution)/shard_map/ppermute | solution.py:493
  2.9 2.6 %collective-permute-start.3 = (f32[224,128]{1,0:T(8,128)S(1)}, f32[224,128]{1,0:T(8,128)S(1)}, u32[]{:S(2)}, u32[]{:S(2)}) collective-permute-start(f32[224,128]{1,0:T(8,128)S(1)} %get-tuple-element.44), channel_id=1, source_target_pairs={{0,4},{1,2},{2,1},{3,7},{4,0},{5,6},{6,5},{7,3},{8,12},{9,10},{10,... | collective-permute-start | bytes 344072 | tf_op jit(solution)/shard_map/ppermute | solution.py:493
  5.5 0.1 collective-permute-start.4
  5.6 2.0 %collective-permute-start = (f32[144,128]{1,0:T(8,128)S(1)}, f32[144,128]{1,0:T(8,128)S(1)}, u32[]{:S(2)}, u32[]{:S(2)}) collective-permute-start(f32[144,128]{1,0:T(8,128)S(1)} %get-tuple-element.41), channel_id=1, source_target_pairs={{0,8},{1,9},{2,10},{3,11},{4,12},{5,13},{6,14},{7,15},{8,0},{9,1},... | collective-permute-start | bytes 221192 | tf_op jit(solution)/shard_map/ppermute | solution.py:493
  7.6 0.5 %collective-permute-start.1 = (f32[144,128]{1,0:T(8,128)S(1)}, f32[144,128]{1,0:T(8,128)S(1)}, u32[]{:S(2)}, u32[]{:S(2)}) collective-permute-start(f32[144,128]{1,0:T(8,128)S(1)} %get-tuple-element.42), channel_id=1, source_target_pairs={{0,1},{1,0},{2,3},{3,2},{4,5},{5,4},{6,7},{7,6},{8,16},{9,17},{10,... | collective-permute-start | bytes 221192 | tf_op jit(solution)/shard_map/ppermute | solution.py:493
  8.1 2.7 %first_local_kernel.1 = (f32[1632,128]{1,0:T(8,128)S(1)}, f32[96,128]{1,0:T(8,128)S(1)}, bf16[816,432]{1,0:T(8,128)(2,1)S(1)}, bf16[136,144]{1,0:T(8,128)(2,1)S(...) custom-call(f32[1632,128]{1,0:T(8,128)S(1)} %get-tuple-element.31.adj, f32[17,96,128]{2,1,0:T(8,128)S(1)} %bitcast.7, ...), custom_call_target="tpu_custom_call" | custom-call | flops 1000000000 | bytes 1974512 | tf_op jit(solution)/shard_map/first_local_kernel/pallas_call | solution.py:515
  10.9 0.0 collective-permute-done.4.zl.zr
  10.9 0.0 collective-permute-done.s0
  10.9 0.0 collective-permute-done.1.s1
  10.9 0.0 collective-permute-done.2.w0
  10.9 0.0 collective-permute-done.3.w1
  10.9 1.6 %first_halo_kernel.1 = (f32[1632,128]{1,0:T(8,128)S(1)}, f32[96,128]{1,0:T(8,128)S(1)}, f32[208,128]{1,0:T(8,128)S(1)}, f32[144,128]{1,0:T(8,128)S(1)}, f32[144,...) custom-call(f32[1632,128]{1,0:T(8,128)S(1)} %get-tuple-element.39.partial, ...), custom_call_target="tpu_custom_call" | custom-call | flops 100000000 | bytes 3188224 | tf_op jit(solution)/shard_map/first_halo_kernel/pallas_call | solution.py:515
  12.6 0.1 collective-permute-start.7
  12.6 1.4 %collective-permute-start.8 = (f32[224,128]{1,0:T(8,128)S(1)}, f32[224,128]{1,0:T(8,128)S(1)}, u32[]{:S(2)}, u32[]{:S(2)}) collective-permute-start(f32[224,128]{1,0:T(8,128)S(1)} %get-tuple-element.56), channel_id=1, source_target_pairs={{0,4},{1,2},{2,1},{3,7},{4,0},{5,6},{6,5},{7,3},{8,12},{9,10},{10,... | collective-permute-start | bytes 344072 | tf_op jit(solution)/shard_map/ppermute | solution.py:493
  14.1 0.6 %collective-permute-start.9 = (f32[32,128]{1,0:T(8,128)S(1)}, f32[32,128]{1,0:T(8,128)S(1)}, u32[]{:S(2)}, u32[]{:S(2)}) collective-permute-start(f32[32,128]{1,0:T(8,128)S(1)} %get-tuple-element.57), channel_id=1, source_target_pairs={{0,4},{4,0},{1,5},{5,1},{2,6},{6,2},{3,7},{7,3},{8,12},{12,8},{9,1... | collective-permute-start | bytes 49160 | tf_op jit(solution)/shard_map/ppermute | solution.py:502
  14.7 2.8 %collective-permute-start.5 = (f32[144,128]{1,0:T(8,128)S(1)}, f32[144,128]{1,0:T(8,128)S(1)}, u32[]{:S(2)}, u32[]{:S(2)}) collective-permute-start(f32[144,128]{1,0:T(8,128)S(1)} %get-tuple-element.53), channel_id=1, source_target_pairs={{0,8},{1,9},{2,10},{3,11},{4,12},{5,13},{6,14},{7,15},{8,0},{9,1},... | collective-permute-start | bytes 221192 | tf_op jit(solution)/shard_map/ppermute | solution.py:493
  17.5 0.0 collective-permute-start.6
  17.5 1.8 %later_local_kernel.1.partial = f32[1632,128]{1,0:T(8,128)S(1)} custom-call(f32[1632,128]{1,0:T(8,128)S(1)} %get-tuple-element.49.adj, f32[17,96,128]{2,1,0:T(8,128)S(1)} %bitcast.8, f32[288,128]{1,0:T(8,128)S(1)} %get-tuple-element.32.vel, f32[96,128]{1,0:T(8,128)S(1)} %get-tuple-element.33.snd, f32[96,128]{1,0:T(8,128)S(1)} %get-tuple-element.50.rs.rs_full, ...), custom_call_target="tpu_custom_call" | custom-call | flops 1000000000 | bytes 2726400 | tf_op jit(solution)/shard_map/later_local_kernel/pallas_call | solution.py:515
  19.4 0.0 collective-permute-done.9.zl.zr
  19.4 0.5 %collective-permute-done.5.s0 = f32[144,128]{1,0:T(8,128)S(1)} collective-permute-done((f32[144,128]{1,0:T(8,128)S(1)}, f32[144,128]{1,0:T(8,128)S(1)}, u32[]{:S(2)}, u32[]{:S(2)}) %collective-permute-start.5) | collective-permute-done | bytes 73760 | tf_op jit(solution)/shard_map/ppermute | solution.py:493
  19.9 0.0 collective-permute-done.6.s1
  19.9 0.0 collective-permute-done.7.w0
  19.9 2.3 %last_halo_kernel.1 = (f32[17,96,128]{2,1,0:T(8,128)}, f32[17,96,128]{2,1,0:T(8,128)}) custom-call(f32[1632,128]{1,0:T(8,128)S(1)} %later_local_kernel.1.partial, f32[1632,128]{1,0:T(8,128)S(1)} %get-tuple-element.49.adj, f32[96,128]{1,0:T(8,128)S(1)} %get-tuple-element.50.rs.rs_full, f32[208,128]{1,0:T(8,128)S(1)} %get-tuple-element.52.rates, ...), custom_call_target="tpu_custom_call" | custom-call | flops 100000000 | bytes 3098112 | tf_op jit(solution)/shard_map/last_halo_kernel/pallas_call | solution.py:515
  (6 shorter events, 0.0 us)
Async XLA Ops:
  0.6 7.5 %copy-start = (f32[17,12,8,128]{3,2,1,0:T(8,128)S(1)}, f32[17,12,8,128]{3,2,1,0:T(8,128)}, u32[]{:S(2)}) copy-start(f32[17,12,8,128]{3,2,1,0:T(8,128)} %param.11) | copy-start | bytes 2506756
  0.6 7.5 %copy-start.1 = (f32[3,2,17,17]{3,1,2,0:T(2,128)S(1)}, f32[3,2,17,17]{3,1,2,0:T(2,128)}, u32[]{:S(2)}) copy-start(f32[3,2,17,17]{3,1,2,0:T(2,128)} %param.14) | copy-start | bytes 20812
  2.4 8.5 %collective-permute-start.2 = (f32[224,128]{1,0:T(8,128)S(1)}, f32[224,128]{1,0:T(8,128)S(1)}, u32[]{:S(2)}, u32[]{:S(2)}) collective-permute-start(f32[224,128]{1,0:T(8,128)S(1)} %get-tuple-element.43), channel_id=1, source_target_pairs={{0,1},{1,0},{2,3},{3,2},{4,5},{5,4},{6,7},{7,6},{8,9},{9,8},{10,11... | collective-permute-start | bytes 344072 | tf_op jit(solution)/shard_map/ppermute | solution.py:493
  2.9 8.0 %collective-permute-start.3 = (f32[224,128]{1,0:T(8,128)S(1)}, f32[224,128]{1,0:T(8,128)S(1)}, u32[]{:S(2)}, u32[]{:S(2)}) collective-permute-start(f32[224,128]{1,0:T(8,128)S(1)} %get-tuple-element.44), channel_id=1, source_target_pairs={{0,4},{1,2},{2,1},{3,7},{4,0},{5,6},{6,5},{7,3},{8,12},{9,10},{10,... | collective-permute-start | bytes 344072 | tf_op jit(solution)/shard_map/ppermute | solution.py:493
  5.5 5.4 %collective-permute-start.4 = (f32[32,128]{1,0:T(8,128)S(1)}, f32[32,128]{1,0:T(8,128)S(1)}, u32[]{:S(2)}, u32[]{:S(2)}) collective-permute-start(f32[32,128]{1,0:T(8,128)S(1)} %get-tuple-element.45), channel_id=1, source_target_pairs={{0,4},{4,0},{1,5},{5,1},{2,6},{6,2},{3,7},{7,3},{8,12},{12,8},{9,1... | collective-permute-start | bytes 49160 | tf_op jit(solution)/shard_map/ppermute | solution.py:502
  5.6 5.3 %collective-permute-start = (f32[144,128]{1,0:T(8,128)S(1)}, f32[144,128]{1,0:T(8,128)S(1)}, u32[]{:S(2)}, u32[]{:S(2)}) collective-permute-start(f32[144,128]{1,0:T(8,128)S(1)} %get-tuple-element.41), channel_id=1, source_target_pairs={{0,8},{1,9},{2,10},{3,11},{4,12},{5,13},{6,14},{7,15},{8,0},{9,1},... | collective-permute-start | bytes 221192 | tf_op jit(solution)/shard_map/ppermute | solution.py:493
  7.6 3.3 %collective-permute-start.1 = (f32[144,128]{1,0:T(8,128)S(1)}, f32[144,128]{1,0:T(8,128)S(1)}, u32[]{:S(2)}, u32[]{:S(2)}) collective-permute-start(f32[144,128]{1,0:T(8,128)S(1)} %get-tuple-element.42), channel_id=1, source_target_pairs={{0,1},{1,0},{2,3},{3,2},{4,5},{5,4},{6,7},{7,6},{8,16},{9,17},{10,... | collective-permute-start | bytes 221192 | tf_op jit(solution)/shard_map/ppermute | solution.py:493
  12.6 7.3 %collective-permute-start.7 = (f32[224,128]{1,0:T(8,128)S(1)}, f32[224,128]{1,0:T(8,128)S(1)}, u32[]{:S(2)}, u32[]{:S(2)}) collective-permute-start(f32[224,128]{1,0:T(8,128)S(1)} %get-tuple-element.55), channel_id=1, source_target_pairs={{0,1},{1,0},{2,3},{3,2},{4,5},{5,4},{6,7},{7,6},{8,9},{9,8},{10,11... | collective-permute-start | bytes 344072 | tf_op jit(solution)/shard_map/ppermute | solution.py:493
  12.6 7.2 %collective-permute-start.8 = (f32[224,128]{1,0:T(8,128)S(1)}, f32[224,128]{1,0:T(8,128)S(1)}, u32[]{:S(2)}, u32[]{:S(2)}) collective-permute-start(f32[224,128]{1,0:T(8,128)S(1)} %get-tuple-element.56), channel_id=1, source_target_pairs={{0,4},{1,2},{2,1},{3,7},{4,0},{5,6},{6,5},{7,3},{8,12},{9,10},{10,... | collective-permute-start | bytes 344072 | tf_op jit(solution)/shard_map/ppermute | solution.py:493
  14.1 5.3 %collective-permute-start.9 = (f32[32,128]{1,0:T(8,128)S(1)}, f32[32,128]{1,0:T(8,128)S(1)}, u32[]{:S(2)}, u32[]{:S(2)}) collective-permute-start(f32[32,128]{1,0:T(8,128)S(1)} %get-tuple-element.57), channel_id=1, source_target_pairs={{0,4},{4,0},{1,5},{5,1},{2,6},{6,2},{3,7},{7,3},{8,12},{12,8},{9,1... | collective-permute-start | bytes 49160 | tf_op jit(solution)/shard_map/ppermute | solution.py:502
  14.7 5.1 %collective-permute-start.5 = (f32[144,128]{1,0:T(8,128)S(1)}, f32[144,128]{1,0:T(8,128)S(1)}, u32[]{:S(2)}, u32[]{:S(2)}) collective-permute-start(f32[144,128]{1,0:T(8,128)S(1)} %get-tuple-element.53), channel_id=1, source_target_pairs={{0,8},{1,9},{2,10},{3,11},{4,12},{5,13},{6,14},{7,15},{8,0},{9,1},... | collective-permute-start | bytes 221192 | tf_op jit(solution)/shard_map/ppermute | solution.py:493
  17.5 2.3 %collective-permute-start.6 = (f32[144,128]{1,0:T(8,128)S(1)}, f32[144,128]{1,0:T(8,128)S(1)}, u32[]{:S(2)}, u32[]{:S(2)}) collective-permute-start(f32[144,128]{1,0:T(8,128)S(1)} %get-tuple-element.54), channel_id=1, source_target_pairs={{0,1},{1,0},{2,3},{3,2},{4,5},{5,4},{6,7},{7,6},{8,16},{9,17},{10,... | collective-permute-start | bytes 221192 | tf_op jit(solution)/shard_map/ppermute | solution.py:493

commit v2 on v1

--- a/solution.py
+++ b/solution.py
@@ -11,8 +11,7 @@
 AXES = ("stream", "span", "wall")
 F32 = jnp.float32
 BF16 = jnp.bfloat16
-HIGHEST = lax.Precision.HIGHEST
-STORE = 6
+STORE = 4
 
 
 class Dims:
@@ -26,6 +25,7 @@
         self.rows = self.n * self.X
         self.wall_rows = self.X * self.G + 8
         self.wall_k = -(-self.G // 8) * 8
+        self.stack = -(-self.V // 8) * 8
         self.per = self.Z // (2 * self.X)
         self.span_groups = -(-(self.V + 1) // self.per)
 
@@ -152,66 +152,51 @@
     )
 
 
-def make_matrices(d, couple, precond, mk, mw, pk):
-    V, W, B, n, K = d.V, d.W, d.B, d.n, d.wall_k
-    stack = -(-V // 8) * 8
-
-    def expand(m, contract, high_mask, low_mask):
-        high = m.astype(BF16)
-        low = (m - high.astype(F32)).astype(BF16)
-        dims = (((contract,), (0,)), ((), ()))
-        wide = lax.dot_general(high, high_mask, dims, preferred_element_type=F32)
-        wide = wide + lax.dot_general(low, low_mask, dims, preferred_element_type=F32)
-        extra = jnp.zeros((stack - V, wide.shape[1]), F32)
-        return jnp.concatenate([wide, extra], axis=0) if stack > V else wide
-
-    down = lax.broadcasted_iota(jnp.int32, (V, 3 * B), 0)
-    across = lax.broadcasted_iota(jnp.int32, (V, 3 * B), 1)
-    match = lax.rem(across, B) // W == down
-    high_mask, low_mask = (match & (across < 2 * B)), (match & (across >= 2 * B))
-    high_mask, low_mask = high_mask.astype(BF16), low_mask.astype(BF16)
-    blocks = [(couple[k // 2, k % 2], 0) for k in range(6)] + [(precond[...], 1)]
-    wide = [expand(m, contract, high_mask, low_mask) for m, contract in blocks]
-    wide = jnp.concatenate(wide, axis=0).astype(BF16)
-    lane = lax.broadcasted_iota(jnp.int32, (W, 7 * stack), 1)
-    spread = [(lane == k * stack + v).astype(F32) for k in range(7) for v in range(V)]
-    full = dot(jnp.concatenate(spread, axis=0).astype(BF16), wide)
+def make_matrices(d, couple, precond, mk, mw, pk, wide, wide_wall):
+    V, W, B, n, K, S = d.V, d.W, d.B, d.n, d.wall_k, d.stack
+    gap = jnp.zeros((V, S - V), F32)
+    blocks = [couple[k // 2, k % 2] for k in range(6)] + [precond[...].T]
+    blocks = [piece for m in blocks for piece in ((m, gap) if S > V else (m,))]
+    blocks = jnp.concatenate(blocks, axis=1)
+    high = blocks.astype(BF16).astype(F32)
+    gap = jnp.zeros((S - V, 7 * S), F32)
+    pieces = (high, gap, blocks - high, gap) if S > V else (high, blocks - high)
+    blocks = jnp.concatenate(pieces, axis=0).astype(BF16)
+    dims = (((0,), (0,)), ((), ()))
+
+    def spread(some, width, keep):
+        row = lax.broadcasted_iota(jnp.int32, (2 * S, 3 * width), 0)
+        col = lax.broadcasted_iota(jnp.int32, (2 * S, 3 * width), 1)
+        part = keep(lax.rem(col, width), jnp.where(row < S, row, row - S))
+        part = part & ((row < S) == (col < 2 * width))
+        return lax.dot_general(some, part.astype(BF16), dims, preferred_element_type=F32)
+
+    wide[...] = spread(blocks, B, lambda col, v: col // W == v)
+    for side in range(2):
+        some = blocks[:, (2 + side) * S : (3 + side) * S]
+        wide_wall[side * S : (side + 1) * S, :] = spread(some, 2 * K, lambda col, v: col - side * K == v)
     row = lax.broadcasted_iota(jnp.int32, (W, 3 * B), 0)
     col = lax.rem(lax.broadcasted_iota(jnp.int32, (W, 3 * B), 1), W)
     same, lower, upper = [(col - row == k).astype(F32) for k in (0, -1, 1)]
-    for k in range(7):
+
+    def rows(k):
         mask = {2: lower, 3: upper}.get(k, same)
-        block = full[k * n : (k + 1) * n].reshape(V, W, 3 * B) * mask[None]
-        block = block.reshape(n, 3 * B).astype(BF16)
-        if k < 6:
-            mk[k * n : (k + 1) * n, :] = block
-        else:
-            pk[...] = block
-    down = lax.broadcasted_iota(jnp.int32, (V, 6 * K), 0)
-    across = lax.broadcasted_iota(jnp.int32, (V, 6 * K), 1)
-    match = lax.rem(across, K) == down
-    side = lax.rem(across // K, 2)
-    wide = [
-        expand(
-            couple[1, k],
-            0,
-            (match & (side == k) & (across < 4 * K)).astype(BF16),
-            (match & (side == k) & (across >= 4 * K)).astype(BF16),
-        )
-        for k in range(2)
+        return [wide[pl.ds(k * S + v, 1), :] * mask for v in range(V)]
+
+    for k in range(0, 6, 2):
+        both = jnp.concatenate(rows(k) + rows(k + 1), axis=0)
+        mk[k * n : (k + 2) * n, :] = both.astype(BF16)
+    pk[...] = jnp.concatenate(rows(6), axis=0).astype(BF16)
+    row = lax.broadcasted_iota(jnp.int32, (W, 6 * K), 0)
+    first, last = (row == 0).astype(F32), (row == W - 1).astype(F32)
+    pieces = [
+        wide_wall[pl.ds(v, 1), :] * first + wide_wall[pl.ds(S + v, 1), :] * last for v in range(V)
     ]
-    wide = jnp.concatenate(wide, axis=0).astype(BF16)
-    lane = lax.broadcasted_iota(jnp.int32, (W, 2 * stack), 1)
-    row = lax.broadcasted_iota(jnp.int32, (W, 2 * stack), 0)
-    spread = [
-        (((lane == v) & (row == 0)) | ((lane == stack + v) & (row == W - 1))).astype(F32)
-        for v in range(V)
-    ]
-    mw[...] = dot(jnp.concatenate(spread, axis=0).astype(BF16), wide).astype(BF16)
+    mw[...] = jnp.concatenate(pieces, axis=0).astype(BF16)
 
 
 def make_wall(d, codes, mask, table, gain, wall_out):
-    X, Z = d.X, d.Z
+    X, Z, V, S = d.X, d.Z, d.V, d.stack
     place = lax.axis_index("stream")
     lane0 = pl.multiple_of(lax.axis_index("span") * Z, Z)
     kinds = table.shape[0]
@@ -223,19 +208,15 @@
         return value
 
     code, spall = window(codes), window(mask).astype(F32)
-    pieces = []
+    column = lambda values: jnp.broadcast_to(values.T, (V, Z))
+    columns = [column(table[k : k + 1, :]) for k in range(kinds)]
+    gains = column(gain[...])
     for x in range(X):
-        here = code[x : x + 1]
-        pieces.append(
-            jnp.concatenate(
-                [(here == k).astype(F32) for k in range(kinds)] + [spall[x : x + 1]], axis=0
-            )
-        )
-    hot = jnp.concatenate(pieces, axis=1)
-    full = jnp.concatenate([table[...], gain[...]], axis=0)
-    wall_out[...] = lax.dot_general(
-        full, hot, (((0,), (0,)), ((), ())), precision=HIGHEST, preferred_element_type=F32
-    )
+        here = jnp.broadcast_to(code[x : x + 1], (V, Z))
+        coef = columns[kinds - 1]
+        for k in range(kinds - 1):
+            coef = jnp.where(here == k, columns[k], coef)
+        wall_out[x * S : x * S + V, :] = coef + gains * spall[x : x + 1]
 
 
 def sweep_local(d, adj, src, vel, snd, mk, wall_coef, rates_of, out, rs_out):
@@ -281,7 +262,7 @@
         d.store_plane(out, x, result)
         spot = pl.ds(x * W, V, stride=X * W)
         factor = wall_flag * radius[1][x][:1]
-        coef = wall_coef[:, x * Z : (x + 1) * Z]
+        coef = wall_coef[x * d.stack : x * d.stack + V, :]
         out[spot, :] = out[spot, :] - factor * coef * adj[spot, :]
 
     done = 0
@@ -298,9 +279,9 @@
 
 def first_local_kernel(
     d, adj, src, vel, snd, couple, precond, codes, mask, table, gain,
-    out, rs, mk, mw, pk, wall_coef,
+    out, rs, mk, mw, pk, wall_coef, wide, wide_wall,
 ):
-    make_matrices(d, couple, precond, mk, mw, pk)
+    make_matrices(d, couple, precond, mk, mw, pk, wide, wide_wall)
     make_wall(d, codes, mask, table, gain, wall_coef)
     sweep_local(d, adj, src, vel, snd, mk, wall_coef, None, out, rs)
 
@@ -363,31 +344,44 @@
 
 
 def finish_sweep(d, partial, adj, rs_of, halo_rates, corrections, halo, mw, pk, put):
-    V, X, W, Z = d.V, d.X, d.W, d.Z
-    n = V * W
+    X, Z = d.X, d.Z
     stream, _, wall, _, span, _ = halo
+    walls = {}
     for start in range(0, X, 2):
         here = list(range(start, min(X, start + 2)))
-        from_wall = dot(mw[...], split3(jnp.concatenate([wall(x) for x in here], axis=1)))
-        residuals = []
+        value = dot(mw[...], split3(jnp.concatenate([wall(x) for x in here], axis=1)))
         for k, x in enumerate(here):
-            low, high, rate_wall, rate_span = halo_rates(x)
-            res = d.plane(partial, x)
-            if corrections is not None:
-                res = res - d.each(corrections(x)) * d.plane(adj, x)
-            res = res - d.each(rate_wall) * from_wall[:n, k * Z : (k + 1) * Z]
-            res = res - d.each(rate_span) * span(x)
-            if low is not None:
-                res = res - d.each(low) * stream[0]
-            if high is not None:
-                res = res - d.each(high) * stream[1]
-            residuals.append(res)
+            walls[x] = value[:, k * Z : (k + 1) * Z]
+
+    def residual(x):
+        low, high, rate_wall, rate_span = halo_rates(x)
+        res = d.plane(partial, x)
+        if corrections is not None:
+            res = res - d.each(corrections(x)) * d.plane(adj, x)
+        res = res - d.each(rate_wall) * walls[x]
+        res = res - d.each(rate_span) * span(x)
+        if low is not None:
+            res = res - d.each(low) * stream[0]
+        if high is not None:
+            res = res - d.each(high) * stream[1]
+        return res
+
+    def updated(here, residuals, update):
+        for k, x in enumerate(here):
+            inverse = 1.0 / rs_of(x)
+            new = d.plane(adj, x) + update[:, k * Z : (k + 1) * Z] * d.each(inverse)
+            put(x, new, residuals[k])
+
+    waiting = None
+    for start in range(0, X, 2):
+        here = list(range(start, min(X, start + 2)))
+        residuals = [residual(x) for x in here]
         right = jnp.concatenate([padded_plane(d, r) for r in residuals], axis=1)
         update = dot(pk[...], split3(right))
-        for k, x in enumerate(here):
-            inverse = 1.0 / rs_of(x)
-            new = d.plane(adj, x) + update[:n, k * Z : (k + 1) * Z] * d.each(inverse)
-            put(x, new, residuals[k])
+        if waiting:
+            updated(*waiting)
+        waiting = here, residuals, update
+    updated(*waiting)
 
 
 def first_halo_kernel(
@@ -564,10 +558,11 @@
             ((6 * n, 3 * B), BF16),
             ((n, 6 * d.wall_k), BF16),
             ((n, 3 * B), BF16),
-            ((V, X * Z), F32),
+            ((X * d.stack, Z), F32),
         ],
         10**9,
         [adj, source, velocity, sound, couple] + kept[3:],
+        scratch=[pltpu.VMEM((7 * d.stack, 3 * B), F32), pltpu.VMEM((2 * d.stack, 6 * d.wall_k), F32)],
     )
     adj1, rs_full, rates, *packets = call(
         first_halo_kernel,

time: 22.3 us -> 21.7 us (0.973)
  Pallas kernels: 10.2 us -> 9.19 us
  starting transfers between devices: 10.7 us -> 11.1 us
    pallas_call x5, Pallas kernels: 10.2 us -> 9.19 us  [call(): pl.pallas_call(functools.partial(kernel, d), out_shape=tuple((out_space(s...]
    ppermute x8, starting transfers between devices: 9.97 us -> 10.4 us  [swap_lines(): move = lambda value, pairs: lax.ppermute(value, AXES, pairs)]
  transfers between devices with their start and end apart: 10 -> 10, of which waited for: 1 -> 1; matrix products, arithmetic and copies ran while one was open for 0% -> 0% of each run, Pallas kernels for 21% -> 19%
where the time goes in v2:
time: 21.7 us; the launch traced here: 21.6 us
  starting transfers between devices  11.1 us (51%)
  Pallas kernels  9.19 us (42%)
  between operations  0.75 us (3%)
  waiting for transfers between devices  0.49 us (2%)
    ppermute x8, starting transfers between devices, swap_lines(): move = lambda value, pairs: lax.ppermute(value, AXES, pairs)  10.4 us
    pallas_call x5, Pallas kernels, call(): pl.pallas_call(functools.partial(kernel, d), out_shape=tuple((out_space(s...  9.19 us
    ppermute x2, starting transfers between devices, swap_lines(): zl = zr = lax.ppermute(z, 'span', [(0, 1), (1, 0)])  0.72 us
    ppermute x8, waiting for transfers between devices, swap_lines(): move = lambda value, pairs: lax.ppermute(value, AXES, pairs)  0.49 us
  transfers between devices with their start and end apart: 10, of which 1 were waited for; matrix products, arithmetic and copies ran while one was open for 0% of the time, Pallas kernels for 19%

profile of v2, /device:TPU:0, one launch (start us, length us, event | category | flops | bytes accessed | tf_op | source)
XLA Modules:
  0.0 21.6 jit_solution(3676215467997190098)
XLA Ops:
  0.7 1.7 %pack_kernel.1 = (f32[1632,128]{1,0:T(8,128)S(1)}, f32[288,128]{1,0:T(8,128)S(1)}, f32[96,128]{1,0:T(8,128)S(1)}, f32[17,17]{1,0:T(8,128)S(1)}, s32[48,256]{1,0:...) custom-call(f32[1632,128]{1,0:T(8,128)} %bitcast.9, ...), custom_call_target="tpu_custom_call" | custom-call | bytes 1131992 | tf_op jit(solution)/shard_map/pack_kernel/pallas_call | solution.py:509
  2.4 0.5 %collective-permute-start.2 = (f32[224,128]{1,0:T(8,128)S(1)}, f32[224,128]{1,0:T(8,128)S(1)}, u32[]{:S(2)}, u32[]{:S(2)}) collective-permute-start(f32[224,128]{1,0:T(8,128)S(1)} %get-tuple-element.43), channel_id=1, source_target_pairs={{0,1},{1,0},{2,3},{3,2},{4,5},{5,4},{6,7},{7,6},{8,9},{9,8},{10,11... | collective-permute-start | bytes 344072 | tf_op jit(solution)/shard_map/ppermute | solution.py:487
  2.9 2.6 %collective-permute-start.3 = (f32[224,128]{1,0:T(8,128)S(1)}, f32[224,128]{1,0:T(8,128)S(1)}, u32[]{:S(2)}, u32[]{:S(2)}) collective-permute-start(f32[224,128]{1,0:T(8,128)S(1)} %get-tuple-element.44), channel_id=1, source_target_pairs={{0,4},{1,2},{2,1},{3,7},{4,0},{5,6},{6,5},{7,3},{8,12},{9,10},{10,... | collective-permute-start | bytes 344072 | tf_op jit(solution)/shard_map/ppermute | solution.py:487
  5.5 0.1 collective-permute-start.4
  5.6 2.0 %collective-permute-start = (f32[144,128]{1,0:T(8,128)S(1)}, f32[144,128]{1,0:T(8,128)S(1)}, u32[]{:S(2)}, u32[]{:S(2)}) collective-permute-start(f32[144,128]{1,0:T(8,128)S(1)} %get-tuple-element.41), channel_id=1, source_target_pairs={{0,8},{1,9},{2,10},{3,11},{4,12},{5,13},{6,14},{7,15},{8,0},{9,1},... | collective-permute-start | bytes 221192 | tf_op jit(solution)/shard_map/ppermute | solution.py:487
  7.6 0.5 %collective-permute-start.1 = (f32[144,128]{1,0:T(8,128)S(1)}, f32[144,128]{1,0:T(8,128)S(1)}, u32[]{:S(2)}, u32[]{:S(2)}) collective-permute-start(f32[144,128]{1,0:T(8,128)S(1)} %get-tuple-element.42), channel_id=1, source_target_pairs={{0,1},{1,0},{2,3},{3,2},{4,5},{5,4},{6,7},{7,6},{8,16},{9,17},{10,... | collective-permute-start | bytes 221192 | tf_op jit(solution)/shard_map/ppermute | solution.py:487
  8.1 2.3 %first_local_kernel.1 = (f32[1632,128]{1,0:T(8,128)S(1)}, f32[96,128]{1,0:T(8,128)S(1)}, bf16[816,432]{1,0:T(8,128)(2,1)S(1)}, bf16[136,144]{1,0:T(8,128)(2,1)S(...) custom-call(f32[1632,128]{1,0:T(8,128)S(1)} %get-tuple-element.31.adj, f32[17,96,128]{2,1,0:T(8,128)S(1)} %bitcast.7, ...), custom_call_target="tpu_custom_call" | custom-call | flops 1000000000 | bytes 1974512 | tf_op jit(solution)/shard_map/first_local_kernel/pallas_call | solution.py:509
  10.4 0.0 collective-permute-done.4.zl.zr
  10.4 0.0 collective-permute-done.s0
  10.5 0.0 collective-permute-done.1.s1
  10.5 0.0 collective-permute-done.2.w0
  10.5 0.0 collective-permute-done.3.w1
  10.5 1.2 %first_halo_kernel.1 = (f32[1632,128]{1,0:T(8,128)S(1)}, f32[96,128]{1,0:T(8,128)S(1)}, f32[208,128]{1,0:T(8,128)S(1)}, f32[144,128]{1,0:T(8,128)S(1)}, f32[144,...) custom-call(f32[1632,128]{1,0:T(8,128)S(1)} %get-tuple-element.39.partial, ...), custom_call_target="tpu_custom_call" | custom-call | flops 100000000 | bytes 3188224 | tf_op jit(solution)/shard_map/first_halo_kernel/pallas_call | solution.py:509
  11.7 0.1 collective-permute-start.7
  11.8 1.4 %collective-permute-start.8 = (f32[224,128]{1,0:T(8,128)S(1)}, f32[224,128]{1,0:T(8,128)S(1)}, u32[]{:S(2)}, u32[]{:S(2)}) collective-permute-start(f32[224,128]{1,0:T(8,128)S(1)} %get-tuple-element.56), channel_id=1, source_target_pairs={{0,4},{1,2},{2,1},{3,7},{4,0},{5,6},{6,5},{7,3},{8,12},{9,10},{10,... | collective-permute-start | bytes 344072 | tf_op jit(solution)/shard_map/ppermute | solution.py:487
  13.3 0.6 %collective-permute-start.9 = (f32[32,128]{1,0:T(8,128)S(1)}, f32[32,128]{1,0:T(8,128)S(1)}, u32[]{:S(2)}, u32[]{:S(2)}) collective-permute-start(f32[32,128]{1,0:T(8,128)S(1)} %get-tuple-element.57), channel_id=1, source_target_pairs={{0,4},{4,0},{1,5},{5,1},{2,6},{6,2},{3,7},{7,3},{8,12},{12,8},{9,1... | collective-permute-start | bytes 49160 | tf_op jit(solution)/shard_map/ppermute | solution.py:496
  13.9 3.2 %collective-permute-start.5 = (f32[144,128]{1,0:T(8,128)S(1)}, f32[144,128]{1,0:T(8,128)S(1)}, u32[]{:S(2)}, u32[]{:S(2)}) collective-permute-start(f32[144,128]{1,0:T(8,128)S(1)} %get-tuple-element.53), channel_id=1, source_target_pairs={{0,8},{1,9},{2,10},{3,11},{4,12},{5,13},{6,14},{7,15},{8,0},{9,1},... | collective-permute-start | bytes 221192 | tf_op jit(solution)/shard_map/ppermute | solution.py:487
  17.1 0.0 collective-permute-start.6
  17.1 1.8 %later_local_kernel.1.partial = f32[1632,128]{1,0:T(8,128)S(1)} custom-call(f32[1632,128]{1,0:T(8,128)S(1)} %get-tuple-element.49.adj, f32[17,96,128]{2,1,0:T(8,128)S(1)} %bitcast.8, f32[288,128]{1,0:T(8,128)S(1)} %get-tuple-element.32.vel, f32[96,128]{1,0:T(8,128)S(1)} %get-tuple-element.33.snd, f32[96,128]{1,0:T(8,128)S(1)} %get-tuple-element.50.rs.rs_full, ...), custom_call_target="tpu_custom_call" | custom-call | flops 1000000000 | bytes 2769408 | tf_op jit(solution)/shard_map/later_local_kernel/pallas_call | solution.py:509
  19.0 0.0 collective-permute-done.9.zl.zr
  19.0 0.5 %collective-permute-done.5.s0 = f32[144,128]{1,0:T(8,128)S(1)} collective-permute-done((f32[144,128]{1,0:T(8,128)S(1)}, f32[144,128]{1,0:T(8,128)S(1)}, u32[]{:S(2)}, u32[]{:S(2)}) %collective-permute-start.5) | collective-permute-done | bytes 73760 | tf_op jit(solution)/shard_map/ppermute | solution.py:487
  19.5 0.0 collective-permute-done.7.w0
  19.5 0.0 collective-permute-done.8.w1
  19.5 2.1 %last_halo_kernel.1 = (f32[17,96,128]{2,1,0:T(8,128)}, f32[17,96,128]{2,1,0:T(8,128)}) custom-call(f32[1632,128]{1,0:T(8,128)S(1)} %later_local_kernel.1.partial, f32[1632,128]{1,0:T(8,128)S(1)} %get-tuple-element.49.adj, f32[96,128]{1,0:T(8,128)S(1)} %get-tuple-element.50.rs.rs_full, f32[208,128]{1,0:T(8,128)S(1)} %get-tuple-element.52.rates, ...), custom_call_target="tpu_custom_call" | custom-call | flops 100000000 | bytes 3098112 | tf_op jit(solution)/shard_map/last_halo_kernel/pallas_call | solution.py:509
  (6 shorter events, 0.0 us)
Async XLA Ops:
  0.6 7.5 %copy-start = (f32[17,12,8,128]{3,2,1,0:T(8,128)S(1)}, f32[17,12,8,128]{3,2,1,0:T(8,128)}, u32[]{:S(2)}) copy-start(f32[17,12,8,128]{3,2,1,0:T(8,128)} %param.11) | copy-start | bytes 2506756
  0.6 7.5 %copy-start.1 = (f32[3,2,17,17]{3,1,2,0:T(2,128)S(1)}, f32[3,2,17,17]{3,1,2,0:T(2,128)}, u32[]{:S(2)}) copy-start(f32[3,2,17,17]{3,1,2,0:T(2,128)} %param.14) | copy-start | bytes 20812
  2.4 8.1 %collective-permute-start.2 = (f32[224,128]{1,0:T(8,128)S(1)}, f32[224,128]{1,0:T(8,128)S(1)}, u32[]{:S(2)}, u32[]{:S(2)}) collective-permute-start(f32[224,128]{1,0:T(8,128)S(1)} %get-tuple-element.43), channel_id=1, source_target_pairs={{0,1},{1,0},{2,3},{3,2},{4,5},{5,4},{6,7},{7,6},{8,9},{9,8},{10,11... | collective-permute-start | bytes 344072 | tf_op jit(solution)/shard_map/ppermute | solution.py:487
  2.9 7.6 %collective-permute-start.3 = (f32[224,128]{1,0:T(8,128)S(1)}, f32[224,128]{1,0:T(8,128)S(1)}, u32[]{:S(2)}, u32[]{:S(2)}) collective-permute-start(f32[224,128]{1,0:T(8,128)S(1)} %get-tuple-element.44), channel_id=1, source_target_pairs={{0,4},{1,2},{2,1},{3,7},{4,0},{5,6},{6,5},{7,3},{8,12},{9,10},{10,... | collective-permute-start | bytes 344072 | tf_op jit(solution)/shard_map/ppermute | solution.py:487
  5.5 5.0 %collective-permute-start.4 = (f32[32,128]{1,0:T(8,128)S(1)}, f32[32,128]{1,0:T(8,128)S(1)}, u32[]{:S(2)}, u32[]{:S(2)}) collective-permute-start(f32[32,128]{1,0:T(8,128)S(1)} %get-tuple-element.45), channel_id=1, source_target_pairs={{0,4},{4,0},{1,5},{5,1},{2,6},{6,2},{3,7},{7,3},{8,12},{12,8},{9,1... | collective-permute-start | bytes 49160 | tf_op jit(solution)/shard_map/ppermute | solution.py:496
  5.6 4.9 %collective-permute-start = (f32[144,128]{1,0:T(8,128)S(1)}, f32[144,128]{1,0:T(8,128)S(1)}, u32[]{:S(2)}, u32[]{:S(2)}) collective-permute-start(f32[144,128]{1,0:T(8,128)S(1)} %get-tuple-element.41), channel_id=1, source_target_pairs={{0,8},{1,9},{2,10},{3,11},{4,12},{5,13},{6,14},{7,15},{8,0},{9,1},... | collective-permute-start | bytes 221192 | tf_op jit(solution)/shard_map/ppermute | solution.py:487
  7.6 2.9 %collective-permute-start.1 = (f32[144,128]{1,0:T(8,128)S(1)}, f32[144,128]{1,0:T(8,128)S(1)}, u32[]{:S(2)}, u32[]{:S(2)}) collective-permute-start(f32[144,128]{1,0:T(8,128)S(1)} %get-tuple-element.42), channel_id=1, source_target_pairs={{0,1},{1,0},{2,3},{3,2},{4,5},{5,4},{6,7},{7,6},{8,16},{9,17},{10,... | collective-permute-start | bytes 221192 | tf_op jit(solution)/shard_map/ppermute | solution.py:487
  11.7 7.7 %collective-permute-start.7 = (f32[224,128]{1,0:T(8,128)S(1)}, f32[224,128]{1,0:T(8,128)S(1)}, u32[]{:S(2)}, u32[]{:S(2)}) collective-permute-start(f32[224,128]{1,0:T(8,128)S(1)} %get-tuple-element.55), channel_id=1, source_target_pairs={{0,1},{1,0},{2,3},{3,2},{4,5},{5,4},{6,7},{7,6},{8,9},{9,8},{10,11... | collective-permute-start | bytes 344072 | tf_op jit(solution)/shard_map/ppermute | solution.py:487
  11.8 7.6 %collective-permute-start.8 = (f32[224,128]{1,0:T(8,128)S(1)}, f32[224,128]{1,0:T(8,128)S(1)}, u32[]{:S(2)}, u32[]{:S(2)}) collective-permute-start(f32[224,128]{1,0:T(8,128)S(1)} %get-tuple-element.56), channel_id=1, source_target_pairs={{0,4},{1,2},{2,1},{3,7},{4,0},{5,6},{6,5},{7,3},{8,12},{9,10},{10,... | collective-permute-start | bytes 344072 | tf_op jit(solution)/shard_map/ppermute | solution.py:487
  13.3 5.7 %collective-permute-start.9 = (f32[32,128]{1,0:T(8,128)S(1)}, f32[32,128]{1,0:T(8,128)S(1)}, u32[]{:S(2)}, u32[]{:S(2)}) collective-permute-start(f32[32,128]{1,0:T(8,128)S(1)} %get-tuple-element.57), channel_id=1, source_target_pairs={{0,4},{4,0},{1,5},{5,1},{2,6},{6,2},{3,7},{7,3},{8,12},{12,8},{9,1... | collective-permute-start | bytes 49160 | tf_op jit(solution)/shard_map/ppermute | solution.py:496
  13.9 5.6 %collective-permute-start.5 = (f32[144,128]{1,0:T(8,128)S(1)}, f32[144,128]{1,0:T(8,128)S(1)}, u32[]{:S(2)}, u32[]{:S(2)}) collective-permute-start(f32[144,128]{1,0:T(8,128)S(1)} %get-tuple-element.53), channel_id=1, source_target_pairs={{0,8},{1,9},{2,10},{3,11},{4,12},{5,13},{6,14},{7,15},{8,0},{9,1},... | collective-permute-start | bytes 221192 | tf_op jit(solution)/shard_map/ppermute | solution.py:487
  17.1 2.3 %collective-permute-start.6 = (f32[144,128]{1,0:T(8,128)S(1)}, f32[144,128]{1,0:T(8,128)S(1)}, u32[]{:S(2)}, u32[]{:S(2)}) collective-permute-start(f32[144,128]{1,0:T(8,128)S(1)} %get-tuple-element.54), channel_id=1, source_target_pairs={{0,1},{1,0},{2,3},{3,2},{4,5},{5,4},{6,7},{7,6},{8,16},{9,17},{10,... | collective-permute-start | bytes 221192 | tf_op jit(solution)/shard_map/ppermute | solution.py:487

commit v3 on v2

--- a/solution.py
+++ b/solution.py
@@ -11,7 +11,6 @@
 AXES = ("stream", "span", "wall")
 F32 = jnp.float32
 BF16 = jnp.bfloat16
-STORE = 4
 
 
 class Dims:
@@ -23,6 +22,8 @@
         self.B = self.G * self.W
         self.n = self.V * self.W
         self.rows = self.n * self.X
+        self.edges = sorted({0, self.X - 1})
+        self.inner = range(1, self.X - 1)
         self.wall_rows = self.X * self.G + 8
         self.wall_k = -(-self.G // 8) * 8
         self.stack = -(-self.V // 8) * 8
@@ -32,6 +33,9 @@
     def block(self, group, x):
         return pl.ds((group * self.X + x) * self.W, self.W)
 
+    def rows_at(self, x, w):
+        return pl.ds(x * self.W + w, self.V, stride=self.X * self.W)
+
     def plane(self, ref, x):
         return jnp.concatenate([ref[self.block(v, x), :] for v in range(self.V)], axis=0)
 
@@ -78,49 +82,54 @@
     return jnp.dot(a, b, preferred_element_type=F32)
 
 
-def pack_faces(
-    d, block_of, radius_of, rows_of, even_s, even_w, s_a, s_b, w_a, w_b, z_out
-):
+def pack_stream(d, block_of, radius_of, s_a, s_b):
+    W, even = d.W, parity("stream")
+    for g in range(d.G):
+        if g < d.V:
+            first, last = block_of(g, 0), block_of(g, d.X - 1)
+        elif g == d.V and radius_of is not None:
+            first, last = radius_of(0, 0), radius_of(0, d.X - 1)
+        else:
+            first = last = jnp.zeros((W, d.Z), F32)
+        s_a[g * W : (g + 1) * W, :] = jnp.where(even, last, first)
+        s_b[g * W : (g + 1) * W, :] = jnp.where(even, first, last)
+
+
+def pack_span(d, planes, block_of, radius_of, given, z_out):
+    V, X, W, Z = d.V, d.X, d.W, d.Z
+    pair = lanes(d, W) // 2
+    for q in range(d.span_groups):
+        rows = pl.ds(q * W, W)
+        group = jnp.zeros((W, Z), F32) if given is None else given[rows, :]
+        for v in range(q * d.per, min(V + 1, (q + 1) * d.per)):
+            if v == V and radius_of is None:
+                continue
+            for x in planes:
+                value = block_of(v, x) if v < V else radius_of(2, x)
+                spot = X * (v % d.per) + x
+                group = jnp.where(pair == spot, pltpu.roll(value, (2 * spot + 1) % Z, 1), group)
+        z_out[rows, :] = group
+
+
+def pack_walls(d, planes, adj, radius_of, w_a, w_b):
     V, X, W, Z, G = d.V, d.X, d.W, d.Z, d.G
-    zero = jnp.zeros((W, Z), F32)
-    pair = lanes(d, W) // 2
-    groups = [zero] * d.span_groups
-
-    def span_columns(v, x, value):
-        spot = X * (v % d.per) + x
-        moved = pltpu.roll(value, (2 * spot + 1) % Z, 1)
-        groups[v // d.per] = jnp.where(pair == spot, moved, groups[v // d.per])
-
-    for g in range(G):
-        if g < V:
-            first, last = block_of(g, 0), block_of(g, X - 1)
-            for x in range(X):
-                span_columns(g, x, block_of(g, x))
-        elif g == V and radius_of is not None:
-            first, last = radius_of(0, 0), radius_of(0, X - 1)
-            for x in range(X):
-                span_columns(V, x, radius_of(2, x))
-        else:
-            first = last = zero
-        s_a[g * W : (g + 1) * W, :] = jnp.where(even_s, last, first)
-        s_b[g * W : (g + 1) * W, :] = jnp.where(even_s, first, last)
-    for q in range(d.span_groups):
-        z_out[q * W : (q + 1) * W, :] = groups[q]
+    even = parity("wall")
     tail = jnp.zeros((G - V, Z), F32)
-    for x in range(X):
-        first, last = rows_of(x, 0), rows_of(x, W - 1)
-        w_a[x * G : x * G + V, :] = jnp.where(even_w, last, first)
-        w_b[x * G : x * G + V, :] = jnp.where(even_w, first, last)
+    for x in planes:
+        first, last = adj[d.rows_at(x, 0), :], adj[d.rows_at(x, W - 1), :]
+        w_a[x * G : x * G + V, :] = jnp.where(even, last, first)
+        w_b[x * G : x * G + V, :] = jnp.where(even, first, last)
         if radius_of is None or G - V > 1:
             w_a[x * G + V : (x + 1) * G, :] = tail
             w_b[x * G + V : (x + 1) * G, :] = tail
         if radius_of is not None:
             radius = radius_of(1, x)
             first, last = radius[:1], radius[W - 1 :]
-            w_a[x * G + V : x * G + V + 1, :] = jnp.where(even_w, last, first)
-            w_b[x * G + V : x * G + V + 1, :] = jnp.where(even_w, first, last)
-    w_a[X * G :, :] = jnp.zeros((8, Z), F32)
-    w_b[X * G :, :] = jnp.zeros((8, Z), F32)
+            w_a[x * G + V : x * G + V + 1, :] = jnp.where(even, last, first)
+            w_b[x * G + V : x * G + V + 1, :] = jnp.where(even, first, last)
+    if X - 1 in planes:
+        w_a[X * G :, :] = jnp.zeros((8, Z), F32)
+        w_b[X * G :, :] = jnp.zeros((8, Z), F32)
 
 
 def parity(axis):
@@ -137,19 +146,11 @@
         copy.start()
     for copy in copies:
         copy.wait()
-    pack_faces(
-        d,
-        lambda v, x: adj[d.block(v, x), :],
-        functools.partial(radius_at, d, vel, snd),
-        lambda x, w: adj[pl.ds(x * d.W + w, d.V, stride=d.X * d.W), :],
-        parity("stream"),
-        parity("wall"),
-        s_a,
-        s_b,
-        w_a,
-        w_b,
-        z_out,
-    )
+    block_of = lambda v, x: adj[d.block(v, x), :]
+    radius_of = functools.partial(radius_at, d, vel, snd)
+    pack_stream(d, block_of, radius_of, s_a, s_b)
+    pack_span(d, range(d.X), block_of, radius_of, None, z_out)
+    pack_walls(d, range(d.X), adj, radius_of, w_a, w_b)
 
 
 def make_matrices(d, couple, precond, mk, mw, pk, wide, wide_wall):
@@ -172,9 +173,11 @@
         return lax.dot_general(some, part.astype(BF16), dims, preferred_element_type=F32)
 
     wide[...] = spread(blocks, B, lambda col, v: col // W == v)
+    sides = []
     for side in range(2):
         some = blocks[:, (2 + side) * S : (3 + side) * S]
-        wide_wall[side * S : (side + 1) * S, :] = spread(some, 2 * K, lambda col, v: col - side * K == v)
+        sides.append(spread(some, 2 * K, lambda col, v: col - side * K == v))
+    wide_wall[...] = jnp.concatenate(sides, axis=0)
     row = lax.broadcasted_iota(jnp.int32, (W, 3 * B), 0)
     col = lax.rem(lax.broadcasted_iota(jnp.int32, (W, 3 * B), 1), W)
     same, lower, upper = [(col - row == k).astype(F32) for k in (0, -1, 1)]
@@ -260,7 +263,7 @@
         for rate, value in terms:
             result = result - d.each(rate) * value
         d.store_plane(out, x, result)
-        spot = pl.ds(x * W, V, stride=X * W)
+        spot = d.rows_at(x, 0)
         factor = wall_flag * radius[1][x][:1]
         coef = wall_coef[x * d.stack : x * d.stack + V, :]
         out[spot, :] = out[spot, :] - factor * coef * adj[spot, :]
@@ -290,36 +293,38 @@
     sweep_local(d, adj, src, vel, snd, mk, wall_coef, rs, out, None)
 
 
-def halo_terms(d, s0, s1, w0, w1, zl, zr, mk, mw):
-    V, X, W, Z, G, n = d.V, d.X, d.W, d.Z, d.G, d.n
-    even_s, even_w = parity("stream"), parity("wall")
-    si, wi = lax.axis_index("stream"), lax.axis_index("wall")
-    has = lambda flag: flag.astype(F32)
-    s_low, s_high = has(si > 0), has(si < lax.axis_size("stream") - 1)
-    w_low, w_high = has(wi > 0), has(wi < lax.axis_size("wall") - 1)
-    low = jnp.where(even_s, s1[...], s0[...]) * s_low
-    high = jnp.where(even_s, s0[...], s1[...]) * s_high
-    both = dot(mk[: 2 * n], split3(jnp.concatenate([low, high], axis=1)))
-    stream = both[:n, :Z], both[n:, Z:]
-    stream_radius = (low[n : n + W], high[n : n + W])
-
-    def wall_rows(x):
-        rows = pl.ds(x * G, d.wall_k)
-        a, b = w0[rows, :], w1[rows, :]
-        return jnp.where(even_w, b, a) * w_low, jnp.where(even_w, a, b) * w_high
-
-    def wall(x):
-        return jnp.concatenate(wall_rows(x), axis=0)
-
+def neighbours(axis):
+    index = lax.axis_index(axis)
+    return (index > 0).astype(F32), (index < lax.axis_size(axis) - 1).astype(F32)
+
+
+def wall_terms(d, w0, w1, mw):
+    X, W, Z, G = d.X, d.W, d.Z, d.G
+    even = parity("wall")
+    has_low, has_high = neighbours("wall")
     row = row_ids(d)
 
-    def wall_radius(x):
-        rows = pl.ds(x * G + V, 1)
-        a, b = w0[rows, :], w1[rows, :]
-        first = jnp.where(even_w, b, a) * w_low
-        last = jnp.where(even_w, a, b) * w_high
+    def received(start, count):
+        a, b = w0[pl.ds(start, count), :], w1[pl.ds(start, count), :]
+        return jnp.where(even, b, a) * has_low, jnp.where(even, a, b) * has_high
+
+    products = {}
+    for start in range(0, X, 2):
+        here = list(range(start, min(X, start + 2)))
+        right = [jnp.concatenate(received(x * G, d.wall_k), axis=0) for x in here]
+        value = dot(mw[...], split3(jnp.concatenate(right, axis=1)))
+        for k, x in enumerate(here):
+            products[x] = value[:, k * Z : (k + 1) * Z]
+
+    def radius(x):
+        first, last = received(x * G + d.V, 1)
         return jnp.where(row == 0, first, jnp.where(row == W - 1, last, 0.0))
 
+    return products.get, radius
+
+
+def span_terms(d, zl, zr, mk):
+    V, X, W, Z, n = d.V, d.X, d.W, d.Z, d.n
     even = lax.rem(lanes(d, W), 2) == 0
     pieces = []
     for v in range(V + 1):
@@ -327,142 +332,173 @@
         value = jnp.where(even, zl[q, :], zr[q, :])
         turn = (Z - 2 * X * (v % d.per)) % Z
         pieces.append(pltpu.roll(value, turn, 1) if turn else value)
-    span_radius = jnp.where(even, pieces[V], pltpu.roll(pieces[V], Z - 2, 1))
-    pieces += [jnp.zeros((W, Z), F32)] * (G - V - 1)
+    radius = jnp.where(even, pieces[V], pltpu.roll(pieces[V], Z - 2, 1))
+    pieces += [jnp.zeros((W, Z), F32)] * (d.G - V - 1)
     both = dot(mk[4 * n :], split3(jnp.concatenate(pieces, axis=0)))
     even = lax.rem(lanes(d, n), 2) == 0
     span = jnp.where(even, both[:n], pltpu.roll(both[n:], Z - 2, 1))
     at = lambda value, x: pltpu.roll(value, (Z - 2 * x) % Z, 1) if x else value
-    return (
-        stream,
-        stream_radius,
-        wall,
-        wall_radius,
-        lambda x: at(span, x),
-        lambda x: at(span_radius, x),
-    )
-
-
-def finish_sweep(d, partial, adj, rs_of, halo_rates, corrections, halo, mw, pk, put):
-    X, Z = d.X, d.Z
-    stream, _, wall, _, span, _ = halo
-    walls = {}
-    for start in range(0, X, 2):
-        here = list(range(start, min(X, start + 2)))
-        value = dot(mw[...], split3(jnp.concatenate([wall(x) for x in here], axis=1)))
-        for k, x in enumerate(here):
-            walls[x] = value[:, k * Z : (k + 1) * Z]
-
-    def residual(x):
-        low, high, rate_wall, rate_span = halo_rates(x)
-        res = d.plane(partial, x)
-        if corrections is not None:
-            res = res - d.each(corrections(x)) * d.plane(adj, x)
-        res = res - d.each(rate_wall) * walls[x]
-        res = res - d.each(rate_span) * span(x)
-        if low is not None:
-            res = res - d.each(low) * stream[0]
-        if high is not None:
-            res = res - d.each(high) * stream[1]
-        return res
-
-    def updated(here, residuals, update):
+    return lambda x: at(span, x), lambda x: at(radius, x)
+
+
+def update_planes(d, planes, residual_of, adj, rs_of, pk, put):
+    Z = d.Z
+
+    def finish(here, residuals, update):
         for k, x in enumerate(here):
             inverse = 1.0 / rs_of(x)
             new = d.plane(adj, x) + update[:, k * Z : (k + 1) * Z] * d.each(inverse)
             put(x, new, residuals[k])
 
     waiting = None
-    for start in range(0, X, 2):
-        here = list(range(start, min(X, start + 2)))
-        residuals = [residual(x) for x in here]
+    for start in range(0, len(planes), 2):
+        here = planes[start : start + 2]
+        residuals = [residual_of(x) for x in here]
         right = jnp.concatenate([padded_plane(d, r) for r in residuals], axis=1)
         update = dot(pk[...], split3(right))
         if waiting:
-            updated(*waiting)
+            finish(*waiting)
         waiting = here, residuals, update
-    updated(*waiting)
-
-
-def first_halo_kernel(
-    d, partial, adj, rs, vel, snd, s0, s1, w0, w1, zl, zr, mk, mw, pk,
-    new_adj, rs_full, rates, s_a, s_b, w_a, w_b, z_out,
+    if waiting:
+        finish(*waiting)
+
+
+def first_inner_kernel(
+    d, partial, adj, rs, vel, snd, w0, w1, zl, zr, mk, mw, pk,
+    new_adj, rs_full, rates, edge, w_a, w_b, z_out,
 ):
-    X, W, Z = d.X, d.W, d.Z
-    halo = halo_terms(d, s0, s1, w0, w1, zl, zr, mk, mw)
-    _, stream_radius, _, wall_radius, _, span_radius = halo
+    V, X, W, Z, n = d.V, d.X, d.W, d.Z, d.n
+    span, span_radius = span_terms(d, zl, zr, mk)
+    wall, wall_radius = wall_terms(d, w0, w1, mw)
     lane, row = lanes(d, W), row_ids(d)
     edge_lane = (lane == 0) | (lane == Z - 1)
     edge_row = (row == 0) | (row == W - 1)
-    kept = {}
-    for x in range(X):
+    totals = {}
+
+    def residual_of(x):
         from_wall = 0.5 * wall_radius(x)
         from_span = jnp.where(edge_lane, 0.5 * span_radius(x), 0.0)
         rate_wall = jnp.where(edge_row, 0.5 * radius_at(d, vel, snd, 1, x) + from_wall, 0.0)
         rate_span = jnp.where(edge_lane, 0.5 * radius_at(d, vel, snd, 2, x) + from_span, 0.0)
         correction = from_wall + from_span
-        low = high = None
-        if x == 0:
-            correction = correction + 0.5 * stream_radius[0]
-            low = 0.5 * (radius_at(d, vel, snd, 0, x) + stream_radius[0])
-            rates[d.block(2, 0), :] = low
-        if x == X - 1:
-            correction = correction + 0.5 * stream_radius[1]
-            high = 0.5 * (radius_at(d, vel, snd, 0, x) + stream_radius[1])
-            rates[d.block(2, 1 % X) if X > 1 else pl.ds((2 * X + 1) * W, W), :] = high
+        totals[x] = rs[d.block(0, x), :] + correction
         rates[d.block(0, x), :] = rate_wall
         rates[d.block(1, x), :] = rate_span
-        total = rs[d.block(0, x), :] + correction
-        rs_full[d.block(0, x), :] = total
-        kept[x] = (correction, total, (low, high, rate_wall, rate_span))
+        rs_full[d.block(0, x), :] = totals[x]
+        result = d.plane(partial, x) - d.each(correction) * d.plane(adj, x)
+        return result - d.each(rate_wall) * wall(x) - d.each(rate_span) * span(x)
+
+    for k, x in enumerate(d.edges):
+        edge[k * n : (k + 1) * n, :] = residual_of(x)
+    put = lambda x, new, _: d.store_plane(new_adj, x, new)
+    update_planes(d, list(d.inner), residual_of, adj, totals.get, pk, put)
+    pack_walls(d, d.inner, new_adj, None, w_a, w_b)
+    pack_span(d, d.inner, lambda v, x: new_adj[d.block(v, x), :], None, None, z_out)
+
+
+def later_inner_kernel(
+    d, partial, adj, rs_full, rates, w0, w1, zl, zr, mk, mw, pk, new_adj, residual, edge
+):
+    W, n = d.W, d.n
+    span, _ = span_terms(d, zl, zr, mk)
+    wall, _ = wall_terms(d, w0, w1, mw)
+
+    def residual_of(x):
+        result = d.plane(partial, x) - d.each(rates[d.block(0, x), :]) * wall(x)
+        return result - d.each(rates[d.block(1, x), :]) * span(x)
+
+    def put(x, new, res):
+        new_adj[d.planes_at(x, 1)] = new.reshape(d.V, W, d.Z)
+        residual[d.planes_at(x, 1)] = res.reshape(d.V, W, d.Z)
+
+    for k, x in enumerate(d.edges):
+        edge[k * n : (k + 1) * n, :] = residual_of(x)
+    rs_of = lambda x: rs_full[d.block(0, x), :]
+    update_planes(d, list(d.inner), residual_of, adj, rs_of, pk, put)
+
+
+def stream_terms(d, s0, s1, mk):
+    n, Z = d.n, d.Z
+    even = parity("stream")
+    has_low, has_high = neighbours("stream")
+    low = jnp.where(even, s1[...], s0[...]) * has_low
+    high = jnp.where(even, s0[...], s1[...]) * has_high
+    both = dot(mk[: 2 * n], split3(jnp.concatenate([low, high], axis=1)))
+    return (both[:n, :Z], both[n:, Z:]), (low[n : n + d.W], high[n : n + d.W])
+
+
+def first_stream_kernel(
+    d, edge, adj, rs, vel, snd, s0, s1, mk, pk, inner, w_in0, w_in1, z_in,
+    new_adj, rs_full, w_a, w_b, z_out, rates, s_a, s_b,
+):
+    X, W, n = d.X, d.W, d.n
+    products, received = stream_terms(d, s0, s1, mk)
+    totals = {}
+
+    def residual_of(x):
+        k = d.edges.index(x)
+        result = edge[k * n : (k + 1) * n, :]
+        totals[x] = rs[d.block(0, x), :]
+        for side, at in enumerate((0, X - 1)):
+            if x == at:
+                rate = 0.5 * (radius_at(d, vel, snd, 0, x) + received[side])
+                rates[side * W : (side + 1) * W, :] = rate
+                totals[x] = totals[x] + 0.5 * received[side]
+                result = result - d.each(0.5 * received[side]) * d.plane(adj, x)
+                result = result - d.each(rate) * products[side]
+        rs_full[d.block(0, x), :] = totals[x]
+        return result
+
+    planes = {}
 
     def put(x, new, _):
         d.store_plane(new_adj, x, new)
-
-    finish_sweep(
-        d, partial, adj, lambda x: kept[x][1], lambda x: kept[x][2], lambda x: kept[x][0],
-        halo, mw, pk, put,
-    )
-    pack_faces(
-        d,
-        lambda v, x: new_adj[d.block(v, x), :],
-        None,
-        lambda x, w: new_adj[pl.ds(x * W + w, d.V, stride=X * W), :],
-        parity("stream"),
-        parity("wall"),
-        s_a, s_b, w_a, w_b, z_out,
-    )
-
-
-def last_halo_kernel(
-    d, partial, adj, rs_full, rates, s0, s1, w0, w1, zl, zr, mk, mw, pk,
-    new_adj, residual, new_adj_here, residual_here, sems,
+        planes[x] = new
+
+    update_planes(d, d.edges, residual_of, adj, totals.get, pk, put)
+    block_of = lambda v, x: planes[x][v * W : (v + 1) * W]
+    pack_stream(d, block_of, None, s_a, s_b)
+    pack_span(d, d.edges, block_of, None, z_in, z_out)
+    pack_walls(d, d.edges, new_adj, None, w_a, w_b)
+
+
+def later_stream_kernel(
+    d, edge, adj, rs_full, rates, s0, s1, mk, pk, inner_adj, inner_residual,
+    new_adj, residual, edge_adj, edge_residual, sems,
 ):
-    X, W, Z = d.X, d.W, d.Z
-    halo = halo_terms(d, s0, s1, w0, w1, zl, zr, mk, mw)
-
-    def halo_rates(x):
-        low = rates[pl.ds(2 * X * W, W), :] if x == 0 else None
-        high = rates[pl.ds((2 * X + 1) * W, W), :] if x == X - 1 else None
-        return low, high, rates[d.block(0, x), :], rates[d.block(1, x), :]
-
+    X, W, Z, n = d.X, d.W, d.Z, d.n
     copies = []
 
+    def store(source, target, part, here):
+        copy = pltpu.make_async_copy(source.at[here], target.at[part], sems.at[len(copies)])
+        copy.start()
+        copies.append(copy)
+
+    if len(d.inner):
+        part = d.planes_at(1, len(d.inner))
+        store(inner_residual, residual, part, part)
+        store(inner_adj, new_adj, part, part)
+    products, _ = stream_terms(d, s0, s1, mk)
+
+    def residual_of(x):
+        k = d.edges.index(x)
+        result = edge[k * n : (k + 1) * n, :]
+        for side, at in enumerate((0, X - 1)):
+            if x == at:
+                result = result - d.each(rates[side * W : (side + 1) * W, :]) * products[side]
+        return result
+
     def put(x, new, res):
-        here = d.planes_at(x, 1)
-        new_adj_here[here] = new.reshape(d.V, W, Z)
-        residual_here[here] = res.reshape(d.V, W, Z)
-        if (x + 1) % STORE == 0 or x == X - 1:
-            start = x - x % STORE
-            part = d.planes_at(start, x + 1 - start)
-            for k, (a, b) in enumerate(((new_adj_here, new_adj), (residual_here, residual))):
-                copy = pltpu.make_async_copy(a.at[part], b.at[part], sems.at[k, start // STORE])
-                copy.start()
-                copies.append(copy)
-
-    finish_sweep(
-        d, partial, adj, lambda x: rs_full[d.block(0, x), :], halo_rates, None, halo, mw, pk, put
-    )
+        here = d.planes_at(d.edges.index(x), 1)
+        for value, held, target in (
+            (res, edge_residual, residual),
+            (new, edge_adj, new_adj),
+        ):
+            held[here] = value.reshape(d.V, W, Z)
+            store(held, target, d.planes_at(x, 1), here)
+
+    rs_of = lambda x: rs_full[d.block(0, x), :]
+    update_planes(d, d.edges, residual_of, adj, rs_of, pk, put)
     for copy in copies:
         copy.wait()
 
@@ -501,7 +537,7 @@
     return s0, s1, w0, w1, zl, zr
 
 
-def call(kernel, d, outs, flops, args, held=(), scratch=(), out_held=False):
+def call(kernel, d, outs, flops, args, held=(), scratch=(), out_held=False, aliases=None):
     space = lambda k: pltpu.HBM if k in held else pltpu.VMEM
     out_space = pltpu.HBM if out_held else pltpu.VMEM
     args = [pltpu.with_memory_space_constraint(a, space(k)) for k, a in enumerate(args)]
@@ -512,6 +548,7 @@
         in_specs=[pl.BlockSpec(memory_space=space(k)) for k in range(len(args))],
         out_specs=tuple(pl.BlockSpec(memory_space=out_space) for _ in outs),
         scratch_shapes=scratch,
+        input_output_aliases=aliases or {},
         compiler_params=pltpu.CompilerParams(vmem_limit_bytes=24 * 2**20),
         cost_estimate=pl.CostEstimate(flops=flops, bytes_accessed=moved, transcendentals=0),
         name=kernel.__name__,
@@ -536,7 +573,6 @@
     faces = [((B, Z), F32)] * 2 + [((d.wall_rows, Z), F32)] * 2 + [((d.span_groups * W, Z), F32)]
     field, scalar = ((d.rows, Z), F32), ((X * W, Z), F32)
     planes = ((V, X * W, Z), F32)
-    stores = -(-X // STORE)
     sems = lambda *counts: pltpu.SemaphoreType.DMA(counts)
     *kept, s_a, s_b, w_a, w_b, z = call(
         pack_kernel,
@@ -564,28 +600,46 @@
         [adj, source, velocity, sound, couple] + kept[3:],
         scratch=[pltpu.VMEM((7 * d.stack, 3 * B), F32), pltpu.VMEM((2 * d.stack, 6 * d.wall_k), F32)],
     )
-    adj1, rs_full, rates, *packets = call(
-        first_halo_kernel,
+    s0, s1, w0, w1, zl, zr = got
+    edge = ((len(d.edges) * n, Z), F32)
+    inner, rs, rates, held, w_a, w_b, z = call(
+        first_inner_kernel,
         d,
-        [field, scalar, ((2 * (X + 1) * W, Z), F32)] + faces,
+        [field, scalar, ((2 * X * W, Z), F32), edge] + faces[2:],
         10**8,
-        [partial, adj, rs, velocity, sound, *got, mk, mw, pk],
-    )
-    got = swap_lines(sizes, *packets)
+        [partial, adj, rs, velocity, sound, w0, w1, zl, zr, mk, mw, pk],
+    )
+    adj1, rs, w_a, w_b, z, stream_rates, s_a, s_b = call(
+        first_stream_kernel,
+        d,
+        [field, scalar] + faces[2:] + [((2 * W, Z), F32)] + faces[:2],
+        10**7,
+        [held, adj, rs, velocity, sound, s0, s1, mk, pk, inner, w_a, w_b, z],
+        aliases={9: 0, 2: 1, 10: 2, 11: 3, 12: 4},
+    )
+    s0, s1, w0, w1, zl, zr = swap_lines(sizes, s_a, s_b, w_a, w_b, z)
     (partial,) = call(
         later_local_kernel,
         d,
         [field],
         10**9,
-        [adj1, source, velocity, sound, rs_full, mk, wall_coef],
-    )
+        [adj1, source, velocity, sound, rs, mk, wall_coef],
+    )
+    inner, inner_residual, held = call(
+        later_inner_kernel,
+        d,
+        [planes, planes, edge],
+        10**8,
+        [partial, adj1, rs, rates, w0, w1, zl, zr, mk, mw, pk],
+    )
+    edge = ((V, len(d.edges) * W, Z), F32)
     adj2, residual = call(
-        last_halo_kernel,
+        later_stream_kernel,
         d,
         [planes, planes],
-        10**8,
-        [partial, adj1, rs_full, rates, *got, mk, mw, pk],
-        scratch=[pltpu.VMEM(*planes), pltpu.VMEM(*planes), sems(2, stores)],
+        10**7,
+        [held, adj1, rs, stream_rates, s0, s1, mk, pk, inner, inner_residual],
+        scratch=[pltpu.VMEM(*edge), pltpu.VMEM(*edge), sems(2 + 2 * len(d.edges))],
         out_held=True,
     )
     return adj2.reshape(shape), residual.reshape(shape)

time: 21.7 us -> 21.5 us (level)
  Pallas kernels: 9.19 us -> 9.78 us
  waiting for transfers between devices: 0.49 us -> 0.03 us
  starting transfers between devices: 11.1 us -> 10.7 us
    pallas_call x5 -> x7, Pallas kernels: 9.19 us -> 9.78 us  [call(): pl.pallas_call(functools.partial(kernel, d), out_shape=tuple((out_space(s...]
    ppermute x8, waiting for transfers between devices: 0.49 us -> 0.02 us  [swap_lines(): move = lambda value, pairs: lax.ppermute(value, AXES, pairs)]
    ppermute x8, starting transfers between devices: 10.4 us -> 9.97 us  [swap_lines(): move = lambda value, pairs: lax.ppermute(value, AXES, pairs)]
  transfers between devices with their start and end apart: 10 -> 10, of which waited for: 1 -> 0; matrix products, arithmetic and copies ran while one was open for 0% -> 0% of each run, Pallas kernels for 19% -> 29%
where the time goes in v3:
time: 21.5 us; the launch traced here: 21.3 us
  starting transfers between devices  10.7 us (50%)
  Pallas kernels  9.78 us (45%)
  between operations  0.8 us (4%)
    ppermute x8, starting transfers between devices, swap_lines(): move = lambda value, pairs: lax.ppermute(value, AXES, pairs)  9.97 us
    pallas_call x7, Pallas kernels, call(): pl.pallas_call(functools.partial(kernel, d), out_shape=tuple((out_space(s...  9.78 us
    ppermute x2, starting transfers between devices, swap_lines(): zl = zr = lax.ppermute(z, 'span', [(0, 1), (1, 0)])  0.72 us
  transfers between devices with their start and end apart: 10, of which 0 were waited for; matrix products, arithmetic and copies ran while one was open for 0% of the time, Pallas kernels for 29%

profile of v3, /device:TPU:0, one launch (start us, length us, event | category | flops | bytes accessed | tf_op | source)
XLA Modules:
  0.0 21.3 jit_solution(8353913966878527712)
XLA Ops:
  0.7 1.8 %pack_kernel.1 = (f32[1632,128]{1,0:T(8,128)S(1)}, f32[288,128]{1,0:T(8,128)S(1)}, f32[96,128]{1,0:T(8,128)S(1)}, f32[17,17]{1,0:T(8,128)S(1)}, s32[48,256]{1,0:...) custom-call(f32[1632,128]{1,0:T(8,128)} %bitcast.9, ...), custom_call_target="tpu_custom_call" | custom-call | bytes 1131992 | tf_op jit(solution)/shard_map/pack_kernel/pallas_call | solution.py:545
  2.4 0.5 %collective-permute-start = (f32[224,128]{1,0:T(8,128)S(1)}, f32[224,128]{1,0:T(8,128)S(1)}, u32[]{:S(2)}, u32[]{:S(2)}) collective-permute-start(f32[224,128]{1,0:T(8,128)S(1)} %get-tuple-element.51), channel_id=1, source_target_pairs={{0,1},{1,0},{2,3},{3,2},{4,5},{5,4},{6,7},{7,6},{8,9},{9,8},{10,11... | collective-permute-start | bytes 344072 | tf_op jit(solution)/shard_map/ppermute | solution.py:523
  3.0 2.6 %collective-permute-start.1 = (f32[224,128]{1,0:T(8,128)S(1)}, f32[224,128]{1,0:T(8,128)S(1)}, u32[]{:S(2)}, u32[]{:S(2)}) collective-permute-start(f32[224,128]{1,0:T(8,128)S(1)} %get-tuple-element.52), channel_id=1, source_target_pairs={{0,4},{1,2},{2,1},{3,7},{4,0},{5,6},{6,5},{7,3},{8,12},{9,10},{10,... | collective-permute-start | bytes 344072 | tf_op jit(solution)/shard_map/ppermute | solution.py:523
  5.5 0.1 collective-permute-start.2
  5.6 2.0 %collective-permute-start.3 = (f32[144,128]{1,0:T(8,128)S(1)}, f32[144,128]{1,0:T(8,128)S(1)}, u32[]{:S(2)}, u32[]{:S(2)}) collective-permute-start(f32[144,128]{1,0:T(8,128)S(1)} %get-tuple-element.59), channel_id=1, source_target_pairs={{0,8},{1,9},{2,10},{3,11},{4,12},{5,13},{6,14},{7,15},{8,0},{9,1},... | collective-permute-start | bytes 221192 | tf_op jit(solution)/shard_map/ppermute | solution.py:523
  7.6 0.5 %collective-permute-start.4 = (f32[144,128]{1,0:T(8,128)S(1)}, f32[144,128]{1,0:T(8,128)S(1)}, u32[]{:S(2)}, u32[]{:S(2)}) collective-permute-start(f32[144,128]{1,0:T(8,128)S(1)} %get-tuple-element.60), channel_id=1, source_target_pairs={{0,1},{1,0},{2,3},{3,2},{4,5},{5,4},{6,7},{7,6},{8,16},{9,17},{10,... | collective-permute-start | bytes 221192 | tf_op jit(solution)/shard_map/ppermute | solution.py:523
  8.2 2.3 %first_local_kernel.1 = (f32[1632,128]{1,0:T(8,128)S(1)}, f32[96,128]{1,0:T(8,128)S(1)}, bf16[816,432]{1,0:T(8,128)(2,1)S(1)}, bf16[136,144]{1,0:T(8,128)(2,1)S(...) custom-call(f32[1632,128]{1,0:T(8,128)S(1)} %get-tuple-element.41.adj, f32[17,96,128]{2,1,0:T(8,128)S(1)} %bitcast.7, ...), custom_call_target="tpu_custom_call" | custom-call | flops 1000000000 | bytes 1974512 | tf_op jit(solution)/shard_map/first_local_kernel/pallas_call | solution.py:545
  10.5 0.0 collective-permute-done.2.zl.zr
  10.5 0.0 collective-permute-done.w0
  10.5 0.0 collective-permute-done.1.w1
  10.5 1.1 %first_inner_kernel.1 = (f32[1632,128]{1,0:T(8,128)S(1)}, f32[96,128]{1,0:T(8,128)S(1)}, f32[192,128]{1,0:T(8,128)S(1)}, f32[272,128]{1,0:T(8,128)S(1)}, f32[224...) custom-call(f32[1632,128]{1,0:T(8,128)S(1)} %get-tuple-element.49.partial, ...), custom_call_target="tpu_custom_call" | custom-call | flops 100000000 | bytes 3040768 | tf_op jit(solution)/shard_map/first_inner_kernel/pallas_call | solution.py:545
  11.7 0.0 collective-permute-done.3.s0
  11.7 0.0 collective-permute-done.4.s1
  11.7 0.6 %first_stream_kernel.1 = (f32[1632,128]{1,0:T(8,128)S(1)}, f32[96,128]{1,0:T(8,128)S(1)}, f32[224,128]{1,0:T(8,128)S(1)}, f32[224,128]{1,0:T(8,128)S(1)}, f32[32...) custom-call(f32[272,128]{1,0:T(8,128)S(1)} %get-tuple-element.57.edg, ...), custom_call_target="tpu_custom_call", output_to_operand_aliasing={{0}: (9, {}), {1}: (2, {}), {2}: (10, {}), {3}: (11, {}), {... | custom-call | flops 10000000 | bytes 3271936 | tf_op jit(solution)/shard_map/first_stream_kernel/pallas_call | solution.py:545
  12.3 0.1 collective-permute-start.5
  12.4 1.4 %collective-permute-start.6 = (f32[224,128]{1,0:T(8,128)S(1)}, f32[224,128]{1,0:T(8,128)S(1)}, u32[]{:S(2)}, u32[]{:S(2)}) collective-permute-start(f32[224,128]{1,0:T(8,128)S(1)} %get-tuple-element.70), channel_id=1, source_target_pairs={{0,4},{1,2},{2,1},{3,7},{4,0},{5,6},{6,5},{7,3},{8,12},{9,10},{10,... | collective-permute-start | bytes 344072 | tf_op jit(solution)/shard_map/ppermute | solution.py:523
  13.8 0.6 %collective-permute-start.7 = (f32[32,128]{1,0:T(8,128)S(1)}, f32[32,128]{1,0:T(8,128)S(1)}, u32[]{:S(2)}, u32[]{:S(2)}) collective-permute-start(f32[32,128]{1,0:T(8,128)S(1)} %get-tuple-element.71), channel_id=1, source_target_pairs={{0,4},{4,0},{1,5},{5,1},{2,6},{6,2},{3,7},{7,3},{8,12},{12,8},{9,1... | collective-permute-start | bytes 49160 | tf_op jit(solution)/shard_map/ppermute | solution.py:532
  14.4 2.8 %collective-permute-start.8 = (f32[144,128]{1,0:T(8,128)S(1)}, f32[144,128]{1,0:T(8,128)S(1)}, u32[]{:S(2)}, u32[]{:S(2)}) collective-permute-start(f32[144,128]{1,0:T(8,128)S(1)} %get-tuple-element.74), channel_id=1, source_target_pairs={{0,8},{1,9},{2,10},{3,11},{4,12},{5,13},{6,14},{7,15},{8,0},{9,1},... | collective-permute-start | bytes 221192 | tf_op jit(solution)/shard_map/ppermute | solution.py:523
  17.2 0.0 collective-permute-start.9
  17.2 1.8 %later_local_kernel.1.partial = f32[1632,128]{1,0:T(8,128)S(1)} custom-call(f32[1632,128]{1,0:T(8,128)S(1)} %get-tuple-element.65.adj, f32[17,96,128]{2,1,0:T(8,128)S(1)} %bitcast.8, f32[288,128]{1,0:T(8,128)S(1)} %get-tuple-element.42.vel, f32[96,128]{1,0:T(8,128)S(1)} %get-tuple-element.43.snd, f32[96,128]{1,0:T(8,128)S(1)} %get-tuple-element.66.rs.rs_full, ...), custom_call_target="tpu_custom_call" | custom-call | flops 1000000000 | bytes 2769408 | tf_op jit(solution)/shard_map/later_local_kernel/pallas_call | solution.py:545
  19.1 0.0 collective-permute-done.5.w0
  19.1 0.0 collective-permute-done.6.w1
  19.1 0.9 %later_inner_kernel.1 = (f32[17,96,128]{2,1,0:T(8,128)S(1)}, f32[17,96,128]{2,1,0:T(8,128)S(1)}, f32[272,128]{1,0:T(8,128)S(1)}) custom-call(f32[1632,128]{1,0:T(8,128)S(1)} %later_local_kernel.1.partial, f32[1632,128]{1,0:T(8,128)S(1)} %get-tuple-element.65.adj, f32[96,128]{1,0:T(8,128)S(1)} %get-tuple-element.66.rs.rs_full, ...), custom_call_target="tpu_custom_call" | custom-call | flops 100000000 | bytes 2942464 | tf_op jit(solution)/shard_map/later_inner_kernel/pallas_call | solution.py:545
  20.1 1.2 %later_stream_kernel.1 = (f32[17,96,128]{2,1,0:T(8,128)}, f32[17,96,128]{2,1,0:T(8,128)}) custom-call(f32[272,128]{1,0:T(8,128)S(1)} %get-tuple-element.72.edge, f32[1632,128]{1,0:T(8,128)S(1)} %get-tuple-element.65.adj, f32[96,128]{1,0:T(8,128)S(1)} %get-tuple-element.66.rs.rs_full, f32[16,128]{1,0:T(8,128)S(1)} %get-tuple-element.73.rates, ...), custom_call_target="tpu_custom_call" | custom-call | flops 10000000 | bytes 3673344 | tf_op jit(solution)/shard_map/later_stream_kernel/pallas_call | solution.py:545
  (8 shorter events, 0.0 us)
Async XLA Ops:
  0.6 7.6 %copy-start = (f32[17,12,8,128]{3,2,1,0:T(8,128)S(1)}, f32[17,12,8,128]{3,2,1,0:T(8,128)}, u32[]{:S(2)}) copy-start(f32[17,12,8,128]{3,2,1,0:T(8,128)} %param.11) | copy-start | bytes 2506756
  0.6 7.5 %copy-start.1 = (f32[3,2,17,17]{3,1,2,0:T(2,128)S(1)}, f32[3,2,17,17]{3,1,2,0:T(2,128)}, u32[]{:S(2)}) copy-start(f32[3,2,17,17]{3,1,2,0:T(2,128)} %param.14) | copy-start | bytes 20812
  2.4 8.1 %collective-permute-start = (f32[224,128]{1,0:T(8,128)S(1)}, f32[224,128]{1,0:T(8,128)S(1)}, u32[]{:S(2)}, u32[]{:S(2)}) collective-permute-start(f32[224,128]{1,0:T(8,128)S(1)} %get-tuple-element.51), channel_id=1, source_target_pairs={{0,1},{1,0},{2,3},{3,2},{4,5},{5,4},{6,7},{7,6},{8,9},{9,8},{10,11... | collective-permute-start | bytes 344072 | tf_op jit(solution)/shard_map/ppermute | solution.py:523
  3.0 7.6 %collective-permute-start.1 = (f32[224,128]{1,0:T(8,128)S(1)}, f32[224,128]{1,0:T(8,128)S(1)}, u32[]{:S(2)}, u32[]{:S(2)}) collective-permute-start(f32[224,128]{1,0:T(8,128)S(1)} %get-tuple-element.52), channel_id=1, source_target_pairs={{0,4},{1,2},{2,1},{3,7},{4,0},{5,6},{6,5},{7,3},{8,12},{9,10},{10,... | collective-permute-start | bytes 344072 | tf_op jit(solution)/shard_map/ppermute | solution.py:523
  5.5 5.0 %collective-permute-start.2 = (f32[32,128]{1,0:T(8,128)S(1)}, f32[32,128]{1,0:T(8,128)S(1)}, u32[]{:S(2)}, u32[]{:S(2)}) collective-permute-start(f32[32,128]{1,0:T(8,128)S(1)} %get-tuple-element.53), channel_id=1, source_target_pairs={{0,4},{4,0},{1,5},{5,1},{2,6},{6,2},{3,7},{7,3},{8,12},{12,8},{9,1... | collective-permute-start | bytes 49160 | tf_op jit(solution)/shard_map/ppermute | solution.py:532
  5.6 6.1 %collective-permute-start.3 = (f32[144,128]{1,0:T(8,128)S(1)}, f32[144,128]{1,0:T(8,128)S(1)}, u32[]{:S(2)}, u32[]{:S(2)}) collective-permute-start(f32[144,128]{1,0:T(8,128)S(1)} %get-tuple-element.59), channel_id=1, source_target_pairs={{0,8},{1,9},{2,10},{3,11},{4,12},{5,13},{6,14},{7,15},{8,0},{9,1},... | collective-permute-start | bytes 221192 | tf_op jit(solution)/shard_map/ppermute | solution.py:523
  7.6 4.0 %collective-permute-start.4 = (f32[144,128]{1,0:T(8,128)S(1)}, f32[144,128]{1,0:T(8,128)S(1)}, u32[]{:S(2)}, u32[]{:S(2)}) collective-permute-start(f32[144,128]{1,0:T(8,128)S(1)} %get-tuple-element.60), channel_id=1, source_target_pairs={{0,1},{1,0},{2,3},{3,2},{4,5},{5,4},{6,7},{7,6},{8,16},{9,17},{10,... | collective-permute-start | bytes 221192 | tf_op jit(solution)/shard_map/ppermute | solution.py:523
  12.3 6.8 %collective-permute-start.5 = (f32[224,128]{1,0:T(8,128)S(1)}, f32[224,128]{1,0:T(8,128)S(1)}, u32[]{:S(2)}, u32[]{:S(2)}) collective-permute-start(f32[224,128]{1,0:T(8,128)S(1)} %get-tuple-element.69), channel_id=1, source_target_pairs={{0,1},{1,0},{2,3},{3,2},{4,5},{5,4},{6,7},{7,6},{8,9},{9,8},{10,11... | collective-permute-start | bytes 344072 | tf_op jit(solution)/shard_map/ppermute | solution.py:523
  12.4 6.8 %collective-permute-start.6 = (f32[224,128]{1,0:T(8,128)S(1)}, f32[224,128]{1,0:T(8,128)S(1)}, u32[]{:S(2)}, u32[]{:S(2)}) collective-permute-start(f32[224,128]{1,0:T(8,128)S(1)} %get-tuple-element.70), channel_id=1, source_target_pairs={{0,4},{1,2},{2,1},{3,7},{4,0},{5,6},{6,5},{7,3},{8,12},{9,10},{10,... | collective-permute-start | bytes 344072 | tf_op jit(solution)/shard_map/ppermute | solution.py:523
  13.8 5.3 %collective-permute-start.7 = (f32[32,128]{1,0:T(8,128)S(1)}, f32[32,128]{1,0:T(8,128)S(1)}, u32[]{:S(2)}, u32[]{:S(2)}) collective-permute-start(f32[32,128]{1,0:T(8,128)S(1)} %get-tuple-element.71), channel_id=1, source_target_pairs={{0,4},{4,0},{1,5},{5,1},{2,6},{6,2},{3,7},{7,3},{8,12},{12,8},{9,1... | collective-permute-start | bytes 49160 | tf_op jit(solution)/shard_map/ppermute | solution.py:532
  14.4 5.6 %collective-permute-start.8 = (f32[144,128]{1,0:T(8,128)S(1)}, f32[144,128]{1,0:T(8,128)S(1)}, u32[]{:S(2)}, u32[]{:S(2)}) collective-permute-start(f32[144,128]{1,0:T(8,128)S(1)} %get-tuple-element.74), channel_id=1, source_target_pairs={{0,8},{1,9},{2,10},{3,11},{4,12},{5,13},{6,14},{7,15},{8,0},{9,1},... | collective-permute-start | bytes 221192 | tf_op jit(solution)/shard_map/ppermute | solution.py:523
  17.2 2.8 %collective-permute-start.9 = (f32[144,128]{1,0:T(8,128)S(1)}, f32[144,128]{1,0:T(8,128)S(1)}, u32[]{:S(2)}, u32[]{:S(2)}) collective-permute-start(f32[144,128]{1,0:T(8,128)S(1)} %get-tuple-element.75), channel_id=1, source_target_pairs={{0,1},{1,0},{2,3},{3,2},{4,5},{5,4},{6,7},{7,6},{8,16},{9,17},{10,... | collective-permute-start | bytes 221192 | tf_op jit(solution)/shard_map/ppermute | solution.py:523

commit v4 on v3

--- a/solution.py
+++ b/solution.py
@@ -156,7 +156,7 @@
 def make_matrices(d, couple, precond, mk, mw, pk, wide, wide_wall):
     V, W, B, n, K, S = d.V, d.W, d.B, d.n, d.wall_k, d.stack
     gap = jnp.zeros((V, S - V), F32)
-    blocks = [couple[k // 2, k % 2] for k in range(6)] + [precond[...].T]
+    blocks = [couple[k // 2, :, k % 2, :] for k in range(6)] + [precond[...].T]
     blocks = [piece for m in blocks for piece in ((m, gap) if S > V else (m,))]
     blocks = jnp.concatenate(blocks, axis=1)
     high = blocks.astype(BF16).astype(F32)
@@ -280,12 +280,29 @@
             done += 1
 
 
+def early():
+    return 2 * lax.axis_index("stream") < lax.axis_size("stream")
+
+
+def early_kernel(d, couple, precond, codes, mask, table, gain, *refs):
+    mk, mw, pk, wall_coef = refs[5:9]
+    wide, wide_wall = refs[-2:]
+
+    @pl.when(early())
+    def _():
+        make_matrices(d, couple, precond, mk, mw, pk, wide, wide_wall)
+        make_wall(d, codes, mask, table, gain, wall_coef)
+
+
 def first_local_kernel(
-    d, adj, src, vel, snd, couple, precond, codes, mask, table, gain,
+    d, adj, src, vel, snd, couple, precond, codes, mask, table, gain, _mk, _mw, _pk, _wall_coef,
     out, rs, mk, mw, pk, wall_coef, wide, wide_wall,
 ):
-    make_matrices(d, couple, precond, mk, mw, pk, wide, wide_wall)
-    make_wall(d, codes, mask, table, gain, wall_coef)
+    @pl.when(jnp.logical_not(early()))
+    def _():
+        make_matrices(d, couple, precond, mk, mw, pk, wide, wide_wall)
+        make_wall(d, codes, mask, table, gain, wall_coef)
+
     sweep_local(d, adj, src, vel, snd, mk, wall_coef, None, out, rs)
 
 
@@ -563,6 +580,7 @@
         adj.reshape(d.rows, Z),
         velocity.reshape(3 * X * W, Z),
         sound.reshape(X * W, Z),
+        couple.transpose(0, 2, 1, 3),
         precond,
         codes,
         mask,
@@ -584,21 +602,32 @@
         scratch=[sems(len(inputs))],
     )
     adj, velocity, sound = kept[:3]
+    made = [
+        ((6 * n, 3 * B), BF16),
+        ((n, 6 * d.wall_k), BF16),
+        ((n, 3 * B), BF16),
+        ((X * d.stack, Z), F32),
+    ]
+    room = [pltpu.VMEM((7 * d.stack, 3 * B), F32), pltpu.VMEM((2 * d.stack, 6 * d.wall_k), F32)]
+    params = kept[3:]
+    *matrices, s_a, s_b, w_a, w_b, z = call(
+        early_kernel,
+        d,
+        made + faces,
+        0,
+        params + [s_a, s_b, w_a, w_b, z],
+        scratch=room,
+        aliases={len(params) + k: len(made) + k for k in range(5)},
+    )
     got = swap_lines(sizes, s_a, s_b, w_a, w_b, z)
     partial, rs, mk, mw, pk, wall_coef = call(
         first_local_kernel,
         d,
-        [
-            field,
-            scalar,
-            ((6 * n, 3 * B), BF16),
-            ((n, 6 * d.wall_k), BF16),
-            ((n, 3 * B), BF16),
-            ((X * d.stack, Z), F32),
-        ],
+        [field, scalar] + made,
         10**9,
-        [adj, source, velocity, sound, couple] + kept[3:],
-        scratch=[pltpu.VMEM((7 * d.stack, 3 * B), F32), pltpu.VMEM((2 * d.stack, 6 * d.wall_k), F32)],
+        [adj, source, velocity, sound] + params + matrices,
+        scratch=room,
+        aliases={4 + len(params) + k: 2 + k for k in range(len(made))},
     )
     s0, s1, w0, w1, zl, zr = got
     edge = ((len(d.edges) * n, Z), F32)

time: 21.5 us -> 21.1 us (0.981)
  starting transfers between devices: 10.7 us -> 10.2 us
    ppermute x8, starting transfers between devices: 9.97 us -> 9.46 us  [swap_lines(): move = lambda value, pairs: lax.ppermute(value, AXES, pairs)]
    pallas_call x7 -> x8, Pallas kernels: 9.78 us -> 9.91 us  [call(): pl.pallas_call(functools.partial(kernel, d), out_shape=tuple((out_space(s...]
  transfers between devices with their start and end apart: 10 -> 10, of which waited for: 0 -> 0; matrix products, arithmetic and copies ran while one was open for 0% -> 0% of each run, Pallas kernels for 29% -> 28%
where the time goes in v4:
time: 21.1 us; the launch traced here: 20.9 us
  starting transfers between devices  10.2 us (48%)
  Pallas kernels  9.91 us (47%)
  between operations  0.79 us (4%)
    pallas_call x8, Pallas kernels, call(): pl.pallas_call(functools.partial(kernel, d), out_shape=tuple((out_space(s...  9.91 us
    ppermute x8, starting transfers between devices, swap_lines(): move = lambda value, pairs: lax.ppermute(value, AXES, pairs)  9.46 us
    ppermute x2, starting transfers between devices, swap_lines(): zl = zr = lax.ppermute(z, 'span', [(0, 1), (1, 0)])  0.72 us
  transfers between devices with their start and end apart: 10, of which 0 were waited for; matrix products, arithmetic and copies ran while one was open for 0% of the time, Pallas kernels for 28%

profile of v4, /device:TPU:0, one launch (start us, length us, event | category | flops | bytes accessed | tf_op | source)
XLA Modules:
  0.0 20.9 jit_solution(11267227046664986526)
XLA Ops:
  0.6 1.8 %pack_kernel.1 = (f32[1632,128]{1,0:T(8,128)S(1)}, f32[288,128]{1,0:T(8,128)S(1)}, f32[96,128]{1,0:T(8,128)S(1)}, f32[3,17,2,17]{3,2,1,0:T(2,128)S(1)}, f32[17,1...) custom-call(f32[1632,128]{1,0:T(8,128)} %bitcast.10, ...), custom_call_target="tpu_custom_call" | custom-call | bytes 1138928 | tf_op jit(solution)/shard_map/pack_kernel/pallas_call | solution.py:562
  2.4 0.5 %early_kernel.1 = (bf16[816,432]{1,0:T(8,128)(2,1)S(1)}, bf16[136,144]{1,0:T(8,128)(2,1)S(1)}, bf16[136,432]{1,0:T(8,128)(2,1)S(1)}, f32[288,128]{1,0:T(8,128)S(...) custom-call(f32[3,17,2,17]{3,2,1,0:T(2,128)S(1)} %get-tuple-element., ...), custom_call_target="tpu_custom_call", output_to_operand_aliasing={{4}: (6, {}), {5}: (7, {}), {6}: (8, {}), {7}: (9, {}), {8}... | custom-call | bytes 499952 | tf_op jit(solution)/shard_map/early_kernel/pallas_call | solution.py:562
  3.0 0.5 %collective-permute-start = (f32[224,128]{1,0:T(8,128)S(1)}, f32[224,128]{1,0:T(8,128)S(1)}, u32[]{:S(2)}, u32[]{:S(2)}) collective-permute-start(f32[224,128]{1,0:T(8,128)S(1)} %get-tuple-element.71), channel_id=1, source_target_pairs={{0,1},{1,0},{2,3},{3,2},{4,5},{5,4},{6,7},{7,6},{8,9},{9,8},{10,11... | collective-permute-start | bytes 344072 | tf_op jit(solution)/shard_map/ppermute | solution.py:540
  3.5 2.6 %collective-permute-start.1 = (f32[224,128]{1,0:T(8,128)S(1)}, f32[224,128]{1,0:T(8,128)S(1)}, u32[]{:S(2)}, u32[]{:S(2)}) collective-permute-start(f32[224,128]{1,0:T(8,128)S(1)} %get-tuple-element.72), channel_id=1, source_target_pairs={{0,4},{1,2},{2,1},{3,7},{4,0},{5,6},{6,5},{7,3},{8,12},{9,10},{10,... | collective-permute-start | bytes 344072 | tf_op jit(solution)/shard_map/ppermute | solution.py:540
  6.0 0.1 collective-permute-start.2
  6.1 2.0 %collective-permute-start.3 = (f32[144,128]{1,0:T(8,128)S(1)}, f32[144,128]{1,0:T(8,128)S(1)}, u32[]{:S(2)}, u32[]{:S(2)}) collective-permute-start(f32[144,128]{1,0:T(8,128)S(1)} %get-tuple-element.79), channel_id=1, source_target_pairs={{0,8},{1,9},{2,10},{3,11},{4,12},{5,13},{6,14},{7,15},{8,0},{9,1},... | collective-permute-start | bytes 221192 | tf_op jit(solution)/shard_map/ppermute | solution.py:540
  8.2 0.5 %collective-permute-start.4 = (f32[144,128]{1,0:T(8,128)S(1)}, f32[144,128]{1,0:T(8,128)S(1)}, u32[]{:S(2)}, u32[]{:S(2)}) collective-permute-start(f32[144,128]{1,0:T(8,128)S(1)} %get-tuple-element.80), channel_id=1, source_target_pairs={{0,1},{1,0},{2,3},{3,2},{4,5},{5,4},{6,7},{7,6},{8,16},{9,17},{10,... | collective-permute-start | bytes 221192 | tf_op jit(solution)/shard_map/ppermute | solution.py:540
  8.7 1.9 %first_local_kernel.1 = (f32[1632,128]{1,0:T(8,128)S(1)}, f32[96,128]{1,0:T(8,128)S(1)}, bf16[816,432]{1,0:T(8,128)(2,1)S(1)}, bf16[136,144]{1,0:T(8,128)(2,1)S(...) custom-call(f32[1632,128]{1,0:T(8,128)S(1)} %get-tuple-element.51.ad, ...), custom_call_target="tpu_custom_call", output_to_operand_aliasing={{2}: (10, {}), {3}: (11, {}), {4}: (12, {}), {5}: (13, {})} | custom-call | flops 1000000000 | bytes 2983664 | tf_op jit(solution)/shard_map/first_local_kernel/pallas_call | solution.py:562
  10.6 0.0 collective-permute-done.2.zl.zr
  10.6 0.0 collective-permute-done.w0
  10.6 0.0 collective-permute-done.1.w1
  10.6 1.1 %first_inner_kernel.1 = (f32[1632,128]{1,0:T(8,128)S(1)}, f32[96,128]{1,0:T(8,128)S(1)}, f32[192,128]{1,0:T(8,128)S(1)}, f32[272,128]{1,0:T(8,128)S(1)}, f32[224...) custom-call(f32[1632,128]{1,0:T(8,128)S(1)} %get-tuple-element.69.partial, ...), custom_call_target="tpu_custom_call" | custom-call | flops 100000000 | bytes 3040768 | tf_op jit(solution)/shard_map/first_inner_kernel/pallas_call | solution.py:562
  11.8 0.6 %first_stream_kernel.1 = (f32[1632,128]{1,0:T(8,128)S(1)}, f32[96,128]{1,0:T(8,128)S(1)}, f32[224,128]{1,0:T(8,128)S(1)}, f32[224,128]{1,0:T(8,128)S(1)}, f32[32...) custom-call(f32[272,128]{1,0:T(8,128)S(1)} %get-tuple-element.77.edg, ...), custom_call_target="tpu_custom_call", output_to_operand_aliasing={{0}: (9, {}), {1}: (2, {}), {2}: (10, {}), {3}: (11, {}), {... | custom-call | flops 10000000 | bytes 3271936 | tf_op jit(solution)/shard_map/first_stream_kernel/pallas_call | solution.py:562
  12.4 0.1 collective-permute-start.5
  12.5 1.4 %collective-permute-start.6 = (f32[224,128]{1,0:T(8,128)S(1)}, f32[224,128]{1,0:T(8,128)S(1)}, u32[]{:S(2)}, u32[]{:S(2)}) collective-permute-start(f32[224,128]{1,0:T(8,128)S(1)} %get-tuple-element.90), channel_id=1, source_target_pairs={{0,4},{1,2},{2,1},{3,7},{4,0},{5,6},{6,5},{7,3},{8,12},{9,10},{10,... | collective-permute-start | bytes 344072 | tf_op jit(solution)/shard_map/ppermute | solution.py:540
  13.9 0.6 %collective-permute-start.7 = (f32[32,128]{1,0:T(8,128)S(1)}, f32[32,128]{1,0:T(8,128)S(1)}, u32[]{:S(2)}, u32[]{:S(2)}) collective-permute-start(f32[32,128]{1,0:T(8,128)S(1)} %get-tuple-element.91), channel_id=1, source_target_pairs={{0,4},{4,0},{1,5},{5,1},{2,6},{6,2},{3,7},{7,3},{8,12},{12,8},{9,1... | collective-permute-start | bytes 49160 | tf_op jit(solution)/shard_map/ppermute | solution.py:549
  14.6 2.3 %collective-permute-start.8 = (f32[144,128]{1,0:T(8,128)S(1)}, f32[144,128]{1,0:T(8,128)S(1)}, u32[]{:S(2)}, u32[]{:S(2)}) collective-permute-start(f32[144,128]{1,0:T(8,128)S(1)} %get-tuple-element.94), channel_id=1, source_target_pairs={{0,8},{1,9},{2,10},{3,11},{4,12},{5,13},{6,14},{7,15},{8,0},{9,1},... | collective-permute-start | bytes 221192 | tf_op jit(solution)/shard_map/ppermute | solution.py:540
  16.9 1.8 %later_local_kernel.1.partial = f32[1632,128]{1,0:T(8,128)S(1)} custom-call(f32[1632,128]{1,0:T(8,128)S(1)} %get-tuple-element.85.adj, f32[17,96,128]{2,1,0:T(8,128)S(1)} %bitcast.9, f32[288,128]{1,0:T(8,128)S(1)} %get-tuple-element.52.vel, f32[96,128]{1,0:T(8,128)S(1)} %get-tuple-element.53.snd, f32[96,128]{1,0:T(8,128)S(1)} %get-tuple-element.86.rs.rs_full, ...), custom_call_target="tpu_custom_call" | custom-call | flops 1000000000 | bytes 2769408 | tf_op jit(solution)/shard_map/later_local_kernel/pallas_call | solution.py:562
  18.7 0.0 collective-permute-done.5.w0
  18.7 0.0 collective-permute-done.6.w1
  18.7 0.9 %later_inner_kernel.1 = (f32[17,96,128]{2,1,0:T(8,128)S(1)}, f32[17,96,128]{2,1,0:T(8,128)S(1)}, f32[272,128]{1,0:T(8,128)S(1)}) custom-call(f32[1632,128]{1,0:T(8,128)S(1)} %later_local_kernel.1.partial, f32[1632,128]{1,0:T(8,128)S(1)} %get-tuple-element.85.adj, f32[96,128]{1,0:T(8,128)S(1)} %get-tuple-element.86.rs.rs_full, ...), custom_call_target="tpu_custom_call" | custom-call | flops 100000000 | bytes 2942464 | tf_op jit(solution)/shard_map/later_inner_kernel/pallas_call | solution.py:562
  19.7 0.0 collective-permute-done.8.s0
  19.7 0.0 collective-permute-done.9.s1
  19.7 1.2 %later_stream_kernel.1 = (f32[17,96,128]{2,1,0:T(8,128)}, f32[17,96,128]{2,1,0:T(8,128)}) custom-call(f32[272,128]{1,0:T(8,128)S(1)} %get-tuple-element.92.edge, f32[1632,128]{1,0:T(8,128)S(1)} %get-tuple-element.85.adj, f32[96,128]{1,0:T(8,128)S(1)} %get-tuple-element.86.rs.rs_full, f32[16,128]{1,0:T(8,128)S(1)} %get-tuple-element.93.rates, ...), custom_call_target="tpu_custom_call" | custom-call | flops 10000000 | bytes 3673344 | tf_op jit(solution)/shard_map/later_stream_kernel/pallas_call | solution.py:562
  (6 shorter events, 0.0 us)
Async XLA Ops:
  0.6 8.1 %copy-start = (f32[17,12,8,128]{3,2,1,0:T(8,128)S(1)}, f32[17,12,8,128]{3,2,1,0:T(8,128)}, u32[]{:S(2)}) copy-start(f32[17,12,8,128]{3,2,1,0:T(8,128)} %param.11) | copy-start | bytes 2506756
  3.0 7.7 %collective-permute-start = (f32[224,128]{1,0:T(8,128)S(1)}, f32[224,128]{1,0:T(8,128)S(1)}, u32[]{:S(2)}, u32[]{:S(2)}) collective-permute-start(f32[224,128]{1,0:T(8,128)S(1)} %get-tuple-element.71), channel_id=1, source_target_pairs={{0,1},{1,0},{2,3},{3,2},{4,5},{5,4},{6,7},{7,6},{8,9},{9,8},{10,11... | collective-permute-start | bytes 344072 | tf_op jit(solution)/shard_map/ppermute | solution.py:540
  3.5 7.1 %collective-permute-start.1 = (f32[224,128]{1,0:T(8,128)S(1)}, f32[224,128]{1,0:T(8,128)S(1)}, u32[]{:S(2)}, u32[]{:S(2)}) collective-permute-start(f32[224,128]{1,0:T(8,128)S(1)} %get-tuple-element.72), channel_id=1, source_target_pairs={{0,4},{1,2},{2,1},{3,7},{4,0},{5,6},{6,5},{7,3},{8,12},{9,10},{10,... | collective-permute-start | bytes 344072 | tf_op jit(solution)/shard_map/ppermute | solution.py:540
  6.0 4.6 %collective-permute-start.2 = (f32[32,128]{1,0:T(8,128)S(1)}, f32[32,128]{1,0:T(8,128)S(1)}, u32[]{:S(2)}, u32[]{:S(2)}) collective-permute-start(f32[32,128]{1,0:T(8,128)S(1)} %get-tuple-element.73), channel_id=1, source_target_pairs={{0,4},{4,0},{1,5},{5,1},{2,6},{6,2},{3,7},{7,3},{8,12},{12,8},{9,1... | collective-permute-start | bytes 49160 | tf_op jit(solution)/shard_map/ppermute | solution.py:549
  6.1 5.7 %collective-permute-start.3 = (f32[144,128]{1,0:T(8,128)S(1)}, f32[144,128]{1,0:T(8,128)S(1)}, u32[]{:S(2)}, u32[]{:S(2)}) collective-permute-start(f32[144,128]{1,0:T(8,128)S(1)} %get-tuple-element.79), channel_id=1, source_target_pairs={{0,8},{1,9},{2,10},{3,11},{4,12},{5,13},{6,14},{7,15},{8,0},{9,1},... | collective-permute-start | bytes 221192 | tf_op jit(solution)/shard_map/ppermute | solution.py:540
  8.2 3.6 %collective-permute-start.4 = (f32[144,128]{1,0:T(8,128)S(1)}, f32[144,128]{1,0:T(8,128)S(1)}, u32[]{:S(2)}, u32[]{:S(2)}) collective-permute-start(f32[144,128]{1,0:T(8,128)S(1)} %get-tuple-element.80), channel_id=1, source_target_pairs={{0,1},{1,0},{2,3},{3,2},{4,5},{5,4},{6,7},{7,6},{8,16},{9,17},{10,... | collective-permute-start | bytes 221192 | tf_op jit(solution)/shard_map/ppermute | solution.py:540
  12.4 6.3 %collective-permute-start.5 = (f32[224,128]{1,0:T(8,128)S(1)}, f32[224,128]{1,0:T(8,128)S(1)}, u32[]{:S(2)}, u32[]{:S(2)}) collective-permute-start(f32[224,128]{1,0:T(8,128)S(1)} %get-tuple-element.89), channel_id=1, source_target_pairs={{0,1},{1,0},{2,3},{3,2},{4,5},{5,4},{6,7},{7,6},{8,9},{9,8},{10,11... | collective-permute-start | bytes 344072 | tf_op jit(solution)/shard_map/ppermute | solution.py:540
  12.5 6.2 %collective-permute-start.6 = (f32[224,128]{1,0:T(8,128)S(1)}, f32[224,128]{1,0:T(8,128)S(1)}, u32[]{:S(2)}, u32[]{:S(2)}) collective-permute-start(f32[224,128]{1,0:T(8,128)S(1)} %get-tuple-element.90), channel_id=1, source_target_pairs={{0,4},{1,2},{2,1},{3,7},{4,0},{5,6},{6,5},{7,3},{8,12},{9,10},{10,... | collective-permute-start | bytes 344072 | tf_op jit(solution)/shard_map/ppermute | solution.py:540
  13.9 4.8 %collective-permute-start.7 = (f32[32,128]{1,0:T(8,128)S(1)}, f32[32,128]{1,0:T(8,128)S(1)}, u32[]{:S(2)}, u32[]{:S(2)}) collective-permute-start(f32[32,128]{1,0:T(8,128)S(1)} %get-tuple-element.91), channel_id=1, source_target_pairs={{0,4},{4,0},{1,5},{5,1},{2,6},{6,2},{3,7},{7,3},{8,12},{12,8},{9,1... | collective-permute-start | bytes 49160 | tf_op jit(solution)/shard_map/ppermute | solution.py:549
  14.6 5.1 %collective-permute-start.8 = (f32[144,128]{1,0:T(8,128)S(1)}, f32[144,128]{1,0:T(8,128)S(1)}, u32[]{:S(2)}, u32[]{:S(2)}) collective-permute-start(f32[144,128]{1,0:T(8,128)S(1)} %get-tuple-element.94), channel_id=1, source_target_pairs={{0,8},{1,9},{2,10},{3,11},{4,12},{5,13},{6,14},{7,15},{8,0},{9,1},... | collective-permute-start | bytes 221192 | tf_op jit(solution)/shard_map/ppermute | solution.py:540
  16.9 2.8 %collective-permute-start.9 = (f32[144,128]{1,0:T(8,128)S(1)}, f32[144,128]{1,0:T(8,128)S(1)}, u32[]{:S(2)}, u32[]{:S(2)}) collective-permute-start(f32[144,128]{1,0:T(8,128)S(1)} %get-tuple-element.95), channel_id=1, source_target_pairs={{0,1},{1,0},{2,3},{3,2},{4,5},{5,4},{6,7},{7,6},{8,16},{9,17},{10,... | collective-permute-start | bytes 221192 | tf_op jit(solution)/shard_map/ppermute | solution.py:540

commit v5 on v4

--- a/solution.py
+++ b/solution.py
@@ -223,61 +223,68 @@
 
 
 def sweep_local(d, adj, src, vel, snd, mk, wall_coef, rates_of, out, rs_out):
-    V, X, W, Z, n = d.V, d.X, d.W, d.Z, d.n
+    X, W, Z, n = d.X, d.W, d.Z, d.n
     lane, row = lanes(d, W), row_ids(d)
     wall_flag = (lax.axis_index("wall") == 0).astype(F32)
-    radius = [[radius_at(d, vel, snd, k, x) for x in range(X)] for k in range(3)]
-    step = 2
-    products = {}
-
-    def product(x, k):
-        chunk, offset = products[x]
-        return chunk[k * n : (k + 1) * n, offset * Z : (offset + 1) * Z]
-
-    def finish(x):
-        a = d.plane(adj, x)
+    half = [[0.5 * radius_at(d, vel, snd, k, x) for x in range(X)] for k in range(3)]
+    sums = {}
+
+    def begin(x):
         total = 1.0
-        terms = []
-        half = [0.5 * radius[k][x] for k in range(3)]
-        for k, neighbour in ((0, x - 1), (1, x + 1)):
-            rate = half[0]
+        for neighbour in (x - 1, x + 1):
+            total = total + half[0][x]
             if 0 <= neighbour < X:
-                rate = rate + 0.5 * radius[0][neighbour]
-                terms.append((rate, product(neighbour, k)))
-            total = total + rate
-        for k, edge, turn in ((2, 0, 1), (3, W - 1, W - 1)):
-            near = jnp.where(row == edge, 0.0, pltpu.roll(half[1], turn, 0))
-            rate = half[1] + near
-            terms.append((rate, product(x, k)))
-            total = total + rate
-        for k, edge, turn in ((4, 0, 1), (5, Z - 1, Z - 1)):
-            near = jnp.where(lane == edge, 0.0, pltpu.roll(half[2], turn, 1))
-            total = total + half[2] + near
-            rate = jnp.where(lane == edge, 0.0, half[2] + near)
-            terms.append((rate, pltpu.roll(product(x, k), turn, 1)))
+                total = total + half[0][neighbour]
+        rates = []
+        for edge, turn in ((0, 1), (W - 1, W - 1)):
+            near = jnp.where(row == edge, 0.0, pltpu.roll(half[1][x], turn, 0))
+            rates.append(half[1][x] + near)
+            total = total + rates[-1]
+        for edge, turn in ((0, 1), (Z - 1, Z - 1)):
+            near = jnp.where(lane == edge, 0.0, pltpu.roll(half[2][x], turn, 1))
+            total = total + half[2][x] + near
+            rates.append(jnp.where(lane == edge, 0.0, half[2][x] + near))
         if rates_of is None:
             rs_out[d.block(0, x), :] = total
         else:
             total = rates_of[d.block(0, x), :]
-        result = d.plane3(src, x) - d.each(total) * a
-        for rate, value in terms:
-            result = result - d.each(rate) * value
-        d.store_plane(out, x, result)
-        spot = d.rows_at(x, 0)
-        factor = wall_flag * radius[1][x][:1]
-        coef = wall_coef[x * d.stack : x * d.stack + V, :]
-        out[spot, :] = out[spot, :] - factor * coef * adj[spot, :]
+        sums[x] = d.plane3(src, x) - d.each(total) * d.plane(adj, x)
+        return rates
+
+    def subtract(x, rate, value):
+        sums[x] = sums[x] - d.each(rate) * value
 
     done = 0
+    step = 2
+    begun = {}
     for start in range(0, X, step):
         here = list(range(start, min(X, start + step)))
-        right = jnp.concatenate([padded_plane(d, d.plane(adj, x)) for x in here], axis=1)
-        chunk = dot(mk[...], split3(right))
-        for offset, x in enumerate(here):
-            products[x] = (chunk, offset)
-        while done < X and (done + 1 in products or (done + 1 == X and done in products)):
-            finish(done)
+        for x in range(max(0, start - 1), min(X, start + step + 1)):
+            if x not in begun:
+                begun[x] = begin(x)
+        right = split3(jnp.concatenate([padded_plane(d, d.plane(adj, x)) for x in here], axis=1))
+        for k in (0, 2, 4):
+            both = dot(mk[k * n : (k + 2) * n, :], right)
+            for side in range(2):
+                for offset, x in enumerate(here):
+                    value = both[side * n : (side + 1) * n, offset * Z : (offset + 1) * Z]
+                    if k == 0:
+                        to = x + 1 - 2 * side
+                        if 0 <= to < X:
+                            subtract(to, half[0][x] + half[0][to], value)
+                    elif k == 2:
+                        subtract(x, begun[x][side], value)
+                    else:
+                        turn = (1, Z - 1)[side]
+                        subtract(x, begun[x][2 + side], pltpu.roll(value, turn, 1))
+        while done < X and (done < here[-1] or here[-1] == X - 1):
+            d.store_plane(out, done, sums.pop(done))
             done += 1
+    for x in range(X):
+        spot = d.rows_at(x, 0)
+        factor = wall_flag * (2.0 * half[1][x][:1])
+        coef = wall_coef[x * d.stack : x * d.stack + d.V, :]
+        out[spot, :] = out[spot, :] - factor * coef * adj[spot, :]
 
 
 def early():

time: 21.1 us -> 21 us (level)
  transfers between devices with their start and end apart: 10 -> 10, of which waited for: 0 -> 0; matrix products, arithmetic and copies ran while one was open for 0% -> 0% of each run, Pallas kernels for 28% -> 27%
where the time goes in v5:
time: 21 us; the launch traced here: 20.8 us
  starting transfers between devices  10.2 us (49%)
  Pallas kernels  9.75 us (46%)
  between operations  0.79 us (4%)
    pallas_call x8, Pallas kernels, call(): pl.pallas_call(functools.partial(kernel, d), out_shape=tuple((out_space(s...  9.75 us
    ppermute x8, starting transfers between devices, swap_lines(): move = lambda value, pairs: lax.ppermute(value, AXES, pairs)  9.47 us
    ppermute x2, starting transfers between devices, swap_lines(): zl = zr = lax.ppermute(z, 'span', [(0, 1), (1, 0)])  0.72 us
  transfers between devices with their start and end apart: 10, of which 0 were waited for; matrix products, arithmetic and copies ran while one was open for 0% of the time, Pallas kernels for 27%

profile of v5, /device:TPU:0, one launch (start us, length us, event | category | flops | bytes accessed | tf_op | source)
XLA Modules:
  0.0 20.8 jit_solution(4681754686612397935)
XLA Ops:
  0.6 1.8 %pack_kernel.1 = (f32[1632,128]{1,0:T(8,128)S(1)}, f32[288,128]{1,0:T(8,128)S(1)}, f32[96,128]{1,0:T(8,128)S(1)}, f32[3,17,2,17]{3,2,1,0:T(2,128)S(1)}, f32[17,1...) custom-call(f32[1632,128]{1,0:T(8,128)} %bitcast.10, ...), custom_call_target="tpu_custom_call" | custom-call | bytes 1138928 | tf_op jit(solution)/shard_map/pack_kernel/pallas_call | solution.py:569
  2.4 0.5 %early_kernel.1 = (bf16[816,432]{1,0:T(8,128)(2,1)S(1)}, bf16[136,144]{1,0:T(8,128)(2,1)S(1)}, bf16[136,432]{1,0:T(8,128)(2,1)S(1)}, f32[288,128]{1,0:T(8,128)S(...) custom-call(f32[3,17,2,17]{3,2,1,0:T(2,128)S(1)} %get-tuple-element., ...), custom_call_target="tpu_custom_call", output_to_operand_aliasing={{4}: (6, {}), {5}: (7, {}), {6}: (8, {}), {7}: (9, {}), {8}... | custom-call | bytes 499952 | tf_op jit(solution)/shard_map/early_kernel/pallas_call | solution.py:569
  3.0 0.5 %collective-permute-start = (f32[224,128]{1,0:T(8,128)S(1)}, f32[224,128]{1,0:T(8,128)S(1)}, u32[]{:S(2)}, u32[]{:S(2)}) collective-permute-start(f32[224,128]{1,0:T(8,128)S(1)} %get-tuple-element.71), channel_id=1, source_target_pairs={{0,1},{1,0},{2,3},{3,2},{4,5},{5,4},{6,7},{7,6},{8,9},{9,8},{10,11... | collective-permute-start | bytes 344072 | tf_op jit(solution)/shard_map/ppermute | solution.py:547
  3.5 2.6 %collective-permute-start.1 = (f32[224,128]{1,0:T(8,128)S(1)}, f32[224,128]{1,0:T(8,128)S(1)}, u32[]{:S(2)}, u32[]{:S(2)}) collective-permute-start(f32[224,128]{1,0:T(8,128)S(1)} %get-tuple-element.72), channel_id=1, source_target_pairs={{0,4},{1,2},{2,1},{3,7},{4,0},{5,6},{6,5},{7,3},{8,12},{9,10},{10,... | collective-permute-start | bytes 344072 | tf_op jit(solution)/shard_map/ppermute | solution.py:547
  6.0 0.1 collective-permute-start.2
  6.1 2.0 %collective-permute-start.3 = (f32[144,128]{1,0:T(8,128)S(1)}, f32[144,128]{1,0:T(8,128)S(1)}, u32[]{:S(2)}, u32[]{:S(2)}) collective-permute-start(f32[144,128]{1,0:T(8,128)S(1)} %get-tuple-element.79), channel_id=1, source_target_pairs={{0,8},{1,9},{2,10},{3,11},{4,12},{5,13},{6,14},{7,15},{8,0},{9,1},... | collective-permute-start | bytes 221192 | tf_op jit(solution)/shard_map/ppermute | solution.py:547
  8.2 0.5 %collective-permute-start.4 = (f32[144,128]{1,0:T(8,128)S(1)}, f32[144,128]{1,0:T(8,128)S(1)}, u32[]{:S(2)}, u32[]{:S(2)}) collective-permute-start(f32[144,128]{1,0:T(8,128)S(1)} %get-tuple-element.80), channel_id=1, source_target_pairs={{0,1},{1,0},{2,3},{3,2},{4,5},{5,4},{6,7},{7,6},{8,16},{9,17},{10,... | collective-permute-start | bytes 221192 | tf_op jit(solution)/shard_map/ppermute | solution.py:547
  8.7 1.8 %first_local_kernel.1 = (f32[1632,128]{1,0:T(8,128)S(1)}, f32[96,128]{1,0:T(8,128)S(1)}, bf16[816,432]{1,0:T(8,128)(2,1)S(1)}, bf16[136,144]{1,0:T(8,128)(2,1)S(...) custom-call(f32[1632,128]{1,0:T(8,128)S(1)} %get-tuple-element.51.ad, ...), custom_call_target="tpu_custom_call", output_to_operand_aliasing={{2}: (10, {}), {3}: (11, {}), {4}: (12, {}), {5}: (13, {})} | custom-call | flops 1000000000 | bytes 2983664 | tf_op jit(solution)/shard_map/first_local_kernel/pallas_call | solution.py:569
  10.5 0.0 collective-permute-done.2.zl.zr
  10.5 0.0 collective-permute-done.w0
  10.5 1.1 %first_inner_kernel.1 = (f32[1632,128]{1,0:T(8,128)S(1)}, f32[96,128]{1,0:T(8,128)S(1)}, f32[192,128]{1,0:T(8,128)S(1)}, f32[272,128]{1,0:T(8,128)S(1)}, f32[224...) custom-call(f32[1632,128]{1,0:T(8,128)S(1)} %get-tuple-element.69.partial, ...), custom_call_target="tpu_custom_call" | custom-call | flops 100000000 | bytes 3040768 | tf_op jit(solution)/shard_map/first_inner_kernel/pallas_call | solution.py:569
  11.7 0.0 collective-permute-done.3.s0
  11.7 0.6 %first_stream_kernel.1 = (f32[1632,128]{1,0:T(8,128)S(1)}, f32[96,128]{1,0:T(8,128)S(1)}, f32[224,128]{1,0:T(8,128)S(1)}, f32[224,128]{1,0:T(8,128)S(1)}, f32[32...) custom-call(f32[272,128]{1,0:T(8,128)S(1)} %get-tuple-element.77.edg, ...), custom_call_target="tpu_custom_call", output_to_operand_aliasing={{0}: (9, {}), {1}: (2, {}), {2}: (10, {}), {3}: (11, {}), {... | custom-call | flops 10000000 | bytes 3271936 | tf_op jit(solution)/shard_map/first_stream_kernel/pallas_call | solution.py:569
  12.3 0.1 collective-permute-start.5
  12.4 1.4 %collective-permute-start.6 = (f32[224,128]{1,0:T(8,128)S(1)}, f32[224,128]{1,0:T(8,128)S(1)}, u32[]{:S(2)}, u32[]{:S(2)}) collective-permute-start(f32[224,128]{1,0:T(8,128)S(1)} %get-tuple-element.90), channel_id=1, source_target_pairs={{0,4},{1,2},{2,1},{3,7},{4,0},{5,6},{6,5},{7,3},{8,12},{9,10},{10,... | collective-permute-start | bytes 344072 | tf_op jit(solution)/shard_map/ppermute | solution.py:547
  13.8 0.6 %collective-permute-start.7 = (f32[32,128]{1,0:T(8,128)S(1)}, f32[32,128]{1,0:T(8,128)S(1)}, u32[]{:S(2)}, u32[]{:S(2)}) collective-permute-start(f32[32,128]{1,0:T(8,128)S(1)} %get-tuple-element.91), channel_id=1, source_target_pairs={{0,4},{4,0},{1,5},{5,1},{2,6},{6,2},{3,7},{7,3},{8,12},{12,8},{9,1... | collective-permute-start | bytes 49160 | tf_op jit(solution)/shard_map/ppermute | solution.py:556
  14.5 2.3 %collective-permute-start.8 = (f32[144,128]{1,0:T(8,128)S(1)}, f32[144,128]{1,0:T(8,128)S(1)}, u32[]{:S(2)}, u32[]{:S(2)}) collective-permute-start(f32[144,128]{1,0:T(8,128)S(1)} %get-tuple-element.94), channel_id=1, source_target_pairs={{0,8},{1,9},{2,10},{3,11},{4,12},{5,13},{6,14},{7,15},{8,0},{9,1},... | collective-permute-start | bytes 221192 | tf_op jit(solution)/shard_map/ppermute | solution.py:547
  16.8 0.0 collective-permute-start.9
  16.8 1.8 %later_local_kernel.1.partial = f32[1632,128]{1,0:T(8,128)S(1)} custom-call(f32[1632,128]{1,0:T(8,128)S(1)} %get-tuple-element.85.adj, f32[17,96,128]{2,1,0:T(8,128)S(1)} %bitcast.9, f32[288,128]{1,0:T(8,128)S(1)} %get-tuple-element.52.vel, f32[96,128]{1,0:T(8,128)S(1)} %get-tuple-element.53.snd, f32[96,128]{1,0:T(8,128)S(1)} %get-tuple-element.86.rs.rs_full, ...), custom_call_target="tpu_custom_call" | custom-call | flops 1000000000 | bytes 2769408 | tf_op jit(solution)/shard_map/later_local_kernel/pallas_call | solution.py:569
  18.6 0.0 collective-permute-done.7.zl.zr
  18.6 0.0 collective-permute-done.5.w0
  18.6 0.9 %later_inner_kernel.1 = (f32[17,96,128]{2,1,0:T(8,128)S(1)}, f32[17,96,128]{2,1,0:T(8,128)S(1)}, f32[272,128]{1,0:T(8,128)S(1)}) custom-call(f32[1632,128]{1,0:T(8,128)S(1)} %later_local_kernel.1.partial, f32[1632,128]{1,0:T(8,128)S(1)} %get-tuple-element.85.adj, f32[96,128]{1,0:T(8,128)S(1)} %get-tuple-element.86.rs.rs_full, ...), custom_call_target="tpu_custom_call" | custom-call | flops 100000000 | bytes 2942464 | tf_op jit(solution)/shard_map/later_inner_kernel/pallas_call | solution.py:569
  19.5 0.0 collective-permute-done.8.s0
  19.5 1.2 %later_stream_kernel.1 = (f32[17,96,128]{2,1,0:T(8,128)}, f32[17,96,128]{2,1,0:T(8,128)}) custom-call(f32[272,128]{1,0:T(8,128)S(1)} %get-tuple-element.92.edge, f32[1632,128]{1,0:T(8,128)S(1)} %get-tuple-element.85.adj, f32[96,128]{1,0:T(8,128)S(1)} %get-tuple-element.86.rs.rs_full, f32[16,128]{1,0:T(8,128)S(1)} %get-tuple-element.93.rates, ...), custom_call_target="tpu_custom_call" | custom-call | flops 10000000 | bytes 3673344 | tf_op jit(solution)/shard_map/later_stream_kernel/pallas_call | solution.py:569
  (6 shorter events, 0.0 us)
Async XLA Ops:
  0.6 8.1 %copy-start = (f32[17,12,8,128]{3,2,1,0:T(8,128)S(1)}, f32[17,12,8,128]{3,2,1,0:T(8,128)}, u32[]{:S(2)}) copy-start(f32[17,12,8,128]{3,2,1,0:T(8,128)} %param.11) | copy-start | bytes 2506756
  3.0 7.5 %collective-permute-start = (f32[224,128]{1,0:T(8,128)S(1)}, f32[224,128]{1,0:T(8,128)S(1)}, u32[]{:S(2)}, u32[]{:S(2)}) collective-permute-start(f32[224,128]{1,0:T(8,128)S(1)} %get-tuple-element.71), channel_id=1, source_target_pairs={{0,1},{1,0},{2,3},{3,2},{4,5},{5,4},{6,7},{7,6},{8,9},{9,8},{10,11... | collective-permute-start | bytes 344072 | tf_op jit(solution)/shard_map/ppermute | solution.py:547
  3.5 7.0 %collective-permute-start.1 = (f32[224,128]{1,0:T(8,128)S(1)}, f32[224,128]{1,0:T(8,128)S(1)}, u32[]{:S(2)}, u32[]{:S(2)}) collective-permute-start(f32[224,128]{1,0:T(8,128)S(1)} %get-tuple-element.72), channel_id=1, source_target_pairs={{0,4},{1,2},{2,1},{3,7},{4,0},{5,6},{6,5},{7,3},{8,12},{9,10},{10,... | collective-permute-start | bytes 344072 | tf_op jit(solution)/shard_map/ppermute | solution.py:547
  6.0 4.5 %collective-permute-start.2 = (f32[32,128]{1,0:T(8,128)S(1)}, f32[32,128]{1,0:T(8,128)S(1)}, u32[]{:S(2)}, u32[]{:S(2)}) collective-permute-start(f32[32,128]{1,0:T(8,128)S(1)} %get-tuple-element.73), channel_id=1, source_target_pairs={{0,4},{4,0},{1,5},{5,1},{2,6},{6,2},{3,7},{7,3},{8,12},{12,8},{9,1... | collective-permute-start | bytes 49160 | tf_op jit(solution)/shard_map/ppermute | solution.py:556
  6.1 5.6 %collective-permute-start.3 = (f32[144,128]{1,0:T(8,128)S(1)}, f32[144,128]{1,0:T(8,128)S(1)}, u32[]{:S(2)}, u32[]{:S(2)}) collective-permute-start(f32[144,128]{1,0:T(8,128)S(1)} %get-tuple-element.79), channel_id=1, source_target_pairs={{0,8},{1,9},{2,10},{3,11},{4,12},{5,13},{6,14},{7,15},{8,0},{9,1},... | collective-permute-start | bytes 221192 | tf_op jit(solution)/shard_map/ppermute | solution.py:547
  8.2 3.5 %collective-permute-start.4 = (f32[144,128]{1,0:T(8,128)S(1)}, f32[144,128]{1,0:T(8,128)S(1)}, u32[]{:S(2)}, u32[]{:S(2)}) collective-permute-start(f32[144,128]{1,0:T(8,128)S(1)} %get-tuple-element.80), channel_id=1, source_target_pairs={{0,1},{1,0},{2,3},{3,2},{4,5},{5,4},{6,7},{7,6},{8,16},{9,17},{10,... | collective-permute-start | bytes 221192 | tf_op jit(solution)/shard_map/ppermute | solution.py:547
  12.3 6.3 %collective-permute-start.5 = (f32[224,128]{1,0:T(8,128)S(1)}, f32[224,128]{1,0:T(8,128)S(1)}, u32[]{:S(2)}, u32[]{:S(2)}) collective-permute-start(f32[224,128]{1,0:T(8,128)S(1)} %get-tuple-element.89), channel_id=1, source_target_pairs={{0,1},{1,0},{2,3},{3,2},{4,5},{5,4},{6,7},{7,6},{8,9},{9,8},{10,11... | collective-permute-start | bytes 344072 | tf_op jit(solution)/shard_map/ppermute | solution.py:547
  12.4 6.2 %collective-permute-start.6 = (f32[224,128]{1,0:T(8,128)S(1)}, f32[224,128]{1,0:T(8,128)S(1)}, u32[]{:S(2)}, u32[]{:S(2)}) collective-permute-start(f32[224,128]{1,0:T(8,128)S(1)} %get-tuple-element.90), channel_id=1, source_target_pairs={{0,4},{1,2},{2,1},{3,7},{4,0},{5,6},{6,5},{7,3},{8,12},{9,10},{10,... | collective-permute-start | bytes 344072 | tf_op jit(solution)/shard_map/ppermute | solution.py:547
  13.8 4.7 %collective-permute-start.7 = (f32[32,128]{1,0:T(8,128)S(1)}, f32[32,128]{1,0:T(8,128)S(1)}, u32[]{:S(2)}, u32[]{:S(2)}) collective-permute-start(f32[32,128]{1,0:T(8,128)S(1)} %get-tuple-element.91), channel_id=1, source_target_pairs={{0,4},{4,0},{1,5},{5,1},{2,6},{6,2},{3,7},{7,3},{8,12},{12,8},{9,1... | collective-permute-start | bytes 49160 | tf_op jit(solution)/shard_map/ppermute | solution.py:556
  14.5 5.1 %collective-permute-start.8 = (f32[144,128]{1,0:T(8,128)S(1)}, f32[144,128]{1,0:T(8,128)S(1)}, u32[]{:S(2)}, u32[]{:S(2)}) collective-permute-start(f32[144,128]{1,0:T(8,128)S(1)} %get-tuple-element.94), channel_id=1, source_target_pairs={{0,8},{1,9},{2,10},{3,11},{4,12},{5,13},{6,14},{7,15},{8,0},{9,1},... | collective-permute-start | bytes 221192 | tf_op jit(solution)/shard_map/ppermute | solution.py:547
  16.8 2.8 %collective-permute-start.9 = (f32[144,128]{1,0:T(8,128)S(1)}, f32[144,128]{1,0:T(8,128)S(1)}, u32[]{:S(2)}, u32[]{:S(2)}) collective-permute-start(f32[144,128]{1,0:T(8,128)S(1)} %get-tuple-element.95), channel_id=1, source_target_pairs={{0,1},{1,0},{2,3},{3,2},{4,5},{5,4},{6,7},{7,6},{8,16},{9,17},{10,... | collective-permute-start | bytes 221192 | tf_op jit(solution)/shard_map/ppermute | solution.py:547

commit v6 on v5

--- a/solution.py
+++ b/solution.py
@@ -95,10 +95,10 @@
         s_b[g * W : (g + 1) * W, :] = jnp.where(even, first, last)
 
 
-def pack_span(d, planes, block_of, radius_of, given, z_out):
+def pack_span(d, planes, block_of, radius_of, given, z_out, groups=None):
     V, X, W, Z = d.V, d.X, d.W, d.Z
     pair = lanes(d, W) // 2
-    for q in range(d.span_groups):
+    for q in range(d.span_groups) if groups is None else groups:
         rows = pl.ds(q * W, W)
         group = jnp.zeros((W, Z), F32) if given is None else given[rows, :]
         for v in range(q * d.per, min(V + 1, (q + 1) * d.per)):
@@ -141,15 +141,25 @@
     held, kept = refs[:count], refs[count : 2 * count]
     s_a, s_b, w_a, w_b, z_out, sems = refs[2 * count :]
     adj, vel, snd = kept[:3]
-    copies = [pltpu.make_async_copy(held[k], kept[k], sems.at[k]) for k in range(count)]
+    groups = -(-d.span_groups // 2)
+    size = d.X * d.W
+    front = min(d.V, groups * d.per) * size
+    parts = [pl.ds(0, front), pl.ds(front, d.rows - front)] if front < d.rows else [pl.ds(0, front)]
+    copies = [
+        pltpu.make_async_copy(held[0].at[part], adj.at[part], sems.at[count + k])
+        for k, part in enumerate(parts)
+    ]
+    copies += [pltpu.make_async_copy(held[k], kept[k], sems.at[k]) for k in range(1, count)]
     for copy in copies:
         copy.start()
-    for copy in copies:
-        copy.wait()
+    copies[0].wait()
     block_of = lambda v, x: adj[d.block(v, x), :]
     radius_of = functools.partial(radius_at, d, vel, snd)
+    pack_span(d, range(d.X), block_of, radius_of, None, z_out, range(groups))
+    for copy in copies[1:]:
+        copy.wait()
+    pack_span(d, range(d.X), block_of, radius_of, None, z_out, range(groups, d.span_groups))
     pack_stream(d, block_of, radius_of, s_a, s_b)
-    pack_span(d, range(d.X), block_of, radius_of, None, z_out)
     pack_walls(d, range(d.X), adj, radius_of, w_a, w_b)
 
 
@@ -421,7 +431,7 @@
 
 
 def later_inner_kernel(
-    d, partial, adj, rs_full, rates, w0, w1, zl, zr, mk, mw, pk, new_adj, residual, edge
+    d, partial, adj, rs_full, rates, w1, w0, zl, zr, mk, mw, pk, new_adj, residual, edge
 ):
     W, n = d.W, d.n
     span, _ = span_terms(d, zl, zr, mk)
@@ -535,7 +545,9 @@
         step = 1 if (at[axis] - odd) % 2 == 0 else -1
         if at[axis] >= odd and 0 <= at[axis] + step < sizes[axis]:
             to[axis] += step
-        elif (at[spare] ^ 1) < sizes[spare]:
+        elif spare == axis and sizes[axis] % 2 == 0:
+            to[axis] = sizes[axis] - 1 - at[axis]
+        elif spare != axis and (at[spare] ^ 1) < sizes[spare]:
             to[spare] ^= 1
         else:
             continue
@@ -547,7 +559,7 @@
     move = lambda value, pairs: lax.ppermute(value, AXES, pairs)
     s0 = move(s_a, exchange_pairs(sizes, 0, 0, 2))
     s1 = move(s_b, exchange_pairs(sizes, 0, 1, 2))
-    w1 = move(w_b, exchange_pairs(sizes, 2, 1, 1))
+    w1 = move(w_b, exchange_pairs(sizes, 2, 1, 2))
     w0 = move(w_a, exchange_pairs(sizes, 2, 0, 1))
     peers = sizes[1]
     if peers == 1:
@@ -606,7 +618,7 @@
         0,
         inputs,
         held=range(len(inputs)),
-        scratch=[sems(len(inputs))],
+        scratch=[sems(len(inputs) + 2)],
     )
     adj, velocity, sound = kept[:3]
     made = [
@@ -666,7 +678,7 @@
         d,
         [planes, planes, edge],
         10**8,
-        [partial, adj1, rs, rates, w0, w1, zl, zr, mk, mw, pk],
+        [partial, adj1, rs, rates, w1, w0, zl, zr, mk, mw, pk],
     )
     edge = ((V, len(d.edges) * W, Z), F32)
     adj2, residual = call(

time: 21 us -> 20.8 us (level)
    ppermute x8, starting transfers between devices: 9.47 us -> 7.66 us  [swap_lines(): move = lambda value, pairs: lax.ppermute(value, AXES, pairs)]
    ppermute x2, starting transfers between devices: 0.72 us -> 2.45 us  [swap_lines(): zl = zr = lax.ppermute(z, 'span', [(0, 1), (1, 0)])]
where the time goes in v6:
time: 20.8 us; the launch traced here: 20.6 us
  starting transfers between devices  10.1 us (49%)
  Pallas kernels  9.72 us (47%)
  between operations  0.78 us (4%)
    pallas_call x8, Pallas kernels, call(): pl.pallas_call(functools.partial(kernel, d), out_shape=tuple((out_space(s...  9.72 us
    ppermute x8, starting transfers between devices, swap_lines(): move = lambda value, pairs: lax.ppermute(value, AXES, pairs)  7.66 us
    ppermute x2, starting transfers between devices, swap_lines(): zl = zr = lax.ppermute(z, 'span', [(0, 1), (1, 0)])  2.45 us
  transfers between devices with their start and end apart: 10, of which 0 were waited for; matrix products, arithmetic and copies ran while one was open for 0% of the time, Pallas kernels for 27%

profile of v6, /device:TPU:0, one launch (start us, length us, event | category | flops | bytes accessed | tf_op | source)
XLA Modules:
  0.0 20.6 jit_solution(7451309354512227688)
XLA Ops:
  0.6 1.7 %pack_kernel.1 = (f32[1632,128]{1,0:T(8,128)S(1)}, f32[288,128]{1,0:T(8,128)S(1)}, f32[96,128]{1,0:T(8,128)S(1)}, f32[3,17,2,17]{3,2,1,0:T(2,128)S(1)}, f32[17,1...) custom-call(f32[1632,128]{1,0:T(8,128)} %bitcast.10, ...), custom_call_target="tpu_custom_call" | custom-call | bytes 1138928 | tf_op jit(solution)/shard_map/pack_kernel/pallas_call | solution.py:581
  2.4 0.5 %early_kernel.1 = (bf16[816,432]{1,0:T(8,128)(2,1)S(1)}, bf16[136,144]{1,0:T(8,128)(2,1)S(1)}, bf16[136,432]{1,0:T(8,128)(2,1)S(1)}, f32[288,128]{1,0:T(8,128)S(...) custom-call(f32[3,17,2,17]{3,2,1,0:T(2,128)S(1)} %get-tuple-element., ...), custom_call_target="tpu_custom_call", output_to_operand_aliasing={{4}: (6, {}), {5}: (7, {}), {6}: (8, {}), {7}: (9, {}), {8}... | custom-call | bytes 499952 | tf_op jit(solution)/shard_map/early_kernel/pallas_call | solution.py:581
  2.9 0.5 %collective-permute-start = (f32[224,128]{1,0:T(8,128)S(1)}, f32[224,128]{1,0:T(8,128)S(1)}, u32[]{:S(2)}, u32[]{:S(2)}) collective-permute-start(f32[224,128]{1,0:T(8,128)S(1)} %get-tuple-element.71), channel_id=1, source_target_pairs={{0,1},{1,0},{2,3},{3,2},{4,5},{5,4},{6,7},{7,6},{8,9},{9,8},{10,11... | collective-permute-start | bytes 344072 | tf_op jit(solution)/shard_map/ppermute | solution.py:559
  3.4 2.6 %collective-permute-start.1 = (f32[224,128]{1,0:T(8,128)S(1)}, f32[224,128]{1,0:T(8,128)S(1)}, u32[]{:S(2)}, u32[]{:S(2)}) collective-permute-start(f32[224,128]{1,0:T(8,128)S(1)} %get-tuple-element.72), channel_id=1, source_target_pairs={{0,3},{1,2},{2,1},{3,0},{4,7},{5,6},{6,5},{7,4},{8,11},{9,10},{10,... | collective-permute-start | bytes 344072 | tf_op jit(solution)/shard_map/ppermute | solution.py:559
  6.1 1.5 %collective-permute-start.2 = (f32[32,128]{1,0:T(8,128)S(1)}, f32[32,128]{1,0:T(8,128)S(1)}, u32[]{:S(2)}, u32[]{:S(2)}) collective-permute-start(f32[32,128]{1,0:T(8,128)S(1)} %get-tuple-element.73), channel_id=1, source_target_pairs={{0,4},{4,0},{1,5},{5,1},{2,6},{6,2},{3,7},{7,3},{8,12},{12,8},{9,1... | collective-permute-start | bytes 49160 | tf_op jit(solution)/shard_map/ppermute | solution.py:568
  7.6 1.6 %collective-permute-start.3 = (f32[144,128]{1,0:T(8,128)S(1)}, f32[144,128]{1,0:T(8,128)S(1)}, u32[]{:S(2)}, u32[]{:S(2)}) collective-permute-start(f32[144,128]{1,0:T(8,128)S(1)} %get-tuple-element.79), channel_id=1, source_target_pairs={{0,8},{1,9},{2,10},{3,11},{4,12},{5,13},{6,14},{7,15},{8,0},{9,1},... | collective-permute-start | bytes 221192 | tf_op jit(solution)/shard_map/ppermute | solution.py:559
  9.1 0.0 collective-permute-start.4
  9.2 1.8 %first_local_kernel.1 = (f32[1632,128]{1,0:T(8,128)S(1)}, f32[96,128]{1,0:T(8,128)S(1)}, bf16[816,432]{1,0:T(8,128)(2,1)S(1)}, bf16[136,144]{1,0:T(8,128)(2,1)S(...) custom-call(f32[1632,128]{1,0:T(8,128)S(1)} %get-tuple-element.51.ad, ...), custom_call_target="tpu_custom_call", output_to_operand_aliasing={{2}: (10, {}), {3}: (11, {}), {4}: (12, {}), {5}: (13, {})} | custom-call | flops 1000000000 | bytes 2983664 | tf_op jit(solution)/shard_map/first_local_kernel/pallas_call | solution.py:581
  11.0 0.0 collective-permute-done.2.zl.zr
  11.0 0.0 collective-permute-done.w0
  11.0 1.1 %first_inner_kernel.1 = (f32[1632,128]{1,0:T(8,128)S(1)}, f32[96,128]{1,0:T(8,128)S(1)}, f32[192,128]{1,0:T(8,128)S(1)}, f32[272,128]{1,0:T(8,128)S(1)}, f32[224...) custom-call(f32[1632,128]{1,0:T(8,128)S(1)} %get-tuple-element.69.partial, ...), custom_call_target="tpu_custom_call" | custom-call | flops 100000000 | bytes 3040768 | tf_op jit(solution)/shard_map/first_inner_kernel/pallas_call | solution.py:581
  12.2 0.0 collective-permute-done.4.s1
  12.2 0.6 %first_stream_kernel.1 = (f32[1632,128]{1,0:T(8,128)S(1)}, f32[96,128]{1,0:T(8,128)S(1)}, f32[224,128]{1,0:T(8,128)S(1)}, f32[224,128]{1,0:T(8,128)S(1)}, f32[32...) custom-call(f32[272,128]{1,0:T(8,128)S(1)} %get-tuple-element.77.edg, ...), custom_call_target="tpu_custom_call", output_to_operand_aliasing={{0}: (9, {}), {1}: (2, {}), {2}: (10, {}), {3}: (11, {}), {... | custom-call | flops 10000000 | bytes 3271936 | tf_op jit(solution)/shard_map/first_stream_kernel/pallas_call | solution.py:581
  12.8 0.7 %collective-permute-start.5 = (f32[224,128]{1,0:T(8,128)S(1)}, f32[224,128]{1,0:T(8,128)S(1)}, u32[]{:S(2)}, u32[]{:S(2)}) collective-permute-start(f32[224,128]{1,0:T(8,128)S(1)} %get-tuple-element.89), channel_id=1, source_target_pairs={{0,3},{1,2},{2,1},{3,0},{4,7},{5,6},{6,5},{7,4},{8,11},{9,10},{10,... | collective-permute-start | bytes 344072 | tf_op jit(solution)/shard_map/ppermute | solution.py:559
  13.4 0.0 collective-permute-start.6
  13.4 0.9 %collective-permute-start.7 = (f32[32,128]{1,0:T(8,128)S(1)}, f32[32,128]{1,0:T(8,128)S(1)}, u32[]{:S(2)}, u32[]{:S(2)}) collective-permute-start(f32[32,128]{1,0:T(8,128)S(1)} %get-tuple-element.91), channel_id=1, source_target_pairs={{0,4},{4,0},{1,5},{5,1},{2,6},{6,2},{3,7},{7,3},{8,12},{12,8},{9,1... | collective-permute-start | bytes 49160 | tf_op jit(solution)/shard_map/ppermute | solution.py:568
  14.4 2.2 %collective-permute-start.8 = (f32[144,128]{1,0:T(8,128)S(1)}, f32[144,128]{1,0:T(8,128)S(1)}, u32[]{:S(2)}, u32[]{:S(2)}) collective-permute-start(f32[144,128]{1,0:T(8,128)S(1)} %get-tuple-element.94), channel_id=1, source_target_pairs={{0,8},{1,9},{2,10},{3,11},{4,12},{5,13},{6,14},{7,15},{8,0},{9,1},... | collective-permute-start | bytes 221192 | tf_op jit(solution)/shard_map/ppermute | solution.py:559
  16.6 0.0 collective-permute-start.9
  16.6 1.8 %later_local_kernel.1.partial = f32[1632,128]{1,0:T(8,128)S(1)} custom-call(f32[1632,128]{1,0:T(8,128)S(1)} %get-tuple-element.85.adj, f32[17,96,128]{2,1,0:T(8,128)S(1)} %bitcast.9, f32[288,128]{1,0:T(8,128)S(1)} %get-tuple-element.52.vel, f32[96,128]{1,0:T(8,128)S(1)} %get-tuple-element.53.snd, f32[96,128]{1,0:T(8,128)S(1)} %get-tuple-element.86.rs.rs_full, ...), custom_call_target="tpu_custom_call" | custom-call | flops 1000000000 | bytes 2769408 | tf_op jit(solution)/shard_map/later_local_kernel/pallas_call | solution.py:581
  18.4 0.0 collective-permute-done.7.zl.zr
  18.5 0.0 collective-permute-done.6.w0
  18.5 0.9 %later_inner_kernel.1 = (f32[17,96,128]{2,1,0:T(8,128)S(1)}, f32[17,96,128]{2,1,0:T(8,128)S(1)}, f32[272,128]{1,0:T(8,128)S(1)}) custom-call(f32[1632,128]{1,0:T(8,128)S(1)} %later_local_kernel.1.partial, f32[1632,128]{1,0:T(8,128)S(1)} %get-tuple-element.85.adj, f32[96,128]{1,0:T(8,128)S(1)} %get-tuple-element.86.rs.rs_full, ...), custom_call_target="tpu_custom_call" | custom-call | flops 100000000 | bytes 2942464 | tf_op jit(solution)/shard_map/later_inner_kernel/pallas_call | solution.py:581
  19.4 0.0 collective-permute-done.9.s1
  19.4 1.2 %later_stream_kernel.1 = (f32[17,96,128]{2,1,0:T(8,128)}, f32[17,96,128]{2,1,0:T(8,128)}) custom-call(f32[272,128]{1,0:T(8,128)S(1)} %get-tuple-element.92.edge, f32[1632,128]{1,0:T(8,128)S(1)} %get-tuple-element.85.adj, f32[96,128]{1,0:T(8,128)S(1)} %get-tuple-element.86.rs.rs_full, f32[16,128]{1,0:T(8,128)S(1)} %get-tuple-element.93.rates, ...), custom_call_target="tpu_custom_call" | custom-call | flops 10000000 | bytes 3673344 | tf_op jit(solution)/shard_map/later_stream_kernel/pallas_call | solution.py:581
  (6 shorter events, 0.0 us)
Async XLA Ops:
  0.6 8.5 %copy-start = (f32[17,12,8,128]{3,2,1,0:T(8,128)S(1)}, f32[17,12,8,128]{3,2,1,0:T(8,128)}, u32[]{:S(2)}) copy-start(f32[17,12,8,128]{3,2,1,0:T(8,128)} %param.11) | copy-start | bytes 2506756
  2.9 8.1 %collective-permute-start = (f32[224,128]{1,0:T(8,128)S(1)}, f32[224,128]{1,0:T(8,128)S(1)}, u32[]{:S(2)}, u32[]{:S(2)}) collective-permute-start(f32[224,128]{1,0:T(8,128)S(1)} %get-tuple-element.71), channel_id=1, source_target_pairs={{0,1},{1,0},{2,3},{3,2},{4,5},{5,4},{6,7},{7,6},{8,9},{9,8},{10,11... | collective-permute-start | bytes 344072 | tf_op jit(solution)/shard_map/ppermute | solution.py:559
  3.4 7.5 %collective-permute-start.1 = (f32[224,128]{1,0:T(8,128)S(1)}, f32[224,128]{1,0:T(8,128)S(1)}, u32[]{:S(2)}, u32[]{:S(2)}) collective-permute-start(f32[224,128]{1,0:T(8,128)S(1)} %get-tuple-element.72), channel_id=1, source_target_pairs={{0,3},{1,2},{2,1},{3,0},{4,7},{5,6},{6,5},{7,4},{8,11},{9,10},{10,... | collective-permute-start | bytes 344072 | tf_op jit(solution)/shard_map/ppermute | solution.py:559
  6.1 4.9 %collective-permute-start.2 = (f32[32,128]{1,0:T(8,128)S(1)}, f32[32,128]{1,0:T(8,128)S(1)}, u32[]{:S(2)}, u32[]{:S(2)}) collective-permute-start(f32[32,128]{1,0:T(8,128)S(1)} %get-tuple-element.73), channel_id=1, source_target_pairs={{0,4},{4,0},{1,5},{5,1},{2,6},{6,2},{3,7},{7,3},{8,12},{12,8},{9,1... | collective-permute-start | bytes 49160 | tf_op jit(solution)/shard_map/ppermute | solution.py:568
  7.6 4.6 %collective-permute-start.3 = (f32[144,128]{1,0:T(8,128)S(1)}, f32[144,128]{1,0:T(8,128)S(1)}, u32[]{:S(2)}, u32[]{:S(2)}) collective-permute-start(f32[144,128]{1,0:T(8,128)S(1)} %get-tuple-element.79), channel_id=1, source_target_pairs={{0,8},{1,9},{2,10},{3,11},{4,12},{5,13},{6,14},{7,15},{8,0},{9,1},... | collective-permute-start | bytes 221192 | tf_op jit(solution)/shard_map/ppermute | solution.py:559
  9.1 3.0 %collective-permute-start.4 = (f32[144,128]{1,0:T(8,128)S(1)}, f32[144,128]{1,0:T(8,128)S(1)}, u32[]{:S(2)}, u32[]{:S(2)}) collective-permute-start(f32[144,128]{1,0:T(8,128)S(1)} %get-tuple-element.80), channel_id=1, source_target_pairs={{0,1},{1,0},{2,3},{3,2},{4,5},{5,4},{6,7},{7,6},{8,16},{9,17},{10,... | collective-permute-start | bytes 221192 | tf_op jit(solution)/shard_map/ppermute | solution.py:559
  12.8 5.7 %collective-permute-start.5 = (f32[224,128]{1,0:T(8,128)S(1)}, f32[224,128]{1,0:T(8,128)S(1)}, u32[]{:S(2)}, u32[]{:S(2)}) collective-permute-start(f32[224,128]{1,0:T(8,128)S(1)} %get-tuple-element.89), channel_id=1, source_target_pairs={{0,3},{1,2},{2,1},{3,0},{4,7},{5,6},{6,5},{7,4},{8,11},{9,10},{10,... | collective-permute-start | bytes 344072 | tf_op jit(solution)/shard_map/ppermute | solution.py:559
  13.4 5.0 %collective-permute-start.6 = (f32[224,128]{1,0:T(8,128)S(1)}, f32[224,128]{1,0:T(8,128)S(1)}, u32[]{:S(2)}, u32[]{:S(2)}) collective-permute-start(f32[224,128]{1,0:T(8,128)S(1)} %get-tuple-element.90), channel_id=1, source_target_pairs={{0,1},{1,0},{2,3},{3,2},{4,5},{5,4},{6,7},{7,6},{8,9},{9,8},{10,11... | collective-permute-start | bytes 344072 | tf_op jit(solution)/shard_map/ppermute | solution.py:559
  13.4 5.0 %collective-permute-start.7 = (f32[32,128]{1,0:T(8,128)S(1)}, f32[32,128]{1,0:T(8,128)S(1)}, u32[]{:S(2)}, u32[]{:S(2)}) collective-permute-start(f32[32,128]{1,0:T(8,128)S(1)} %get-tuple-element.91), channel_id=1, source_target_pairs={{0,4},{4,0},{1,5},{5,1},{2,6},{6,2},{3,7},{7,3},{8,12},{12,8},{9,1... | collective-permute-start | bytes 49160 | tf_op jit(solution)/shard_map/ppermute | solution.py:568
  14.4 5.0 %collective-permute-start.8 = (f32[144,128]{1,0:T(8,128)S(1)}, f32[144,128]{1,0:T(8,128)S(1)}, u32[]{:S(2)}, u32[]{:S(2)}) collective-permute-start(f32[144,128]{1,0:T(8,128)S(1)} %get-tuple-element.94), channel_id=1, source_target_pairs={{0,8},{1,9},{2,10},{3,11},{4,12},{5,13},{6,14},{7,15},{8,0},{9,1},... | collective-permute-start | bytes 221192 | tf_op jit(solution)/shard_map/ppermute | solution.py:559
  16.6 2.8 %collective-permute-start.9 = (f32[144,128]{1,0:T(8,128)S(1)}, f32[144,128]{1,0:T(8,128)S(1)}, u32[]{:S(2)}, u32[]{:S(2)}) collective-permute-start(f32[144,128]{1,0:T(8,128)S(1)} %get-tuple-element.95), channel_id=1, source_target_pairs={{0,1},{1,0},{2,3},{3,2},{4,5},{5,4},{6,7},{7,6},{8,16},{9,17},{10,... | collective-permute-start | bytes 221192 | tf_op jit(solution)/shard_map/ppermute | solution.py:559

commit v7 on v6

--- a/solution.py
+++ b/solution.py
@@ -24,8 +24,10 @@
         self.rows = self.n * self.X
         self.edges = sorted({0, self.X - 1})
         self.inner = range(1, self.X - 1)
-        self.wall_rows = self.X * self.G + 8
         self.wall_k = -(-self.G // 8) * 8
+        self.wall_rows, self.later_wall_rows = [
+            -(-((self.X - 1) * g + self.wall_k) // 8) * 8 for g in (self.G, self.V)
+        ]
         self.stack = -(-self.V // 8) * 8
         self.per = self.Z // (2 * self.X)
         self.span_groups = -(-(self.V + 1) // self.per)
@@ -84,7 +86,7 @@
 
 def pack_stream(d, block_of, radius_of, s_a, s_b):
     W, even = d.W, parity("stream")
-    for g in range(d.G):
+    for g in range(d.V if radius_of is None else d.G):
         if g < d.V:
             first, last = block_of(g, 0), block_of(g, d.X - 1)
         elif g == d.V and radius_of is not None:
@@ -112,14 +114,16 @@
 
 
 def pack_walls(d, planes, adj, radius_of, w_a, w_b):
-    V, X, W, Z, G = d.V, d.X, d.W, d.Z, d.G
+    V, X, W, Z = d.V, d.X, d.W, d.Z
+    G = V if radius_of is None else d.G
     even = parity("wall")
-    tail = jnp.zeros((G - V, Z), F32)
+    tail = jnp.zeros((max(G - V, 1), Z), F32)
+    rest = w_a.shape[0] - X * G
     for x in planes:
         first, last = adj[d.rows_at(x, 0), :], adj[d.rows_at(x, W - 1), :]
         w_a[x * G : x * G + V, :] = jnp.where(even, last, first)
         w_b[x * G : x * G + V, :] = jnp.where(even, first, last)
-        if radius_of is None or G - V > 1:
+        if G - V > 1:
             w_a[x * G + V : (x + 1) * G, :] = tail
             w_b[x * G + V : (x + 1) * G, :] = tail
         if radius_of is not None:
@@ -128,8 +132,8 @@
             w_a[x * G + V : x * G + V + 1, :] = jnp.where(even, last, first)
             w_b[x * G + V : x * G + V + 1, :] = jnp.where(even, first, last)
     if X - 1 in planes:
-        w_a[X * G :, :] = jnp.zeros((8, Z), F32)
-        w_b[X * G :, :] = jnp.zeros((8, Z), F32)
+        w_a[X * G :, :] = jnp.zeros((rest, Z), F32)
+        w_b[X * G :, :] = jnp.zeros((rest, Z), F32)
 
 
 def parity(axis):
@@ -332,8 +336,8 @@
     return (index > 0).astype(F32), (index < lax.axis_size(axis) - 1).astype(F32)
 
 
-def wall_terms(d, w0, w1, mw):
-    X, W, Z, G = d.X, d.W, d.Z, d.G
+def wall_terms(d, w0, w1, mw, G):
+    X, W, Z = d.X, d.W, d.Z
     even = parity("wall")
     has_low, has_high = neighbours("wall")
     row = row_ids(d)
@@ -403,7 +407,7 @@
 ):
     V, X, W, Z, n = d.V, d.X, d.W, d.Z, d.n
     span, span_radius = span_terms(d, zl, zr, mk)
-    wall, wall_radius = wall_terms(d, w0, w1, mw)
+    wall, wall_radius = wall_terms(d, w0, w1, mw, d.G)
     lane, row = lanes(d, W), row_ids(d)
     edge_lane = (lane == 0) | (lane == Z - 1)
     edge_row = (row == 0) | (row == W - 1)
@@ -435,7 +439,7 @@
 ):
     W, n = d.W, d.n
     span, _ = span_terms(d, zl, zr, mk)
-    wall, _ = wall_terms(d, w0, w1, mw)
+    wall, _ = wall_terms(d, w0, w1, mw, d.V)
 
     def residual_of(x):
         result = d.plane(partial, x) - d.each(rates[d.block(0, x), :]) * wall(x)
@@ -457,8 +461,8 @@
     has_low, has_high = neighbours("stream")
     low = jnp.where(even, s1[...], s0[...]) * has_low
     high = jnp.where(even, s0[...], s1[...]) * has_high
-    both = dot(mk[: 2 * n], split3(jnp.concatenate([low, high], axis=1)))
-    return (both[:n, :Z], both[n:, Z:]), (low[n : n + d.W], high[n : n + d.W])
+    both = dot(mk[: 2 * n], split3(padded_plane(d, jnp.concatenate([low, high], axis=1))))
+    return (both[:n, :Z], both[n:, Z:]), [v[n : n + d.W] if v.shape[0] > n else None for v in (low, high)]
 
 
 def first_stream_kernel(
@@ -608,6 +612,7 @@
     ]
     source = source.reshape(V, X * W, Z)
     faces = [((B, Z), F32)] * 2 + [((d.wall_rows, Z), F32)] * 2 + [((d.span_groups * W, Z), F32)]
+    later = [((n, Z), F32)] * 2 + [((d.later_wall_rows, Z), F32)] * 2 + faces[4:]
     field, scalar = ((d.rows, Z), F32), ((X * W, Z), F32)
     planes = ((V, X * W, Z), F32)
     sems = lambda *counts: pltpu.SemaphoreType.DMA(counts)
@@ -653,14 +658,14 @@
     inner, rs, rates, held, w_a, w_b, z = call(
         first_inner_kernel,
         d,
-        [field, scalar, ((2 * X * W, Z), F32), edge] + faces[2:],
+        [field, scalar, ((2 * X * W, Z), F32), edge] + later[2:],
         10**8,
         [partial, adj, rs, velocity, sound, w0, w1, zl, zr, mk, mw, pk],
     )
     adj1, rs, w_a, w_b, z, stream_rates, s_a, s_b = call(
         first_stream_kernel,
         d,
-        [field, scalar] + faces[2:] + [((2 * W, Z), F32)] + faces[:2],
+        [field, scalar] + later[2:] + [((2 * W, Z), F32)] + later[:2],
         10**7,
         [held, adj, rs, velocity, sound, s0, s1, mk, pk, inner, w_a, w_b, z],
         aliases={9: 0, 2: 1, 10: 2, 11: 3, 12: 4},

time: 20.8 us -> 20.8 us (level)
  no operation moved by 1% of the time
where the time goes in v7:
time: 20.8 us; the launch traced here: 20.6 us
  starting transfers between devices  10.1 us (49%)
  Pallas kernels  9.72 us (47%)
  between operations  0.78 us (4%)
    pallas_call x8, Pallas kernels, call(): pl.pallas_call(functools.partial(kernel, d), out_shape=tuple((out_space(s...  9.72 us
    ppermute x8, starting transfers between devices, swap_lines(): move = lambda value, pairs: lax.ppermute(value, AXES, pairs)  7.67 us
    ppermute x2, starting transfers between devices, swap_lines(): zl = zr = lax.ppermute(z, 'span', [(0, 1), (1, 0)])  2.43 us
  transfers between devices with their start and end apart: 10, of which 0 were waited for; matrix products, arithmetic and copies ran while one was open for 0% of the time, Pallas kernels for 27%

profile of v7, /device:TPU:0, one launch (start us, length us, event | category | flops | bytes accessed | tf_op | source)
XLA Modules:
  0.0 20.6 jit_solution(4797809275598201722)
XLA Ops:
  0.6 1.7 %pack_kernel.1 = (f32[1632,128]{1,0:T(8,128)S(1)}, f32[288,128]{1,0:T(8,128)S(1)}, f32[96,128]{1,0:T(8,128)S(1)}, f32[3,17,2,17]{3,2,1,0:T(2,128)S(1)}, f32[17,1...) custom-call(f32[1632,128]{1,0:T(8,128)} %bitcast.10, ...), custom_call_target="tpu_custom_call" | custom-call | bytes 1138928 | tf_op jit(solution)/shard_map/pack_kernel/pallas_call | solution.py:585
  2.4 0.5 %early_kernel.1 = (bf16[816,432]{1,0:T(8,128)(2,1)S(1)}, bf16[136,144]{1,0:T(8,128)(2,1)S(1)}, bf16[136,432]{1,0:T(8,128)(2,1)S(1)}, f32[288,128]{1,0:T(8,128)S(...) custom-call(f32[3,17,2,17]{3,2,1,0:T(2,128)S(1)} %get-tuple-element., ...), custom_call_target="tpu_custom_call", output_to_operand_aliasing={{4}: (6, {}), {5}: (7, {}), {6}: (8, {}), {7}: (9, {}), {8}... | custom-call | bytes 499952 | tf_op jit(solution)/shard_map/early_kernel/pallas_call | solution.py:585
  2.9 0.5 %collective-permute-start = (f32[224,128]{1,0:T(8,128)S(1)}, f32[224,128]{1,0:T(8,128)S(1)}, u32[]{:S(2)}, u32[]{:S(2)}) collective-permute-start(f32[224,128]{1,0:T(8,128)S(1)} %get-tuple-element.71), channel_id=1, source_target_pairs={{0,1},{1,0},{2,3},{3,2},{4,5},{5,4},{6,7},{7,6},{8,9},{9,8},{10,11... | collective-permute-start | bytes 344072 | tf_op jit(solution)/shard_map/ppermute | solution.py:563
  3.4 2.6 %collective-permute-start.1 = (f32[224,128]{1,0:T(8,128)S(1)}, f32[224,128]{1,0:T(8,128)S(1)}, u32[]{:S(2)}, u32[]{:S(2)}) collective-permute-start(f32[224,128]{1,0:T(8,128)S(1)} %get-tuple-element.72), channel_id=1, source_target_pairs={{0,3},{1,2},{2,1},{3,0},{4,7},{5,6},{6,5},{7,4},{8,11},{9,10},{10,... | collective-permute-start | bytes 344072 | tf_op jit(solution)/shard_map/ppermute | solution.py:563
  6.1 1.5 %collective-permute-start.2 = (f32[32,128]{1,0:T(8,128)S(1)}, f32[32,128]{1,0:T(8,128)S(1)}, u32[]{:S(2)}, u32[]{:S(2)}) collective-permute-start(f32[32,128]{1,0:T(8,128)S(1)} %get-tuple-element.73), channel_id=1, source_target_pairs={{0,4},{4,0},{1,5},{5,1},{2,6},{6,2},{3,7},{7,3},{8,12},{12,8},{9,1... | collective-permute-start | bytes 49160 | tf_op jit(solution)/shard_map/ppermute | solution.py:572
  7.6 1.6 %collective-permute-start.3 = (f32[144,128]{1,0:T(8,128)S(1)}, f32[144,128]{1,0:T(8,128)S(1)}, u32[]{:S(2)}, u32[]{:S(2)}) collective-permute-start(f32[144,128]{1,0:T(8,128)S(1)} %get-tuple-element.79), channel_id=1, source_target_pairs={{0,8},{1,9},{2,10},{3,11},{4,12},{5,13},{6,14},{7,15},{8,0},{9,1},... | collective-permute-start | bytes 221192 | tf_op jit(solution)/shard_map/ppermute | solution.py:563
  9.1 0.0 collective-permute-start.4
  9.2 1.8 %first_local_kernel.1 = (f32[1632,128]{1,0:T(8,128)S(1)}, f32[96,128]{1,0:T(8,128)S(1)}, bf16[816,432]{1,0:T(8,128)(2,1)S(1)}, bf16[136,144]{1,0:T(8,128)(2,1)S(...) custom-call(f32[1632,128]{1,0:T(8,128)S(1)} %get-tuple-element.51.ad, ...), custom_call_target="tpu_custom_call", output_to_operand_aliasing={{2}: (10, {}), {3}: (11, {}), {4}: (12, {}), {5}: (13, {})} | custom-call | flops 1000000000 | bytes 2983664 | tf_op jit(solution)/shard_map/first_local_kernel/pallas_call | solution.py:585
  11.0 0.0 collective-permute-done.2.zl.zr
  11.0 0.0 collective-permute-done.w0
  11.0 0.0 collective-permute-done.1.w1
  11.0 1.1 %first_inner_kernel.1 = (f32[1632,128]{1,0:T(8,128)S(1)}, f32[96,128]{1,0:T(8,128)S(1)}, f32[192,128]{1,0:T(8,128)S(1)}, f32[272,128]{1,0:T(8,128)S(1)}, f32[216...) custom-call(f32[1632,128]{1,0:T(8,128)S(1)} %get-tuple-element.69.partial, ...), custom_call_target="tpu_custom_call" | custom-call | flops 100000000 | bytes 3040768 | tf_op jit(solution)/shard_map/first_inner_kernel/pallas_call | solution.py:585
  12.1 0.0 collective-permute-done.3.s0
  12.1 0.0 collective-permute-done.4.s1
  12.2 0.6 %first_stream_kernel.1 = (f32[1632,128]{1,0:T(8,128)S(1)}, f32[96,128]{1,0:T(8,128)S(1)}, f32[216,128]{1,0:T(8,128)S(1)}, f32[216,128]{1,0:T(8,128)S(1)}, f32[32...) custom-call(f32[272,128]{1,0:T(8,128)S(1)} %get-tuple-element.77.edg, ...), custom_call_target="tpu_custom_call", output_to_operand_aliasing={{0}: (9, {}), {1}: (2, {}), {2}: (10, {}), {3}: (11, {}), {... | custom-call | flops 10000000 | bytes 3263744 | tf_op jit(solution)/shard_map/first_stream_kernel/pallas_call | solution.py:585
  12.7 0.7 %collective-permute-start.5 = (f32[216,128]{1,0:T(8,128)S(1)}, f32[216,128]{1,0:T(8,128)S(1)}, u32[]{:S(2)}, u32[]{:S(2)}) collective-permute-start(f32[216,128]{1,0:T(8,128)S(1)} %get-tuple-element.89), channel_id=1, source_target_pairs={{0,3},{1,2},{2,1},{3,0},{4,7},{5,6},{6,5},{7,4},{8,11},{9,10},{10,... | collective-permute-start | bytes 331784 | tf_op jit(solution)/shard_map/ppermute | solution.py:563
  13.4 0.9 %collective-permute-start.7 = (f32[32,128]{1,0:T(8,128)S(1)}, f32[32,128]{1,0:T(8,128)S(1)}, u32[]{:S(2)}, u32[]{:S(2)}) collective-permute-start(f32[32,128]{1,0:T(8,128)S(1)} %get-tuple-element.91), channel_id=1, source_target_pairs={{0,4},{4,0},{1,5},{5,1},{2,6},{6,2},{3,7},{7,3},{8,12},{12,8},{9,1... | collective-permute-start | bytes 49160 | tf_op jit(solution)/shard_map/ppermute | solution.py:572
  14.4 2.2 %collective-permute-start.8 = (f32[136,128]{1,0:T(8,128)S(1)}, f32[136,128]{1,0:T(8,128)S(1)}, u32[]{:S(2)}, u32[]{:S(2)}) collective-permute-start(f32[136,128]{1,0:T(8,128)S(1)} %get-tuple-element.94), channel_id=1, source_target_pairs={{0,8},{1,9},{2,10},{3,11},{4,12},{5,13},{6,14},{7,15},{8,0},{9,1},... | collective-permute-start | bytes 208904 | tf_op jit(solution)/shard_map/ppermute | solution.py:563
  16.6 1.8 %later_local_kernel.1.partial = f32[1632,128]{1,0:T(8,128)S(1)} custom-call(f32[1632,128]{1,0:T(8,128)S(1)} %get-tuple-element.85.adj, f32[17,96,128]{2,1,0:T(8,128)S(1)} %bitcast.9, f32[288,128]{1,0:T(8,128)S(1)} %get-tuple-element.52.vel, f32[96,128]{1,0:T(8,128)S(1)} %get-tuple-element.53.snd, f32[96,128]{1,0:T(8,128)S(1)} %get-tuple-element.86.rs.rs_full, ...), custom_call_target="tpu_custom_call" | custom-call | flops 1000000000 | bytes 2769408 | tf_op jit(solution)/shard_map/later_local_kernel/pallas_call | solution.py:585
  18.4 0.0 collective-permute-done.7.zl.zr
  18.4 0.0 collective-permute-done.5.w1
  18.5 0.9 %later_inner_kernel.1 = (f32[17,96,128]{2,1,0:T(8,128)S(1)}, f32[17,96,128]{2,1,0:T(8,128)S(1)}, f32[272,128]{1,0:T(8,128)S(1)}) custom-call(f32[1632,128]{1,0:T(8,128)S(1)} %later_local_kernel.1.partial, f32[1632,128]{1,0:T(8,128)S(1)} %get-tuple-element.85.adj, f32[96,128]{1,0:T(8,128)S(1)} %get-tuple-element.86.rs.rs_full, ...), custom_call_target="tpu_custom_call" | custom-call | flops 100000000 | bytes 2934272 | tf_op jit(solution)/shard_map/later_inner_kernel/pallas_call | solution.py:585
  19.4 0.0 collective-permute-done.8.s0
  19.4 1.2 %later_stream_kernel.1 = (f32[17,96,128]{2,1,0:T(8,128)}, f32[17,96,128]{2,1,0:T(8,128)}) custom-call(f32[272,128]{1,0:T(8,128)S(1)} %get-tuple-element.92.edge, f32[1632,128]{1,0:T(8,128)S(1)} %get-tuple-element.85.adj, f32[96,128]{1,0:T(8,128)S(1)} %get-tuple-element.86.rs.rs_full, f32[16,128]{1,0:T(8,128)S(1)} %get-tuple-element.93.rates, ...), custom_call_target="tpu_custom_call" | custom-call | flops 10000000 | bytes 3665152 | tf_op jit(solution)/shard_map/later_stream_kernel/pallas_call | solution.py:585
  (6 shorter events, 0.0 us)
Async XLA Ops:
  0.6 8.5 %copy-start = (f32[17,12,8,128]{3,2,1,0:T(8,128)S(1)}, f32[17,12,8,128]{3,2,1,0:T(8,128)}, u32[]{:S(2)}) copy-start(f32[17,12,8,128]{3,2,1,0:T(8,128)} %param.11) | copy-start | bytes 2506756
  2.9 8.0 %collective-permute-start = (f32[224,128]{1,0:T(8,128)S(1)}, f32[224,128]{1,0:T(8,128)S(1)}, u32[]{:S(2)}, u32[]{:S(2)}) collective-permute-start(f32[224,128]{1,0:T(8,128)S(1)} %get-tuple-element.71), channel_id=1, source_target_pairs={{0,1},{1,0},{2,3},{3,2},{4,5},{5,4},{6,7},{7,6},{8,9},{9,8},{10,11... | collective-permute-start | bytes 344072 | tf_op jit(solution)/shard_map/ppermute | solution.py:563
  3.4 7.5 %collective-permute-start.1 = (f32[224,128]{1,0:T(8,128)S(1)}, f32[224,128]{1,0:T(8,128)S(1)}, u32[]{:S(2)}, u32[]{:S(2)}) collective-permute-start(f32[224,128]{1,0:T(8,128)S(1)} %get-tuple-element.72), channel_id=1, source_target_pairs={{0,3},{1,2},{2,1},{3,0},{4,7},{5,6},{6,5},{7,4},{8,11},{9,10},{10,... | collective-permute-start | bytes 344072 | tf_op jit(solution)/shard_map/ppermute | solution.py:563
  6.1 4.9 %collective-permute-start.2 = (f32[32,128]{1,0:T(8,128)S(1)}, f32[32,128]{1,0:T(8,128)S(1)}, u32[]{:S(2)}, u32[]{:S(2)}) collective-permute-start(f32[32,128]{1,0:T(8,128)S(1)} %get-tuple-element.73), channel_id=1, source_target_pairs={{0,4},{4,0},{1,5},{5,1},{2,6},{6,2},{3,7},{7,3},{8,12},{12,8},{9,1... | collective-permute-start | bytes 49160 | tf_op jit(solution)/shard_map/ppermute | solution.py:572
  7.6 4.6 %collective-permute-start.3 = (f32[144,128]{1,0:T(8,128)S(1)}, f32[144,128]{1,0:T(8,128)S(1)}, u32[]{:S(2)}, u32[]{:S(2)}) collective-permute-start(f32[144,128]{1,0:T(8,128)S(1)} %get-tuple-element.79), channel_id=1, source_target_pairs={{0,8},{1,9},{2,10},{3,11},{4,12},{5,13},{6,14},{7,15},{8,0},{9,1},... | collective-permute-start | bytes 221192 | tf_op jit(solution)/shard_map/ppermute | solution.py:563
  9.1 3.0 %collective-permute-start.4 = (f32[144,128]{1,0:T(8,128)S(1)}, f32[144,128]{1,0:T(8,128)S(1)}, u32[]{:S(2)}, u32[]{:S(2)}) collective-permute-start(f32[144,128]{1,0:T(8,128)S(1)} %get-tuple-element.80), channel_id=1, source_target_pairs={{0,1},{1,0},{2,3},{3,2},{4,5},{5,4},{6,7},{7,6},{8,16},{9,17},{10,... | collective-permute-start | bytes 221192 | tf_op jit(solution)/shard_map/ppermute | solution.py:563
  12.7 5.7 %collective-permute-start.5 = (f32[216,128]{1,0:T(8,128)S(1)}, f32[216,128]{1,0:T(8,128)S(1)}, u32[]{:S(2)}, u32[]{:S(2)}) collective-permute-start(f32[216,128]{1,0:T(8,128)S(1)} %get-tuple-element.89), channel_id=1, source_target_pairs={{0,3},{1,2},{2,1},{3,0},{4,7},{5,6},{6,5},{7,4},{8,11},{9,10},{10,... | collective-permute-start | bytes 331784 | tf_op jit(solution)/shard_map/ppermute | solution.py:563
  13.4 5.0 %collective-permute-start.6 = (f32[216,128]{1,0:T(8,128)S(1)}, f32[216,128]{1,0:T(8,128)S(1)}, u32[]{:S(2)}, u32[]{:S(2)}) collective-permute-start(f32[216,128]{1,0:T(8,128)S(1)} %get-tuple-element.90), channel_id=1, source_target_pairs={{0,1},{1,0},{2,3},{3,2},{4,5},{5,4},{6,7},{7,6},{8,9},{9,8},{10,11... | collective-permute-start | bytes 331784 | tf_op jit(solution)/shard_map/ppermute | solution.py:563
  13.4 5.0 %collective-permute-start.7 = (f32[32,128]{1,0:T(8,128)S(1)}, f32[32,128]{1,0:T(8,128)S(1)}, u32[]{:S(2)}, u32[]{:S(2)}) collective-permute-start(f32[32,128]{1,0:T(8,128)S(1)} %get-tuple-element.91), channel_id=1, source_target_pairs={{0,4},{4,0},{1,5},{5,1},{2,6},{6,2},{3,7},{7,3},{8,12},{12,8},{9,1... | collective-permute-start | bytes 49160 | tf_op jit(solution)/shard_map/ppermute | solution.py:572
  14.4 5.0 %collective-permute-start.8 = (f32[136,128]{1,0:T(8,128)S(1)}, f32[136,128]{1,0:T(8,128)S(1)}, u32[]{:S(2)}, u32[]{:S(2)}) collective-permute-start(f32[136,128]{1,0:T(8,128)S(1)} %get-tuple-element.94), channel_id=1, source_target_pairs={{0,8},{1,9},{2,10},{3,11},{4,12},{5,13},{6,14},{7,15},{8,0},{9,1},... | collective-permute-start | bytes 208904 | tf_op jit(solution)/shard_map/ppermute | solution.py:563
  16.6 2.8 %collective-permute-start.9 = (f32[136,128]{1,0:T(8,128)S(1)}, f32[136,128]{1,0:T(8,128)S(1)}, u32[]{:S(2)}, u32[]{:S(2)}) collective-permute-start(f32[136,128]{1,0:T(8,128)S(1)} %get-tuple-element.95), channel_id=1, source_target_pairs={{0,1},{1,0},{2,3},{3,2},{4,5},{5,4},{6,7},{7,6},{8,16},{9,17},{10,... | collective-permute-start | bytes 208904 | tf_op jit(solution)/shard_map/ppermute | solution.py:563
